TPU v7x, 256 devices: a whole 4x4x8 slice. The times are simulated.
256 devices in a mesh: plane: 8 (over x, z_hi), tile: 32 (over y, z_lo, core).
Axes of the slice: x: 4, y: 4, z: 8 (z_hi: 2, z_lo: 4; z = z_hi * 4 + z_lo), core: 2. Of those that a mesh axis runs over, the one named last changes fastest.
Arguments:
- slab_cells: bfloat16 [8, 4, 4096, 4096], P('plane', None, 'tile'), may hold values from -6 to 6
- slab_weight: float32 [8, 4], P('plane'), may hold values from 0.2 to 0.6
- kernel_table: float32 [32], replicated, may hold values from 0.15 to 0.6
- kernel_index: int32 [4, 8], replicated, may hold values from 0 to 31
- ell_index: int32 [1024, 512], P('plane', 'tile'), may hold values from 0 to 16, as said below
- target_spectra: float32 [10, 16], replicated, may hold values from -1.8 to 1.8
Outputs:
- spectra: float32 [10, 16], replicated
- plane_grad: float32 [8, 4096, 4096], P('plane', 'tile')
Inputs may be any that keep to these rules, and one draw needn't show every extreme that they name: `ell_index`: 16 marks a Fourier mode that enters no spectrum.
All inputs are finite; a program needn't handle non-finite values.
Results may differ from a plain program's by a relative error of at most 0.019.
Values may be sent and summed in bfloat16 or wider, within the bound.
No kernel may reach another device: no remote copies, remote signals or barrier semaphores. Data moves between devices by JAX's collectives and lax.ppermute only.
A program may use at most 128 MiB of HBM per device.

v0:
```python
import math

import jax
import jax.numpy as jnp
import numpy as np
from jax import lax
from jax.sharding import PartitionSpec as P

NPIX = 4096
KMAX = 512
BINS = 4
ELLS = 16


HIGHEST = lax.Precision.HIGHEST
TWO_PI = 2.0 * math.pi


def kernel_weights(kernel_table, kernel_index):
    entries = jnp.arange(kernel_table.shape[0], dtype=jnp.int32)
    one_hot = (kernel_index[:, :, None] == entries).astype(jnp.float32)
    return jnp.einsum("bpt,t->bp", one_hot, kernel_table, precision=HIGHEST)


def column_table(amount):
    wave_num = jnp.arange(amount, dtype=jnp.int32)
    offsets = jnp.arange(NPIX, dtype=jnp.int32)
    angles = (wave_num[:, None] * offsets[None, :] % NPIX).astype(jnp.float32) * (TWO_PI / NPIX)
    stacked = jnp.stack([jnp.cos(angles), -jnp.sin(angles)], axis=1)
    return stacked.astype(jnp.bfloat16).reshape(2 * amount, NPIX)


def row_tables(start_row, amount):
    wave_num = start_row + jnp.arange(amount, dtype=jnp.int32) - KMAX
    offsets = jnp.arange(NPIX, dtype=jnp.int32)
    angles = (wave_num[:, None] * offsets[None, :] % NPIX).astype(jnp.float32) * (TWO_PI / NPIX)
    return jnp.stack([jnp.cos(angles), jnp.sin(angles)], axis=0)


def project_band(slab_rows, depth_weight, fourier_table):
    plane_map = jnp.zeros((slab_rows.shape[0], slab_rows.shape[2], slab_rows.shape[3]), jnp.float32)
    for layer_id in range(slab_rows.shape[1]):
        plane_map = (
            plane_map
            + slab_rows[:, layer_id].astype(jnp.float32) * depth_weight[:, layer_id, None, None]
        )
    plane_map = plane_map.astype(jnp.bfloat16)
    flat_rows = plane_map.reshape(-1, plane_map.shape[-1])
    band_part = lax.dot_general(
        fourier_table, flat_rows, (((1,), (1,)), ((), ())), preferred_element_type=jnp.float32
    )
    return band_part.reshape(fourier_table.shape[0] // 2, 2, plane_map.shape[0], plane_map.shape[1])


def forward_rows(tables, band_part, group_kernel):
    products = jnp.einsum("cqr,xspr->cqsxp", tables, band_part, precision=HIGHEST)
    real_part = products[0, :, 0] + products[1, :, 1]
    imag_part = products[0, :, 1] - products[1, :, 0]
    lines = jnp.stack([real_part, imag_part], axis=1)
    return jnp.einsum("qsxp,bp->qsbx", lines, group_kernel, precision=HIGHEST)


def adjoint_rows(mixed_grad, start_row, block_rows):
    row_total = mixed_grad.shape[0]
    block_size = min(row_total, block_rows)

    def adjoint_one_block(block_id, running):
        offset = block_id * block_size
        section = lax.dynamic_slice_in_dim(mixed_grad, offset, block_size, 0)
        tables = row_tables(start_row + offset, block_size)
        products = jnp.einsum("cqr,qspx->csxpr", tables, section, precision=HIGHEST)
        real_part = products[0, 0] - products[1, 1]
        imag_part = products[1, 0] + products[0, 1]
        return running + jnp.stack([real_part, imag_part], axis=1)

    initial = jnp.zeros((mixed_grad.shape[3], 2, mixed_grad.shape[2], NPIX), jnp.float32)
    return lax.fori_loop(0, row_total // block_size, adjoint_one_block, initial)


def column_adjoint(band_grad, fourier_table):
    flat_rows = band_grad.reshape(fourier_table.shape[0], -1)
    result = lax.dot_general(
        flat_rows, fourier_table, (((0,), (0,)), ((), ())), preferred_element_type=jnp.float32
    )
    return result.reshape(band_grad.shape[2], band_grad.shape[3], fourier_table.shape[1])


def pair_select():
    first_bin, second_bin = np.triu_indices(BINS)
    eye_bins = np.eye(BINS, dtype=np.float32)
    return (jnp.asarray(eye_bins[first_bin]), jnp.asarray(eye_bins[second_bin]))


def cycle_area():
    cycle_ids = jnp.arange(ELLS, dtype=jnp.float32)
    return (2.0 * cycle_ids + 1.0) * float((KMAX // ELLS) ** 2) * (0.5 * math.pi)


def mode_one_hot(ell_index):
    return (ell_index[:, :, None] == jnp.arange(ELLS, dtype=jnp.int32)).astype(jnp.float32)


def partial_spectra(kappa_hat, ell_index):
    pick_first, pick_second = pair_select()
    left_terms = jnp.einsum("qsbx,pb->pqsx", kappa_hat, pick_first, precision=HIGHEST)
    right_terms = jnp.einsum("qsbx,pb->pqsx", kappa_hat, pick_second, precision=HIGHEST)
    products = jnp.sum(left_terms * right_terms, axis=2)
    return jnp.einsum("pqx,qxl->pl", products, mode_one_hot(ell_index), precision=HIGHEST)


def mode_gradient(kappa_hat, ell_index, spectra, target_spectra):
    pick_first, pick_second = pair_select()
    pair_mix = (
        pick_first[:, :, None] * pick_second[:, None, :]
        + pick_second[:, :, None] * pick_first[:, None, :]
    )
    weights = (spectra - target_spectra) * (KMAX / (ELLS * NPIX)) / cycle_area()
    coupling = jnp.einsum("pij,pl->lij", pair_mix, weights, precision=HIGHEST)
    per_mode = jnp.einsum("qxl,lij->qxij", mode_one_hot(ell_index), coupling, precision=HIGHEST)
    return jnp.einsum("qxij,qsjx->qsix", per_mode, kappa_hat, precision=HIGHEST)


def body(slab_cells, slab_weight, kernel_table, kernel_index, ell_index, target_spectra):
    kernel_all = kernel_weights(kernel_table, kernel_index)
    local_planes = slab_cells.shape[0]
    local_kernel = lax.dynamic_slice_in_dim(
        kernel_all, lax.axis_index("plane") * local_planes, local_planes, 1
    )
    fourier_table = column_table(KMAX)
    band_part = project_band(slab_cells, slab_weight, fourier_table)
    exchanged = lax.all_to_all(
        band_part.astype(jnp.bfloat16), "tile", split_axis=0, concat_axis=3, tiled=True
    ).astype(band_part.dtype)
    block_rows = ell_index.shape[0]
    block_size = min(block_rows * lax.axis_size("plane"), block_rows)

    def band_one_block(block_id):
        tables = row_tables(block_id * block_size, block_size)
        return forward_rows(tables, exchanged, local_kernel)

    stacked = lax.map(
        band_one_block,
        jnp.arange(block_rows * lax.axis_size("plane") // block_size, dtype=jnp.int32),
    )
    kappa_hat = lax.psum_scatter(
        stacked.reshape((block_rows * lax.axis_size("plane"),) + stacked.shape[2:]).astype(
            jnp.bfloat16
        ),
        "plane",
        scatter_dimension=0,
        tiled=True,
    ).astype(jnp.float32)
    local_sums = partial_spectra(kappa_hat, ell_index)
    summed = lax.psum(local_sums, ("plane", "tile"))
    spectra = summed / (NPIX * NPIX * cycle_area())
    grad_hat = mode_gradient(kappa_hat, ell_index, spectra, target_spectra).astype(jnp.bfloat16)
    initial = jnp.zeros((exchanged.shape[0], 2, local_planes, NPIX), jnp.float32)
    mixed_grad = jnp.einsum(
        "qsbx,bp->qspx",
        lax.all_gather(grad_hat, "plane", axis=0, tiled=True).astype(jnp.float32),
        local_kernel,
        precision=HIGHEST,
    )
    band_grad = initial + adjoint_rows(mixed_grad, jnp.int32(0), block_rows)
    returned = lax.all_to_all(
        band_grad.astype(jnp.bfloat16), "tile", split_axis=3, concat_axis=0, tiled=True
    )
    plane_grad = column_adjoint(returned, fourier_table)
    return (spectra, plane_grad)


def solution(mesh):
    return jax.shard_map(
        body,
        mesh=mesh,
        in_specs=(
            P("plane", None, "tile", None),
            P("plane", None),
            P(),
            P(),
            P("plane", "tile"),
            P(),
        ),
        out_specs=(P(), P("plane", "tile", None)),
        check_vma=False,
    )
```

profile of v0, /device:TPU:1, one launch (start us, length us, event | category | flops | bytes accessed | tf_op | source)
XLA Modules:
  0.0 545.2 jit_solution(14756973370779773559)
XLA Ops:
  7.2 33.4 %negate_convert_fusion = (bf16[512,1,4096]{2,0,1:T(8,128)(2,1)S(1)}, bf16[512,1,4096]{2,0,1:T(8,128)(2,1)S(1)}) fusion(), kind=kLoop, calls=%fused_computation.58 | loop fusion | flops 35651584 | bytes 8388608 | tf_op jit(solution)/shard_map/convert.4
  49.6 10.2 %all-to-all-start = ((bf16[512,2,1,128]{3,1,2,0:T(2,128)(2,1)}), bf16[512,2,1,128]{3,1,2,0:T(2,128)(2,1)S(1)}, u32[]{:S(2)}, u32[]{:S(2)}) async-start(bf16[512,2,1,128]{3,1,2,0:T(2,128)(2,1)} %copy.60), calls=%async_computation | async-start | bytes 524288 | tf_op jit(solution)/shard_map/all_to_all | solution.py:131
  60.3 10.8 %all-to-all-done = bf16[512,2,1,128]{3,1,2,0:T(2,128)(2,1)S(1)} async-done(((bf16[512,2,1,128]{3,1,2,0:T(2,128)(2,1)}), bf16[512,2,1,128]{3,1,2,0:T(2,128)(2,1)S(1)}, u32[]{:S(2)}, u32[]{:S(2)}) %all-to-all-start) | async-done | bytes 262176 | tf_op jit(solution)/shard_map/all_to_all | solution.py:131
  71.8 106.5 %while.28 = (s32[]{:T(128)}, bf16[8,128,2,4,16]{1,4,3,2,0:T(8,128)(2,1)S(1)}, s32[8]{0:T(128)S(1)}, f32[16,2,1,4096]{3,0,1,2:T(8,128)S(1)}, f32[4,1]{0,1:T(1,128)S(1)}, /*index=5*/s32[]{:T(128)}, s32[1]{0:T(128)}) while((s32[]{:T(128)}, bf16[8,128,2,4,16]{1,4,3,2,0:T(8,128)(2,1)S(1)}, s32[8]{0:T(128)S(1)}, f32[16,2,1,4096]{3,0,1,2:T(8,128)S(1)}, ...), condition=%wide.region_1.2_spmd, body=%wide.region_0.1_spmd.sunk | while | flops 411066624 | bytes 9111149 | solution.py:141
  73.6 8.2 %fusion.94 = (f32[1,128,4096]{2,1,0:T(8,128)S(1)}, f32[1,128,4096]{2,1,0:T(8,128)S(1)}) fusion(s32[128]{0:T(128)S(1)} %add_add_fusion.4), kind=kLoop, calls=%fused_computation.14.clone.1 | loop fusion | flops 7340032 | bytes 4194816 | tf_op jit(solution)/shard_map/while/body/eval_jaxpr/cos | solution.py:37
  86.8 8.2 %fusion.94 = (f32[1,128,4096]{2,1,0:T(8,128)S(1)}, f32[1,128,4096]{2,1,0:T(8,128)S(1)}) fusion(s32[128]{0:T(128)S(1)} %add_add_fusion.4), kind=kLoop, calls=%fused_computation.14.clone.1 | loop fusion | flops 7340032 | bytes 4194816 | tf_op jit(solution)/shard_map/while/body/eval_jaxpr/cos | solution.py:37
  100.1 8.2 %fusion.94 = (f32[1,128,4096]{2,1,0:T(8,128)S(1)}, f32[1,128,4096]{2,1,0:T(8,128)S(1)}) fusion(s32[128]{0:T(128)S(1)} %add_add_fusion.4), kind=kLoop, calls=%fused_computation.14.clone.1 | loop fusion | flops 7340032 | bytes 4194816 | tf_op jit(solution)/shard_map/while/body/eval_jaxpr/cos | solution.py:37
  113.3 8.2 %fusion.94 = (f32[1,128,4096]{2,1,0:T(8,128)S(1)}, f32[1,128,4096]{2,1,0:T(8,128)S(1)}) fusion(s32[128]{0:T(128)S(1)} %add_add_fusion.4), kind=kLoop, calls=%fused_computation.14.clone.1 | loop fusion | flops 7340032 | bytes 4194816 | tf_op jit(solution)/shard_map/while/body/eval_jaxpr/cos | solution.py:37
  126.6 8.2 %fusion.94 = (f32[1,128,4096]{2,1,0:T(8,128)S(1)}, f32[1,128,4096]{2,1,0:T(8,128)S(1)}) fusion(s32[128]{0:T(128)S(1)} %add_add_fusion.4), kind=kLoop, calls=%fused_computation.14.clone.1 | loop fusion | flops 7340032 | bytes 4194816 | tf_op jit(solution)/shard_map/while/body/eval_jaxpr/cos | solution.py:37
  139.8 8.2 %fusion.94 = (f32[1,128,4096]{2,1,0:T(8,128)S(1)}, f32[1,128,4096]{2,1,0:T(8,128)S(1)}) fusion(s32[128]{0:T(128)S(1)} %add_add_fusion.4), kind=kLoop, calls=%fused_computation.14.clone.1 | loop fusion | flops 7340032 | bytes 4194816 | tf_op jit(solution)/shard_map/while/body/eval_jaxpr/cos | solution.py:37
  153.1 8.2 %fusion.94 = (f32[1,128,4096]{2,1,0:T(8,128)S(1)}, f32[1,128,4096]{2,1,0:T(8,128)S(1)}) fusion(s32[128]{0:T(128)S(1)} %add_add_fusion.4), kind=kLoop, calls=%fused_computation.14.clone.1 | loop fusion | flops 7340032 | bytes 4194816 | tf_op jit(solution)/shard_map/while/body/eval_jaxpr/cos | solution.py:37
  166.3 8.2 %fusion.94 = (f32[1,128,4096]{2,1,0:T(8,128)S(1)}, f32[1,128,4096]{2,1,0:T(8,128)S(1)}) fusion(s32[128]{0:T(128)S(1)} %add_add_fusion.4), kind=kLoop, calls=%fused_computation.14.clone.1 | loop fusion | flops 7340032 | bytes 4194816 | tf_op jit(solution)/shard_map/while/body/eval_jaxpr/cos | solution.py:37
  182.0 78.8 %reduce-scatter.4.cloned.1.call-done = bf16[128,128]{1,0:T(8,128)(2,1)} async-done(((bf16[1024,128]{1,0:T(8,128)(2,1)}), bf16[128,128]{1,0:T(8,128)(2,1)}) %reduce-scatter.4.cloned.1.call-update) | async-done | bytes 32784
  263.5 75.9 %psum.7 = f32[10,16]{1,0:T(8,128)S(1)} all-reduce(f32[10,16]{1,0:T(8,128)S(1)} %convolution_bitcast_fusion.2), channel_id=1, replica_groups=mesh['plane'=8,'tile'=32] {'plane','tile'}, use_global_device_ids=true, to_apply=%region_4.5 | all-reduce | flops 160 | bytes 1280 | tf_op jit(solution)/shard_map/psum | solution.py:154
  343.2 8.7 %fusion.38 = bf16[128,2,4,16]{2,1,3,0:T(2,128)(2,1)S(1)} fusion(bf16[128,2,4,16]{2,1,3,0:T(2,128)(2,1)S(1)} %copy.65, f32[128,16,4,4]{3,2,1,0:T(4,128)} %copy.66), kind=kOutput, calls=%fused_computation.66 | convolution fusion | flops 802816 | bytes 196608 | tf_op jit(solution)/shard_map/qxij,qsjx->qsix/dot_general | solution.py:120
  352.9 36.0 %all_gather.3 = bf16[1024,2,4,16]{0,3,2,1:T(8,128)(2,1)S(1)} all-gather(bf16[128,2,4,16]{0,3,2,1:T(8,128)(2,1)S(1)} %copy.67), channel_id=1, replica_groups=mesh['plane'=8,'tile'=32] {'plane'}, dimensions={0}, use_global_device_ids=true | all-gather | bytes 294912 | tf_op jit(solution)/shard_map/all_gather | solution.py:160
  389.4 85.7 %while.29 = (s32[]{:T(128)}, f32[16,2,1,4096]{3,0,2,1:T(8,128)S(1)}, f32[1024,2,1,16]{0,3,1,2:T(8,128)S(1)}, s32[]{:T(128)}, s32[]{:T(128)}, /*index=5*/s32[]{:T(128)}, s32[]{:T(128)}) while((s32[]{:T(128)}, f32[16,2,1,4096]{3,0,2,1:T(8,128)S(1)}, f32[1024,2,1,16]{0,3,1,2:T(8,128)S(1)}, s32[]{:T(128)}, s32[]{:T(128)}, ...), condition=%wide.region_6.7_spmd.clone, body=%wide.region_5.6_spmd.clone.sunk | while | flops 411566336 | bytes 12600461 | solution.py:77
  389.7 8.2 %fusion.99 = (f32[1,128,4096]{2,1,0:T(8,128)S(1)}, f32[1,128,4096]{2,1,0:T(8,128)S(1)}) fusion(s32[128]{0:T(128)S(1)} %add_add_fusion.5), kind=kLoop, calls=%fused_computation.38.clone.1 | loop fusion | flops 7340032 | bytes 4194816 | tf_op jit(solution)/shard_map/while/body/eval_jaxpr/cos | solution.py:37
  400.4 8.2 %fusion.99 = (f32[1,128,4096]{2,1,0:T(8,128)S(1)}, f32[1,128,4096]{2,1,0:T(8,128)S(1)}) fusion(s32[128]{0:T(128)S(1)} %add_add_fusion.5), kind=kLoop, calls=%fused_computation.38.clone.1 | loop fusion | flops 7340032 | bytes 4194816 | tf_op jit(solution)/shard_map/while/body/eval_jaxpr/cos | solution.py:37
  411.1 8.2 %fusion.99 = (f32[1,128,4096]{2,1,0:T(8,128)S(1)}, f32[1,128,4096]{2,1,0:T(8,128)S(1)}) fusion(s32[128]{0:T(128)S(1)} %add_add_fusion.5), kind=kLoop, calls=%fused_computation.38.clone.1 | loop fusion | flops 7340032 | bytes 4194816 | tf_op jit(solution)/shard_map/while/body/eval_jaxpr/cos | solution.py:37
  421.8 8.2 %fusion.99 = (f32[1,128,4096]{2,1,0:T(8,128)S(1)}, f32[1,128,4096]{2,1,0:T(8,128)S(1)}) fusion(s32[128]{0:T(128)S(1)} %add_add_fusion.5), kind=kLoop, calls=%fused_computation.38.clone.1 | loop fusion | flops 7340032 | bytes 4194816 | tf_op jit(solution)/shard_map/while/body/eval_jaxpr/cos | solution.py:37
  481.1 11.1 %all-to-all-start.1 = ((bf16[32,2,2048]{2,1,0:T(2,128)(2,1)}), bf16[32,2,2048]{2,1,0:T(2,128)(2,1)S(1)}, u32[]{:S(2)}, u32[]{:S(2)}) async-start(bf16[32,2,2048]{2,1,0:T(2,128)(2,1)} %reshape.572), calls=%async_computation.1 | async-start | bytes 524288 | tf_op jit(solution)/shard_map/all_to_all | solution.py:165
  499.7 16.4 %copy.71 = bf16[512,2,4096]{2,1,0:T(2,128)(2,1)} copy(bf16[512,2,4096]{2,0,1:T(8,128)(2,1)} %pad_maximum_fusion) | data formatting | bytes 16777216 | tf_op jit(solution)/shard_map/stack | solution.py:29
  516.1 13.1 %convert_element_type.171 = bf16[1024,4096]{1,0:T(8,128)(2,1)} reshape(bf16[512,2,4096]{2,1,0:T(2,128)(2,1)} %copy.71) | data formatting | bytes 16777216 | tf_op jit(solution)/shard_map/convert_element_type | solution.py:30
  (166 shorter events, 131.1 us)
Async XLA Ops:
  7.2 52.7 %copy-start = (f32[32]{0:T(128)S(1)}, f32[32]{0:T(128)}, u32[]{:S(2)}) copy-start(f32[32]{0:T(128)} %param.16) | copy-start | bytes 388
  7.2 33.4 %copy-start.6 = (f32[1,4]{1,0:T(1,128)S(1)}, f32[1,4]{1,0:T(1,128)}, u32[]{:S(2)}) copy-start(f32[1,4]{1,0:T(1,128)} %param.15) | copy-start | bytes 52
  40.6 8.0 %copy-start.2 = (bf16[512,1,4096]{2,0,1:T(8,128)(2,1)}, bf16[512,1,4096]{2,0,1:T(8,128)(2,1)S(1)}, u32[]{:S(2)}) copy-start(bf16[512,1,4096]{2,0,1:T(8,128)(2,1)S(1)} %get-tuple-element.197) | copy-start | bytes 12582916
  40.6 8.0 %copy-start.3 = (bf16[512,1,4096]{2,0,1:T(8,128)(2,1)}, bf16[512,1,4096]{2,0,1:T(8,128)(2,1)S(1)}, u32[]{:S(2)}) copy-start(bf16[512,1,4096]{2,0,1:T(8,128)(2,1)S(1)} %get-tuple-element.198) | copy-start | bytes 12582916
  41.4 18.5 %copy-start.12 = (s32[4,8]{1,0:T(4,128)S(1)}, s32[4,8]{1,0:T(4,128)}, u32[]{:S(2)}) copy-start(s32[4,8]{1,0:T(4,128)} %param.17) | copy-start | bytes 388
  49.6 21.5 %all-to-all-start = ((bf16[512,2,1,128]{3,1,2,0:T(2,128)(2,1)}), bf16[512,2,1,128]{3,1,2,0:T(2,128)(2,1)S(1)}, u32[]{:S(2)}, u32[]{:S(2)}) async-start(bf16[512,2,1,128]{3,1,2,0:T(2,128)(2,1)} %copy.60), calls=%async_computation | async-start | bytes 524288 | tf_op jit(solution)/shard_map/all_to_all | solution.py:131
  59.8 201.0 %reduce-scatter.4.cloned.1.call-start = ((), (), s32[]{:S(2)}) async-start(), calls=%async_computation.3 | async-start | bytes 294912
  178.3 3.7 copy-start.8
  178.3 3.7 copy-start.9
  179.7 83.0 %copy-start.11 = (f32[10,4,1,1]{0,1,3,2:T(4,128)S(1)}, f32[10,4,1,1]{0,1,3,2:T(4,128)}, u32[]{:S(2)}) copy-start(f32[10,4,1,1]{0,1,3,2:T(4,128)} %constant.180) | copy-start | bytes 484
  179.7 83.3 %copy-start.10 = (f32[10,4,1,1]{0,1,3,2:T(4,128)S(1)}, f32[10,4,1,1]{0,1,3,2:T(4,128)}, u32[]{:S(2)}) copy-start(f32[10,4,1,1]{0,1,3,2:T(4,128)} %constant.181) | copy-start | bytes 484
  179.7 83.6 %copy-start.4 = (s32[128,16]{0,1:T(8,128)S(1)}, s32[128,16]{0,1:T(8,128)}, u32[]{:S(2)}) copy-start(s32[128,16]{0,1:T(8,128)} %param.18) | copy-start | bytes 24580
  179.7 159.7 %copy-start.7 = (f32[10,16]{1,0:T(8,128)S(1)}, f32[10,16]{1,0:T(8,128)}, u32[]{:S(2)}) copy-start(f32[10,16]{1,0:T(8,128)} %param.19) | copy-start | bytes 1924
  339.3 3.8 copy-start.5
  481.1 48.1 %all-to-all-start.1 = ((bf16[32,2,2048]{2,1,0:T(2,128)(2,1)}), bf16[32,2,2048]{2,1,0:T(2,128)(2,1)S(1)}, u32[]{:S(2)}, u32[]{:S(2)}) async-start(bf16[32,2,2048]{2,1,0:T(2,128)(2,1)} %reshape.572), calls=%async_computation.1 | async-start | bytes 524288 | tf_op jit(solution)/shard_map/all_to_all | solution.py:165
  532.1 6.0 %copy-start.1 = (f32[32]{0:T(128)S(1)}, f32[32]{0:T(128)}, u32[]{:S(2)}) copy-start(f32[32]{0:T(128)} %param.16) | copy-start | bytes 388
Sparse Core Ops, SparseCore 0:
  182.1 78.6 reduce-scatter.3
where the time goes:
time: 551 us; the launch traced here: 545 us
  other arithmetic  175 us (32%)
  blocking collectives  112 us (20%)
  waiting for transfers between devices  89.6 us (16%)
  matrix products  71.3 us (13%)
  local copies, waits for them, and re-layouts  55 us (10%)
  starting transfers between devices  21.3 us (4%)
  between operations  14.7 us (3%)
  loops' own time  6.95 us (1%)
    cos x16, other arithmetic, row_tables(): return jnp.stack([jnp.cos(angles), jnp.sin(angles)], axis=0)  131 us
    unnamed x2, waiting for transfers between devices  78.8 us
    psum x1, blocking collectives, body(): summed = lax.psum(local_sums, ('plane', 'tile'))  75.9 us
    all_gather x1, blocking collectives, body(): lax.all_gather(grad_hat, 'plane', axis=0, tiled=True).astype(jnp.float32)  36 us
    another operation x9, other arithmetic  33.4 us
    dot_general x8, matrix products, forward_rows(): jnp.einsum('cqr,xspr->cqsxp', tables, band_part, precision=HIGHEST)  29.4 us
    dot_general x8, matrix products, adjoint_one_block(): products = jnp.einsum('cqr,qspx->csxpr', tables, section, precision=HIGHEST)  17.9 us
    another operation x1, local copies, waits for them, and re-layouts, column_table(): stacked = jnp.stack([jnp.cos(angles), -jnp.sin(angles)], axis=1)  16.4 us
  transfers between devices with their start and end apart: 3, of which 2 were waited for; matrix products, arithmetic and copies ran while one was open for 7% of the time, Pallas kernels for 0%

commit v1 on v0

v1 whole, which is shorter than its diff:
```python
import functools
import math

import jax
import jax.numpy as jnp
import ml_dtypes
import numpy as np
from jax import lax
from jax.experimental import pallas as pl
from jax.experimental.pallas import tpu as pltpu
from jax.sharding import PartitionSpec as P

NPIX = 4096
KMAX = 512
BINS = 4
ELLS = 16
RADIX = 8
SPAN = NPIX // RADIX
N_PLANE = 8
N_TILE = 32
N_DEV = N_PLANE * N_TILE
ROWS = NPIX // N_TILE
LANES = 128
CHUNK = 32

ORDER = (0, 4, 1, 7, 2, 6, 3, 5)
PLACE = {rho: place for place, rho in enumerate(ORDER)}
DUOS = ((1, 7), (2, 6), (3, 5))
HALF = math.sqrt(0.5)

PAIR_ID = {}
for _number, (_i, _j) in enumerate(zip(*np.triu_indices(BINS))):
    PAIR_ID[(int(_i), int(_j))] = PAIR_ID[(int(_j), int(_i))] = _number
FIRST_GROUP = ((0, 0), (1, 1), (2, 2), (3, 3), (0, 1), (1, 2), (2, 3), (3, 0))
SECOND_GROUP = ((0, 2), (1, 3))

F32 = jnp.float32
BF16 = jnp.bfloat16
VMEM = pl.BlockSpec(memory_space=pltpu.VMEM)
SMEM = pl.BlockSpec(memory_space=pltpu.SMEM)
LIMIT = 32 * 1024 * 1024


def wave_table():
    rows = []
    tiles = np.arange(N_TILE)
    for rho in ORDER:
        k = np.concatenate([16 * tiles + 8 * kk + rho for kk in range(2)])
        m = (k[:, None] * np.arange(SPAN)[None, :]) % NPIX
        angle = 2.0 * np.pi * m / NPIX
        rows += [np.cos(angle), -np.sin(angle)]
    return np.concatenate(rows).astype(ml_dtypes.bfloat16)


def order_matrix():
    out = np.zeros((2 * KMAX, 2 * KMAX), np.float32)
    for place, rho in enumerate(ORDER):
        for sign in range(2):
            for kk in range(2):
                for t in range(N_TILE):
                    j = 16 * t + 8 * kk + rho
                    q = KMAX + j if sign == 0 else (KMAX - j if j else 0)
                    out[q, place * LANES + sign * 64 + kk * N_TILE + t] = 1.0
    return out.astype(ml_dtypes.bfloat16)


def edge_waves():
    step = lax.broadcasted_iota(jnp.int32, (1, SPAN), 1) & 7
    diag = jnp.where(step & 1 == 1, HALF, 1.0)
    cos = jnp.where(step & 3 == 2, 0.0, jnp.where((step >= 3) & (step <= 5), -diag, diag))
    sin = jnp.where(step & 3 == 0, 0.0, jnp.where(step >= 5, -diag, diag))
    return cos.astype(F32), sin.astype(F32)


def dft4(x, sign):
    (r0, i0), (r1, i1), (r2, i2), (r3, i3) = x
    ar, ai, br, bi = r0 + r2, i0 + i2, r0 - r2, i0 - i2
    cr, ci, dr, di = r1 + r3, i1 + i3, r1 - r3, i1 - i3
    if sign < 0:
        dr, di = -dr, -di
    return [(ar + cr, ai + ci), (br - di, bi + dr), (ar - cr, ai - ci), (br + di, bi - dr)]


def dft8(x, sign):
    even = dft4(x[0::2], sign)
    odd = dft4(x[1::2], sign)
    (r1, i1), (r2, i2), (r3, i3) = odd[1:]
    if sign > 0:
        turned = [odd[0], (HALF * (r1 - i1), HALF * (r1 + i1)), (-i2, r2), (-HALF * (r3 + i3), HALF * (r3 - i3))]
    else:
        turned = [odd[0], (HALF * (r1 + i1), HALF * (i1 - r1)), (i2, -r2), (HALF * (i3 - r3), -HALF * (r3 + i3))]
    low = [(a + c, b + d) for (a, b), (c, d) in zip(even, turned)]
    high = [(a - c, b - d) for (a, b), (c, d) in zip(even, turned)]
    return low + high


def dot_nt(a, b):
    return lax.dot_general(a, b, (((1,), (1,)), ((), ())), preferred_element_type=F32)


def dot_nn(a, b):
    return lax.dot_general(a, b, (((1,), (0,)), ((), ())), preferred_element_type=F32)


def dot_tn(a, b):
    return lax.dot_general(a, b, (((0,), (0,)), ((), ())), preferred_element_type=F32)


def table_of(table_ref, *rhos):
    start = PLACE[rhos[0]] * LANES
    return table_ref[start : start + LANES * len(rhos), :]


def columns_kernel(weight_ref, slab_ref, table_ref, out_ref, fold_ref, band_ref):
    step = pl.program_id(0)

    def segment(m):
        cols = slice(m * SPAN, (m + 1) * SPAN)
        total = slab_ref[0, 0, :, cols].astype(F32) * weight_ref[0, 0]
        for layer in range(1, slab_ref.shape[1]):
            total = total + slab_ref[0, layer, :, cols].astype(F32) * weight_ref[0, layer]
        return total

    def keep(index, value):
        fold_ref[index, pl.ds(pl.multiple_of(step * CHUNK, CHUNK), CHUNK), :] = value.astype(BF16)

    x0, x4 = segment(0), segment(4)
    a0, a1 = x0 + x4, x0 - x4
    x2, x6 = segment(2), segment(6)
    a2, a3 = x2 + x6, x2 - x6
    x1, x5 = segment(1), segment(5)
    b0, b1 = x1 + x5, x1 - x5
    x3, x7 = segment(3), segment(7)
    b2, b3 = x3 + x7, x3 - x7
    total, other = a0 + a2, b0 + b2
    keep(0, total + other)
    keep(1, total - other)
    minus, plus = HALF * (b1 - b3), HALF * (b1 + b3)
    keep(2, a1 + minus)
    keep(3, -a3 - plus)
    keep(4, a0 - a2)
    keep(5, b2 - b0)
    keep(6, a1 - minus)
    keep(7, a3 - plus)

    @pl.when(step == pl.num_programs(0) - 1)
    def _():
        def place(rho, re, im):
            for s, part in enumerate((re, im)):
                for kk in range(2):
                    start = rho * LANES + 2 * s + kk
                    band_ref[pl.ds(start, N_TILE, stride=4), :] = part[kk * N_TILE : (kk + 1) * N_TILE]

        for rho in (0, 4):
            got = dot_nt(table_of(table_ref, rho), fold_ref[PLACE[rho]])
            place(rho, got[:64], got[64:])
        for number, (rho, back) in enumerate(DUOS):
            pair = fold_ref[2 + 2 * number : 4 + 2 * number].reshape(2 * ROWS, SPAN)
            got = dot_nt(table_of(table_ref, rho, back), pair)
            cu, cv = got[:64, :ROWS], got[:64, ROWS:]
            su, sv = got[64:128, :ROWS], got[64:128, ROWS:]
            place(rho, cu - sv, cv + su)
            cu, cv = got[128:192, :ROWS], got[128:192, ROWS:]
            su, sv = got[192:, :ROWS], got[192:, ROWS:]
            place(back, cu + sv, su - cv)
        out_ref[...] = band_ref[...].astype(BF16)


def columns(slab, weight, table):
    return pl.pallas_call(
        columns_kernel,
        grid=(ROWS // CHUNK,),
        in_specs=[
            SMEM,
            pl.BlockSpec((1, slab.shape[1], CHUNK, NPIX), lambda i: (0, 0, i, 0)),
            pl.BlockSpec((2 * KMAX, SPAN), lambda i: (0, 0)),
        ],
        out_specs=pl.BlockSpec((2 * KMAX, ROWS), lambda i: (0, 0)),
        out_shape=jax.ShapeDtypeStruct((2 * KMAX, ROWS), BF16),
        scratch_shapes=[pltpu.VMEM((RADIX, ROWS, SPAN), BF16), pltpu.VMEM((2 * KMAX, ROWS), F32)],
        compiler_params=pltpu.CompilerParams(vmem_limit_bytes=LIMIT),
        name="columns",
    )(weight, slab, table)


def bins_kernel(plane_ref, ell_ref, order_ref, out_ref, rows_ref):
    rows_ref[...] = dot_tn(ell_ref[...], order_ref[...])
    plane = plane_ref[0]
    for kk in range(2):
        row = rows_ref[pl.ds(plane + 8 * kk, 1), :]
        out_ref[8 * kk : 8 * kk + 8, :] = jnp.broadcast_to(row, (8, 2 * KMAX)).astype(jnp.int32)


def mode_bins(plane, ell, order):
    return pl.pallas_call(
        bins_kernel,
        in_specs=[SMEM, VMEM, VMEM],
        out_specs=VMEM,
        out_shape=jax.ShapeDtypeStruct((16, 2 * KMAX), jnp.int32),
        scratch_shapes=[pltpu.VMEM((16, 2 * KMAX), F32)],
        compiler_params=pltpu.CompilerParams(vmem_limit_bytes=LIMIT),
        name="mode_bins",
    )(plane, ell, order)


def kernel_value(index_ref, values_ref, b, p):
    return values_ref[index_ref[b, p]]


def modes_kernel(index_ref, values_ref, band_ref, table_ref, ell_ref, kappa_ref, sums_ref, wide_ref, line_ref):
    wide_ref[...] = band_ref[...].astype(F32)

    def gather(m, s):
        parts = []
        for kk in range(2):
            tiles = [wide_ref[pl.ds((4 * m + u) * 4 + 2 * s + kk, N_PLANE, stride=LANES), :] for u in range(4)]
            parts.append(jnp.concatenate(tiles, axis=1))
        return jnp.concatenate(parts, axis=0)

    folded = dft8([(gather(m, 0), gather(m, 1)) for m in range(RADIX)], -1)
    low = lax.broadcasted_iota(jnp.int32, (16, LANES), 1) < 64

    def lines(rho, ahead, back):
        (cu, cv), (du, dv) = ahead, back
        real = jnp.where(low, cu - pltpu.roll(cv, 64, 1), pltpu.roll(du, 64, 1) + dv)
        imag = jnp.where(low, cv + pltpu.roll(cu, 64, 1), pltpu.roll(dv, 64, 1) - du)
        return real, imag

    def keep(rho, real, imag):
        cols = slice(PLACE[rho] * LANES, (PLACE[rho] + 1) * LANES)
        line_ref[0:16, cols] = real
        line_ref[16:32, cols] = imag

    for rho in (0, 4):
        pair = jnp.concatenate(folded[rho], axis=0).astype(BF16)
        got = dot_nt(pair, table_of(table_ref, rho))
        both = (got[:16], got[16:])
        real, imag = lines(rho, both, both)
        if rho == 0:
            cos, sin = edge_waves()
            up, vp = folded[0]
            edge_re = jnp.sum(up * cos - vp * sin, axis=1, keepdims=True)
            edge_im = jnp.sum(vp * cos + up * sin, axis=1, keepdims=True)
            edge = lax.broadcasted_iota(jnp.int32, (16, LANES), 1) == 64
            real = jnp.where(edge, edge_re, real)
            imag = jnp.where(edge, edge_im, imag)
        keep(rho, real, imag)
    for rho, back in DUOS:
        four = jnp.concatenate(folded[rho] + folded[back], axis=0).astype(BF16)
        got = dot_nt(four, table_of(table_ref, rho, back))
        for place, one in enumerate((rho, back)):
            part = got[:, place * LANES : (place + 1) * LANES]
            duo = ((part[0:16], part[16:32]), (part[32:48], part[48:64]))
            keep(one, *lines(one, duo[place], duo[1 - place]))

    bin_row = lax.broadcasted_iota(jnp.int32, (8, 1), 0) & 3
    columns_of = []
    for p in range(N_PLANE):
        column = jnp.full((8, 1), kernel_value(index_ref, values_ref, 0, p), F32)
        for b in range(1, BINS):
            column = jnp.where(bin_row == b, kernel_value(index_ref, values_ref, b, p), column)
        columns_of.append(column)
    upper = lax.broadcasted_iota(jnp.int32, (8, 2 * KMAX), 0) < 4
    first = [0.0, 0.0]
    second = [0.0, 0.0]
    for s in range(2):
        for kk in range(2):
            start = 16 * s + 8 * kk
            kappa = columns_of[0] * line_ref[start : start + 1, :]
            for p in range(1, N_PLANE):
                kappa = kappa + columns_of[p] * line_ref[start + p : start + p + 1, :]
            kappa_ref[start : start + 8, :] = kappa
            first[kk] = first[kk] + kappa * jnp.where(upper, kappa, pltpu.roll(kappa, 7, 0))
            second[kk] = second[kk] + kappa * pltpu.roll(kappa, 2, 0)

    lane = lax.broadcasted_iota(jnp.int32, (8, LANES), 1)
    spread = [jnp.zeros((8, LANES), F32), jnp.zeros((8, LANES), F32)]
    here = [ell_ref[0:8, :], ell_ref[8:16, :]]
    for ell in range(ELLS):
        for group, terms in enumerate((first, second)):
            chosen = jnp.where(here[0] == ell, terms[0], 0.0) + jnp.where(here[1] == ell, terms[1], 0.0)
            spread[group] = jnp.where(lane & 15 == ell, jnp.sum(chosen, axis=1, keepdims=True), spread[group])
    own = (lane >> 4) == lax.broadcasted_iota(jnp.int32, (8, LANES), 0)
    rows = [jnp.sum(jnp.where(own, part, 0.0), axis=0, keepdims=True) for part in spread]
    even = lax.broadcasted_iota(jnp.int32, (8, LANES), 0) & 1 == 0
    pattern = jnp.where(even, rows[0], rows[1])
    sums_ref[...] = jnp.broadcast_to(pattern[None], (N_DEV // 4, 8, LANES)).reshape(2 * N_DEV, LANES)


def modes(index, values, band, table, ell):
    return pl.pallas_call(
        modes_kernel,
        in_specs=[SMEM, SMEM, VMEM, VMEM, VMEM],
        out_specs=[VMEM, VMEM],
        out_shape=[
            jax.ShapeDtypeStruct((32, 2 * KMAX), F32),
            jax.ShapeDtypeStruct((2 * N_DEV, LANES), F32),
        ],
        scratch_shapes=[pltpu.VMEM((2 * KMAX, ROWS), F32), pltpu.VMEM((32, 2 * KMAX), F32)],
        compiler_params=pltpu.CompilerParams(vmem_limit_bytes=LIMIT),
        name="modes",
    )(index, values, band, table, ell)


def adjoint_kernel(
    index_ref, values_ref, sums_ref, kappa_ref, ell_ref, target_ref, table_ref,
    spectra_ref, out_ref, weight_ref, line_ref, wide_ref,
):
    total = jnp.sum(sums_ref[...].reshape(N_DEV // 4, 8, LANES), axis=0)
    total = total + pltpu.roll(total, 2, 0)
    total = total + pltpu.roll(total, 4, 0)
    lane = lax.broadcasted_iota(jnp.int32, (1, LANES), 1)
    area = (2.0 * lane.astype(F32) + 1.0) * (float((KMAX // ELLS) ** 2) * (0.5 * math.pi))
    scale = float(NPIX * NPIX) * area
    for row, group in enumerate((FIRST_GROUP, SECOND_GROUP)):
        line = total[row : row + 1, :]
        for place, pair in enumerate(group):
            turned = line if place == 0 else pltpu.roll(line, LANES - 16 * place, 1)
            number = PAIR_ID[pair]
            spectra_ref[number : number + 1, :] = (turned / scale)[:, :ELLS]
    weight_ref[...] = jnp.zeros_like(weight_ref)
    weight_ref[0:10, 0:ELLS] = (spectra_ref[...] - target_ref[...]) * (
        float(KMAX) / (ELLS * NPIX)
    ) / area[:, :ELLS]

    bin_row = lax.broadcasted_iota(jnp.int32, (8, LANES), 0) & 3
    couplings = []
    for j in range(BINS):
        mixed = None
        for i in range(BINS):
            number = PAIR_ID[(i, j)]
            row = weight_ref[number : number + 1, :]
            row = row + row if i == j else row
            mixed = jnp.broadcast_to(row, (8, LANES)) if mixed is None else jnp.where(bin_row == i, row, mixed)
        couplings.append(mixed)
    plane_row = lax.broadcasted_iota(jnp.int32, (8, 1), 0)
    columns_of = []
    for b in range(BINS):
        column = jnp.full((8, 1), kernel_value(index_ref, values_ref, b, 0), F32)
        for p in range(1, N_PLANE):
            column = jnp.where(plane_row == p, kernel_value(index_ref, values_ref, b, p), column)
        columns_of.append(column)

    for tile in range(RADIX):
        cols = slice(tile * LANES, (tile + 1) * LANES)
        for kk in range(2):
            where = ell_ref[8 * kk : 8 * kk + 8, cols]
            mixers = [jnp.take_along_axis(table, where, axis=1) for table in couplings]
            for s in range(2):
                start = 16 * s + 8 * kk
                grad = mixers[0] * kappa_ref[start : start + 1, cols]
                for j in range(1, BINS):
                    grad = grad + mixers[j] * kappa_ref[start + j : start + j + 1, cols]
                grad = grad.astype(BF16).astype(F32)
                line = columns_of[0] * grad[0:1]
                for b in range(1, BINS):
                    line = line + columns_of[b] * grad[b : b + 1]
                line_ref[start : start + 8, cols] = line

    wide_lane = lax.broadcasted_iota(jnp.int32, (16, LANES), 1)
    low = wide_lane < 64

    def factors(rho):
        cols = slice(PLACE[rho] * LANES, (PLACE[rho] + 1) * LANES)
        g0, g1 = line_ref[0:16, cols], line_ref[16:32, cols]
        if rho == 0:
            g0 = jnp.where(wide_lane == 64, 0.0, g0)
            g1 = jnp.where(wide_lane == 64, 0.0, g1)
        t0, t1 = pltpu.roll(g0, 64, 1), pltpu.roll(g1, 64, 1)
        ahead = (jnp.where(low, g0, t1), jnp.where(low, g1, -t0))
        back = (jnp.where(low, t0, -g1), jnp.where(low, t1, g0))
        return ahead, back

    spread = [None] * RADIX
    for rho in (0, 4):
        ahead, back = factors(rho)
        left = jnp.concatenate([ahead[0] + back[0], ahead[1] + back[1]], axis=0).astype(BF16)
        got = dot_nn(left, table_of(table_ref, rho))
        spread[rho] = (got[:16], got[16:])
    start = PLACE[0] * LANES + 64
    edge0 = line_ref[0:16, start : start + 1]
    edge1 = line_ref[16:32, start : start + 1]
    cos, sin = edge_waves()
    spread[0] = (spread[0][0] + edge0 * cos + edge1 * sin, spread[0][1] + edge1 * cos - edge0 * sin)
    for rho, back in DUOS:
        plus, minus = factors(rho)
        plus_back, minus_back = factors(back)
        left = jnp.concatenate(
            [
                jnp.concatenate(plus + minus, axis=0),
                jnp.concatenate(minus_back + plus_back, axis=0),
            ],
            axis=1,
        ).astype(BF16)
        got = dot_nn(left, table_of(table_ref, rho, back))
        spread[rho] = (got[0:16], got[16:32])
        spread[back] = (got[32:48], got[48:64])
    for m, both in enumerate(dft8(spread, 1)):
        for s in range(2):
            for kk in range(2):
                for u in range(4):
                    begin = (4 * m + u) * 4 + 2 * s + kk
                    wide_ref[pl.ds(begin, N_PLANE, stride=LANES), :] = both[s][
                        8 * kk : 8 * kk + 8, u * LANES : (u + 1) * LANES
                    ]
    out_ref[...] = wide_ref[...].astype(BF16)


def adjoint(index, values, sums, kappa, ell, target, table):
    return pl.pallas_call(
        adjoint_kernel,
        in_specs=[SMEM, SMEM, VMEM, VMEM, VMEM, VMEM, VMEM],
        out_specs=[VMEM, VMEM],
        out_shape=[
            jax.ShapeDtypeStruct(target.shape, F32),
            jax.ShapeDtypeStruct((2 * KMAX, ROWS), BF16),
        ],
        scratch_shapes=[
            pltpu.VMEM((16, LANES), F32),
            pltpu.VMEM((32, 2 * KMAX), F32),
            pltpu.VMEM((2 * KMAX, ROWS), F32),
        ],
        compiler_params=pltpu.CompilerParams(vmem_limit_bytes=LIMIT),
        name="adjoint",
    )(index, values, sums, kappa, ell, target, table)


def maps_kernel(band_ref, table_ref, out_ref, wide_ref):
    wide_ref[...] = band_ref[...].astype(F32)

    def block(rho, s):
        parts = [
            wide_ref[pl.ds(rho * LANES + 2 * s + kk, N_TILE, stride=4), :] for kk in range(2)
        ]
        return jnp.concatenate(parts, axis=0)

    flat = []
    for rho in (0, 4):
        left = jnp.concatenate([block(rho, 0), block(rho, 1)], axis=0).astype(BF16)
        flat.append(dot_tn(left, table_of(table_ref, rho)))
    p, q = [None], [None]
    for rho, back in DUOS:
        b0, b1, e0, e1 = block(rho, 0), block(rho, 1), block(back, 0), block(back, 1)
        left = jnp.concatenate(
            [
                jnp.concatenate([b0, b1, e0, e1], axis=0),
                jnp.concatenate([b1, -b0, -e1, e0], axis=0),
            ],
            axis=1,
        ).astype(BF16)
        got = dot_tn(left, table_of(table_ref, rho, back))
        p.append(got[:ROWS])
        q.append(got[ROWS:])
    plus, minus = flat[0] + flat[1], flat[0] - flat[1]

    def put(m, even, odd):
        out_ref[0, :, m * SPAN : (m + 1) * SPAN] = even + odd
        out_ref[0, :, (m + 4) * SPAN : (m + 5) * SPAN] = even - odd

    put(0, plus + p[2], p[1] + p[3])
    put(1, minus - q[2], HALF * (p[1] - q[1] - p[3] - q[3]))
    put(2, plus - p[2], q[3] - q[1])
    put(3, minus + q[2], HALF * (p[3] - p[1] - q[1] - q[3]))


def maps(band, table):
    return pl.pallas_call(
        maps_kernel,
        in_specs=[VMEM, VMEM],
        out_specs=VMEM,
        out_shape=jax.ShapeDtypeStruct((1, ROWS, NPIX), F32),
        scratch_shapes=[pltpu.VMEM((2 * KMAX, ROWS), F32)],
        compiler_params=pltpu.CompilerParams(vmem_limit_bytes=LIMIT),
        name="maps",
    )(band, table)


def body(slab_cells, slab_weight, kernel_table, kernel_index, ell_index, target_spectra):
    table = jnp.asarray(wave_table())
    order = jnp.asarray(order_matrix())
    exchange = functools.partial(
        lax.all_to_all, axis_name=("plane", "tile"), split_axis=0, concat_axis=0, tiled=True
    )
    plane = lax.axis_index("plane").astype(jnp.int32).reshape(1)
    ell_rows = lax.all_gather(ell_index.astype(BF16), "plane", axis=0, tiled=True)
    band = exchange(columns(slab_cells, slab_weight, table))
    ell = mode_bins(plane, ell_rows, order)
    kappa, sums = modes(kernel_index, kernel_table, band, table, ell)
    sums = exchange(sums)
    spectra, adjoint_band = adjoint(
        kernel_index, kernel_table, sums, kappa, ell, target_spectra, table
    )
    return spectra, maps(exchange(adjoint_band), table)


def solution(mesh):
    return jax.shard_map(
        body,
        mesh=mesh,
        in_specs=(
            P("plane", None, "tile", None),
            P("plane", None),
            P(),
            P(),
            P("plane", "tile"),
            P(),
        ),
        out_specs=(P(), P("plane", "tile", None)),
        check_vma=False,
    )
```

time: 551 us -> 124 us (0.23)
  other arithmetic: 175 us -> 0.01 us
  waiting for transfers between devices: 89.6 us -> 0.01 us
  matrix products: 71.3 us -> 0 us
  local copies, waits for them, and re-layouts: 55 us -> 4.9 us
  blocking collectives: 112 us -> 94.1 us
  between operations: 14.7 us -> 0.74 us
  Pallas kernels: 0 us -> 8.21 us
  loops' own time: 6.95 us -> 0 us
  starting transfers between devices: 21.3 us -> 15.7 us
    cos x16 -> x0, other arithmetic: 131 us -> none  [row_tables(): return jnp.stack([jnp.cos(angles), jnp.sin(angles)], axis=0)]
    unnamed x2 -> x0, waiting for transfers between devices: 78.8 us -> none
    psum x1 -> x0, blocking collectives: 75.9 us -> none  [body(): summed = lax.psum(local_sums, ('plane', 'tile'))]
    dot_general x25 -> x0, matrix products: 71.1 us -> none  [the longest x8 29.4 us: forward_rows(): jnp.einsum('cqr,xspr->cqsxp', tables, band_part, precision=HIGHEST)]
    all_to_all x0 -> x2, blocking collectives: none -> 51.7 us  [the longest x1 30.9 us: body(): sums = exchange(sums)]
    another operation x10 -> x0, other arithmetic: 40.9 us -> none
    convert_element_type x6 -> x1, local copies, waits for them, and re-layouts: 18.2 us -> 0.12 us  [body(): ell_index.astype(BF16)]
    another operation x1 -> x0, local copies, waits for them, and re-layouts: 16.4 us -> none  [column_table(): stacked = jnp.stack([jnp.cos(angles), -jnp.sin(angles)], axis=1)]
  transfers between devices with their start and end apart: 3 -> 1, of which waited for: 2 -> 0; matrix products, arithmetic and copies ran while one was open for 7% -> 0% of each run, Pallas kernels for 0% -> 0%
where the time goes in v1:
time: 124 us
  blocking collectives  94.1 us (76%)
  starting transfers between devices  15.7 us (13%)
  Pallas kernels  8.21 us (7%)
  local copies, waits for them, and re-layouts  4.9 us (4%)
    all_gather x1, blocking collectives, body(): lax.all_gather(ell_index.astype(BF16), 'plane', axis=0, tiled=True)  42.5 us
    all_to_all x1, blocking collectives, body(): sums = exchange(sums)  30.9 us
    all_to_all x1, blocking collectives, body(): return (spectra, maps(exchange(adjoint_band), table))  20.7 us
    all_to_all x1, starting transfers between devices, body(): band = exchange(columns(slab_cells, slab_weight, table))  15.7 us
    unnamed x20, local copies, waits for them, and re-layouts  4.78 us
  transfers between devices with their start and end apart: 1, of which 0 were waited for; matrix products, arithmetic and copies ran while one was open for 0% of the time, Pallas kernels for 0%

profile of v1, /device:TPU:1, one launch (start us, length us, event | category | flops | bytes accessed | tf_op | source)
XLA Modules:
  0.0 123.7 jit_solution(7231361048906865830)
XLA Ops:
  0.6 0.0 copy-start
  0.6 1.2 copy-done
  1.9 0.0 copy-start.2
  1.9 2.2 %copy-done.2 = bf16[1,4,128,4096]{3,2,1,0:T(8,128)(2,1)S(1)} copy-done((bf16[1,4,128,4096]{3,2,1,0:T(8,128)(2,1)S(1)}, bf16[1,4,128,4096]{3,2,1,0:T(8,128)(2,1)}, u32[]{:S(2)}) %copy-start.2) | copy-done | bytes 4194328
  4.0 0.7 copy-done.8
  4.7 2.4 %columns.1 = bf16[1024,128]{1,0:T(8,128)(2,1)S(1)} custom-call(f32[1,4]{1,0:T(1,128)S(1)} %copy-done.8, bf16[1,4,128,4096]{3,2,1,0:T(8,128)(2,1)S(1)} %copy-done.2, bf16[1024,512]{1,0:T(8,128)(2,1)S(1)} %copy-done), custom_call_target="tpu_custom_call" | custom-call | tf_op jit(solution)/shard_map/columns/pallas_call | solution.py:170
  7.1 0.0 copy-start.4
  7.1 0.7 copy-done.4
  7.8 15.7 %all-to-all-start = ((bf16[256,4,128]{2,1,0:T(4,128)(2,1)}), bf16[256,4,128]{2,1,0:T(4,128)(2,1)S(1)}, u32[]{:S(2)}, u32[]{:S(2)}) async-start(bf16[256,4,128]{2,1,0:T(4,128)(2,1)} %bitcast.8), calls=%async_computation | async-start | bytes 524288 | tf_op jit(solution)/shard_map/all_to_all | solution.py:486
  23.5 0.0 copy-done.9
  23.5 0.1 copy.11
  23.6 42.5 %all_gather.3.ell_ref = bf16[1024,16]{1,0:T(8,128)(2,1)S(1)} all-gather(bf16[128,16]{1,0:T(8,128)(2,1)S(1)} %copy.11), channel_id=1, replica_groups=mesh['plane'=8,'tile'=32] {'plane'}, dimensions={0}, use_global_device_ids=true | all-gather | bytes 36864 | tf_op jit(solution)/shard_map/all_gather | solution.py:485
  66.1 0.0 copy-done.3
  66.1 0.4 mode_bins.1.ell_ref
  66.5 0.0 all-to-all-done
  66.5 0.0 copy-done.1
  66.5 0.0 copy-done.6
  66.5 0.0 copy-done.7
  66.6 1.8 %modes.1 = (f32[32,1024]{1,0:T(8,128)S(1)}, f32[512,128]{1,0:T(8,128)S(1)}) custom-call(s32[4,8]{1,0:T(4,128)S(1)} %copy-done.6, f32[32]{0:T(128)S(1)} %copy-done.7, bf16[1024,128]{1,0:T(8,128)(2,1)S(1)} %bitcast.7, bf16[1024,512]{1,0:T(8,128)(2,1)S(1)} %copy-done.1, s32[16,1024]{1,0:T(8,128)S(1)} %mode_bins.1.ell_ref), custom_call_target="tpu_custom_call" | custom-call | tf_op jit(solution)/shard_map/modes/pallas_call | solution.py:291
  68.4 30.9 %all_to_all.33 = f32[256,2,128]{2,1,0:T(2,128)S(1)} all-to-all(f32[256,2,128]{2,1,0:T(2,128)S(1)} %bitcast.12), channel_id=1, replica_groups=mesh['plane'=8,'tile'=32] {'plane','tile'}, dimensions={0} | all-to-all | bytes 524288 | tf_op jit(solution)/shard_map/all_to_all | solution.py:489
  99.3 0.0 copy-done.5
  99.3 1.7 %adjoint.1 = (f32[10,16]{1,0:T(8,128)}, bf16[1024,128]{1,0:T(8,128)(2,1)S(1)}) custom-call(s32[4,8]{1,0:T(4,128)S(1)} %copy-done.6, f32[32]{0:T(128)S(1)} %copy-done.7, f32[512,128]{1,0:T(8,128)S(1)} %bitcast.9, f32[32,1024]{1,0:T(8,128)S(1)} %get-tuple-element.7.kappa_ref, s32[16,1024]{1,0:T(8,128)S(1)} %mode_bins.1.ell_ref, f32[10,16]{1,0:T(8,128)S(1)} %copy-done.5, ...), custom_call_target="tpu_custom_call" | custom-call | tf_op jit(solution)/shard_map/adjoint/pallas_call | solution.py:410
  101.0 20.7 %all_to_all.34 = bf16[256,4,128]{2,1,0:T(4,128)(2,1)S(1)} all-to-all(bf16[256,4,128]{2,1,0:T(4,128)(2,1)S(1)} %bitcast.11), channel_id=1, replica_groups=mesh['plane'=8,'tile'=32] {'plane','tile'}, dimensions={0} | all-to-all | bytes 524288 | tf_op jit(solution)/shard_map/all_to_all | solution.py:493
  121.7 1.9 %maps.1 = f32[1,128,4096]{2,1,0:T(8,128)} custom-call(bf16[1024,128]{1,0:T(8,128)(2,1)S(1)} %bitcast.10, bf16[1024,512]{1,0:T(8,128)(2,1)S(1)} %copy-done.1), custom_call_target="tpu_custom_call" | custom-call | tf_op jit(solution)/shard_map/maps/pallas_call | solution.py:467
  (8 shorter events, 0.0 us)
Async XLA Ops:
  0.6 1.2 copy-start
  1.9 2.2 %copy-start.2 = (bf16[1,4,128,4096]{3,2,1,0:T(8,128)(2,1)S(1)}, bf16[1,4,128,4096]{3,2,1,0:T(8,128)(2,1)}, u32[]{:S(2)}) copy-start(bf16[1,4,128,4096]{3,2,1,0:T(8,128)(2,1)} %slab_ref.1) | copy-start | bytes 12582916
  4.0 0.7 copy-start.8
  4.7 18.8 %copy-start.9 = (s32[128,16]{0,1:T(8,128)S(1)}, s32[128,16]{0,1:T(8,128)}, u32[]{:S(2)}) copy-start(s32[128,16]{0,1:T(8,128)} %param.12) | copy-start | bytes 24580
  4.7 61.4 %copy-start.3 = (bf16[1024,1024]{1,0:T(8,128)(2,1)S(1)}, bf16[1024,1024]{1,0:T(8,128)(2,1)}, u32[]{:S(2)}) copy-start(bf16[1024,1024]{1,0:T(8,128)(2,1)} %constant.11.clone.order_ref) | copy-start | bytes 6291460
  7.1 0.7 copy-start.4
  7.8 58.7 %copy-start.1 = (bf16[1024,512]{1,0:T(8,128)(2,1)S(1)}, bf16[1024,512]{1,0:T(8,128)(2,1)}, u32[]{:S(2)}) copy-start(bf16[1024,512]{1,0:T(8,128)(2,1)} %constant.10.clone.table_ref) | copy-start | bytes 3145732
  7.8 58.7 %copy-start.6 = (s32[4,8]{1,0:T(4,128)S(1)}, s32[4,8]{1,0:T(4,128)}, u32[]{:S(2)}) copy-start(s32[4,8]{1,0:T(4,128)} %index_ref.3) | copy-start | bytes 388
  7.8 58.8 %copy-start.7 = (f32[32]{0:T(128)S(1)}, f32[32]{0:T(128)}, u32[]{:S(2)}) copy-start(f32[32]{0:T(128)} %values_ref.3) | copy-start | bytes 388
  7.8 58.7 %all-to-all-start = ((bf16[256,4,128]{2,1,0:T(4,128)(2,1)}), bf16[256,4,128]{2,1,0:T(4,128)(2,1)S(1)}, u32[]{:S(2)}, u32[]{:S(2)}) async-start(bf16[256,4,128]{2,1,0:T(4,128)(2,1)} %bitcast.8), calls=%async_computation | async-start | bytes 524288 | tf_op jit(solution)/shard_map/all_to_all | solution.py:486
  66.1 33.2 %copy-start.5 = (f32[10,16]{1,0:T(8,128)S(1)}, f32[10,16]{1,0:T(8,128)}, u32[]{:S(2)}) copy-start(f32[10,16]{1,0:T(8,128)} %target_ref.1) | copy-start | bytes 1924

commit v2 on v1

--- a/solution.py
+++ b/solution.py
@@ -21,7 +21,9 @@
 N_DEV = N_PLANE * N_TILE
 ROWS = NPIX // N_TILE
 LANES = 128
-CHUNK = 32
+CHUNK = 16
+PACK = 6
+CHUNKS = ROWS // CHUNK
 
 ORDER = (0, 4, 1, 7, 2, 6, 3, 5)
 PLACE = {rho: place for place, rho in enumerate(ORDER)}
@@ -111,109 +113,135 @@
     return table_ref[start : start + LANES * len(rhos), :]
 
 
-def columns_kernel(weight_ref, slab_ref, table_ref, out_ref, fold_ref, band_ref):
-    step = pl.program_id(0)
-
-    def segment(m):
-        cols = slice(m * SPAN, (m + 1) * SPAN)
-        total = slab_ref[0, 0, :, cols].astype(F32) * weight_ref[0, 0]
-        for layer in range(1, slab_ref.shape[1]):
-            total = total + slab_ref[0, layer, :, cols].astype(F32) * weight_ref[0, layer]
-        return total
-
-    def keep(index, value):
-        fold_ref[index, pl.ds(pl.multiple_of(step * CHUNK, CHUNK), CHUNK), :] = value.astype(BF16)
-
-    x0, x4 = segment(0), segment(4)
-    a0, a1 = x0 + x4, x0 - x4
-    x2, x6 = segment(2), segment(6)
-    a2, a3 = x2 + x6, x2 - x6
-    x1, x5 = segment(1), segment(5)
-    b0, b1 = x1 + x5, x1 - x5
-    x3, x7 = segment(3), segment(7)
-    b2, b3 = x3 + x7, x3 - x7
-    total, other = a0 + a2, b0 + b2
-    keep(0, total + other)
-    keep(1, total - other)
-    minus, plus = HALF * (b1 - b3), HALF * (b1 + b3)
-    keep(2, a1 + minus)
-    keep(3, -a3 - plus)
-    keep(4, a0 - a2)
-    keep(5, b2 - b0)
-    keep(6, a1 - minus)
-    keep(7, a3 - plus)
-
-    @pl.when(step == pl.num_programs(0) - 1)
-    def _():
-        def place(rho, re, im):
-            for s, part in enumerate((re, im)):
-                for kk in range(2):
-                    start = rho * LANES + 2 * s + kk
-                    band_ref[pl.ds(start, N_TILE, stride=4), :] = part[kk * N_TILE : (kk + 1) * N_TILE]
-
-        for rho in (0, 4):
-            got = dot_nt(table_of(table_ref, rho), fold_ref[PLACE[rho]])
-            place(rho, got[:64], got[64:])
-        for number, (rho, back) in enumerate(DUOS):
-            pair = fold_ref[2 + 2 * number : 4 + 2 * number].reshape(2 * ROWS, SPAN)
-            got = dot_nt(table_of(table_ref, rho, back), pair)
-            cu, cv = got[:64, :ROWS], got[:64, ROWS:]
-            su, sv = got[64:128, :ROWS], got[64:128, ROWS:]
-            place(rho, cu - sv, cv + su)
-            cu, cv = got[128:192, :ROWS], got[128:192, ROWS:]
-            su, sv = got[192:, :ROWS], got[192:, ROWS:]
-            place(back, cu + sv, su - cv)
-        out_ref[...] = band_ref[...].astype(BF16)
-
-
-def columns(slab, weight, table):
+def columns_kernel(
+    weight_ref, slab_ref, ell_ref, table_ref, out_ref, cells_ref, held_ref, fold_ref, band_ref,
+    scale_ref, bins_ref, sems, table_sem, small_sems,
+):
+    def fetch(chunk):
+        rows = pl.ds(chunk * CHUNK, CHUNK)
+        return pltpu.make_async_copy(slab_ref.at[0, :, rows, :], cells_ref.at[chunk], sems.at[chunk])
+
+    def fetch_table():
+        return pltpu.make_async_copy(table_ref, held_ref, table_sem)
+
+    for chunk in range(CHUNKS):
+        fetch(chunk).start(priority=chunk % 2)
+    small = (
+        pltpu.make_async_copy(weight_ref, scale_ref, small_sems.at[0]),
+        pltpu.make_async_copy(ell_ref, bins_ref, small_sems.at[1]),
+    )
+    for copy in small:
+        copy.start()
+    fetch_table().start()
+    for copy in small:
+        copy.wait()
+    weights = [scale_ref[0, layer] for layer in range(slab_ref.shape[1])]
+
+    def butterfly(chunk, start):
+        def segment(m):
+            cols = slice(m * SPAN + start, m * SPAN + start + LANES)
+            total = cells_ref[chunk, 0, :, cols].astype(F32) * weights[0]
+            for layer in range(1, len(weights)):
+                total = total + cells_ref[chunk, layer, :, cols].astype(F32) * weights[layer]
+            return total
+
+        def keep(index, value):
+            fold_ref[index, chunk * CHUNK : (chunk + 1) * CHUNK, start : start + LANES] = value.astype(BF16)
+
+        x0, x4 = segment(0), segment(4)
+        a0, a1 = x0 + x4, x0 - x4
+        x2, x6 = segment(2), segment(6)
+        a2, a3 = x2 + x6, x2 - x6
+        x1, x5 = segment(1), segment(5)
+        b0, b1 = x1 + x5, x1 - x5
+        x3, x7 = segment(3), segment(7)
+        b2, b3 = x3 + x7, x3 - x7
+        total, other = a0 + a2, b0 + b2
+        keep(0, total + other)
+        keep(1, total - other)
+        minus, plus = HALF * (b1 - b3), HALF * (b1 + b3)
+        keep(2, a1 + minus)
+        keep(3, -a3 - plus)
+        keep(4, a0 - a2)
+        keep(5, b2 - b0)
+        keep(6, a1 - minus)
+        keep(7, a3 - plus)
+
+    for p in range(N_PLANE):
+        for kk in range(2):
+            line = bins_ref[p + 8 * kk : p + 8 * kk + 1, :].astype(F32)
+            start = p * N_TILE * PACK + 4 + kk
+            band_ref[pl.ds(start, N_TILE, stride=PACK), :] = jnp.broadcast_to(line, (N_TILE, ROWS))
+
+    for chunk in range(CHUNKS):
+        fetch(chunk).wait()
+        for start in range(0, SPAN, LANES):
+            butterfly(chunk, start)
+    fetch_table().wait()
+
+    def place(rho, re, im):
+        for s, part in enumerate((re, im)):
+            for kk in range(2):
+                start = rho * N_TILE * PACK + 2 * s + kk
+                band_ref[pl.ds(start, N_TILE, stride=PACK), :] = part[kk * N_TILE : (kk + 1) * N_TILE]
+
+    for rho in (0, 4):
+        got = dot_nt(table_of(held_ref, rho), fold_ref[PLACE[rho]])
+        place(rho, got[:64], got[64:])
+    for number, (rho, back) in enumerate(DUOS):
+        pair = fold_ref[2 + 2 * number : 4 + 2 * number].reshape(2 * ROWS, SPAN)
+        got = dot_nt(table_of(held_ref, rho, back), pair)
+        cu, cv = got[:64, :ROWS], got[:64, ROWS:]
+        su, sv = got[64:128, :ROWS], got[64:128, ROWS:]
+        place(rho, cu - sv, cv + su)
+        cu, cv = got[128:192, :ROWS], got[128:192, ROWS:]
+        su, sv = got[192:, :ROWS], got[192:, ROWS:]
+        place(back, cu + sv, su - cv)
+    out_ref[...] = band_ref[...].astype(BF16)
+
+
+def columns(slab, weight, ell, table):
+    hbm = pl.BlockSpec(memory_space=pltpu.HBM)
     return pl.pallas_call(
         columns_kernel,
-        grid=(ROWS // CHUNK,),
-        in_specs=[
-            SMEM,
-            pl.BlockSpec((1, slab.shape[1], CHUNK, NPIX), lambda i: (0, 0, i, 0)),
-            pl.BlockSpec((2 * KMAX, SPAN), lambda i: (0, 0)),
+        in_specs=[hbm] * 4,
+        out_specs=VMEM,
+        out_shape=jax.ShapeDtypeStruct((N_DEV * PACK, ROWS), BF16),
+        scratch_shapes=[
+            pltpu.VMEM((CHUNKS, slab.shape[1], CHUNK, NPIX), BF16),
+            pltpu.VMEM(table.shape, BF16),
+            pltpu.VMEM((RADIX, ROWS, SPAN), BF16),
+            pltpu.VMEM((N_DEV * PACK, ROWS), F32),
+            pltpu.SMEM(weight.shape, F32),
+            pltpu.VMEM(ell.shape, jnp.int32),
+            pltpu.SemaphoreType.DMA((CHUNKS,)),
+            pltpu.SemaphoreType.DMA,
+            pltpu.SemaphoreType.DMA((2,)),
         ],
-        out_specs=pl.BlockSpec((2 * KMAX, ROWS), lambda i: (0, 0)),
-        out_shape=jax.ShapeDtypeStruct((2 * KMAX, ROWS), BF16),
-        scratch_shapes=[pltpu.VMEM((RADIX, ROWS, SPAN), BF16), pltpu.VMEM((2 * KMAX, ROWS), F32)],
-        compiler_params=pltpu.CompilerParams(vmem_limit_bytes=LIMIT),
+        compiler_params=pltpu.CompilerParams(vmem_limit_bytes=60 * 1024 * 1024),
         name="columns",
-    )(weight, slab, table)
-
-
-def bins_kernel(plane_ref, ell_ref, order_ref, out_ref, rows_ref):
-    rows_ref[...] = dot_tn(ell_ref[...], order_ref[...])
-    plane = plane_ref[0]
-    for kk in range(2):
-        row = rows_ref[pl.ds(plane + 8 * kk, 1), :]
-        out_ref[8 * kk : 8 * kk + 8, :] = jnp.broadcast_to(row, (8, 2 * KMAX)).astype(jnp.int32)
-
-
-def mode_bins(plane, ell, order):
-    return pl.pallas_call(
-        bins_kernel,
-        in_specs=[SMEM, VMEM, VMEM],
-        out_specs=VMEM,
-        out_shape=jax.ShapeDtypeStruct((16, 2 * KMAX), jnp.int32),
-        scratch_shapes=[pltpu.VMEM((16, 2 * KMAX), F32)],
-        compiler_params=pltpu.CompilerParams(vmem_limit_bytes=LIMIT),
-        name="mode_bins",
-    )(plane, ell, order)
+    )(weight, slab, ell, table)
 
 
 def kernel_value(index_ref, values_ref, b, p):
     return values_ref[index_ref[b, p]]
 
 
-def modes_kernel(index_ref, values_ref, band_ref, table_ref, ell_ref, kappa_ref, sums_ref, wide_ref, line_ref):
+def modes_kernel(
+    tile_ref, index_ref, values_ref, band_ref, table_ref, order_ref,
+    kappa_ref, sums_ref, ell_ref, wide_ref, line_ref,
+):
     wide_ref[...] = band_ref[...].astype(F32)
+    bins = tile_ref[0] * PACK + 4
+    for kk in range(2):
+        parts = [wide_ref[pl.ds(bins + p * N_TILE * PACK + kk, 1), :] for p in range(N_PLANE)]
+        line = jnp.broadcast_to(jnp.concatenate(parts, axis=1), (16, 2 * KMAX)).astype(BF16)
+        ell_ref[8 * kk : 8 * kk + 8, :] = dot_nn(line, order_ref[...])[:8].astype(jnp.int32)
 
     def gather(m, s):
         parts = []
         for kk in range(2):
-            tiles = [wide_ref[pl.ds((4 * m + u) * 4 + 2 * s + kk, N_PLANE, stride=LANES), :] for u in range(4)]
+            tiles = [wide_ref[pl.ds((4 * m + u) * PACK + 2 * s + kk, N_PLANE, stride=N_TILE * PACK), :] for u in range(4)]
             parts.append(jnp.concatenate(tiles, axis=1))
         return jnp.concatenate(parts, axis=0)
 
@@ -287,19 +315,20 @@
     sums_ref[...] = jnp.broadcast_to(pattern[None], (N_DEV // 4, 8, LANES)).reshape(2 * N_DEV, LANES)
 
 
-def modes(index, values, band, table, ell):
+def modes(tile, index, values, band, table, order):
     return pl.pallas_call(
         modes_kernel,
-        in_specs=[SMEM, SMEM, VMEM, VMEM, VMEM],
-        out_specs=[VMEM, VMEM],
+        in_specs=[SMEM, SMEM, SMEM, VMEM, VMEM, VMEM],
+        out_specs=[VMEM, VMEM, VMEM],
         out_shape=[
             jax.ShapeDtypeStruct((32, 2 * KMAX), F32),
             jax.ShapeDtypeStruct((2 * N_DEV, LANES), F32),
+            jax.ShapeDtypeStruct((16, 2 * KMAX), jnp.int32),
         ],
-        scratch_shapes=[pltpu.VMEM((2 * KMAX, ROWS), F32), pltpu.VMEM((32, 2 * KMAX), F32)],
+        scratch_shapes=[pltpu.VMEM((N_DEV * PACK, ROWS), F32), pltpu.VMEM((32, 2 * KMAX), F32)],
         compiler_params=pltpu.CompilerParams(vmem_limit_bytes=LIMIT),
         name="modes",
-    )(index, values, band, table, ell)
+    )(tile, index, values, band, table, order)
 
 
 def adjoint_kernel(
@@ -481,11 +510,10 @@
     exchange = functools.partial(
         lax.all_to_all, axis_name=("plane", "tile"), split_axis=0, concat_axis=0, tiled=True
     )
-    plane = lax.axis_index("plane").astype(jnp.int32).reshape(1)
-    ell_rows = lax.all_gather(ell_index.astype(BF16), "plane", axis=0, tiled=True)
-    band = exchange(columns(slab_cells, slab_weight, table))
-    ell = mode_bins(plane, ell_rows, order)
-    kappa, sums = modes(kernel_index, kernel_table, band, table, ell)
+    tile = lax.axis_index("tile").astype(jnp.int32).reshape(1)
+    band = columns(slab_cells, slab_weight, ell_index.T, table)
+    band = exchange(band.reshape(-1, 2, ROWS)).reshape(-1, ROWS)
+    kappa, sums, ell = modes(tile, kernel_index, kernel_table, band, table, order)
     sums = exchange(sums)
     spectra, adjoint_band = adjoint(
         kernel_index, kernel_table, sums, kappa, ell, target_spectra, table

time: 124 us -> 86.8 us (0.70)
  blocking collectives: 94.1 us -> 41.3 us
  waiting for transfers between devices: 0.01 us -> 18.5 us
  local copies, waits for them, and re-layouts: 4.9 us -> 0.03 us
  Pallas kernels: 8.21 us -> 10.3 us
    all_gather x1 -> x0, blocking collectives: 42.5 us -> none  [body(): lax.all_gather(ell_index.astype(BF16), 'plane', axis=0, tiled=True)]
    all_to_all x1, waiting for transfers between devices: 0.01 us -> 18.5 us  [body(): band = exchange(band.reshape(-1, 2, ROWS)).reshape(-1, ROWS)]
    all_to_all x1, blocking collectives: 30.9 us -> 20.6 us  [body(): sums = exchange(sums)]
    unnamed x20 -> x10, local copies, waits for them, and re-layouts: 4.78 us -> 0.03 us
    pallas_call x3 -> x2, Pallas kernels: 4.58 us -> 6.72 us  [the longest x1 4.4 us: columns(): pl.pallas_call(columns_kernel, in_specs=[hbm] * 4, out_specs=VMEM, out_sh...]
  transfers between devices with their start and end apart: 1 -> 1, of which waited for: 0 -> 1; matrix products, arithmetic and copies ran while one was open for 0% -> 0% of each run, Pallas kernels for 0% -> 0%
where the time goes in v2:
time: 86.8 us; the launch traced here: 86.6 us
  blocking collectives  41.3 us (48%)
  waiting for transfers between devices  18.5 us (21%)
  starting transfers between devices  15.7 us (18%)
  Pallas kernels  10.3 us (12%)
    all_to_all x1, blocking collectives, body(): return (spectra, maps(exchange(adjoint_band), table))  20.7 us
    all_to_all x1, blocking collectives, body(): sums = exchange(sums)  20.6 us
    all_to_all x1, waiting for transfers between devices, body(): band = exchange(band.reshape(-1, 2, ROWS)).reshape(-1, ROWS)  18.5 us
    all_to_all x1, starting transfers between devices, body(): band = exchange(band.reshape(-1, 2, ROWS)).reshape(-1, ROWS)  15.7 us
    pallas_call x1, Pallas kernels, columns(): pl.pallas_call(columns_kernel, in_specs=[hbm] * 4, out_specs=VMEM, out_sh...  4.4 us
    pallas_call x1, Pallas kernels, modes(): pl.pallas_call(modes_kernel, in_specs=[SMEM, SMEM, SMEM, VMEM, VMEM, VMEM...  2.31 us
    pallas_call x1, Pallas kernels, maps(): pl.pallas_call(maps_kernel, in_specs=[VMEM, VMEM], out_specs=VMEM, out_sh...  1.94 us
  transfers between devices with their start and end apart: 1, of which 1 were waited for; matrix products, arithmetic and copies ran while one was open for 0% of the time, Pallas kernels for 0%

profile of v2, /device:TPU:1, one launch (start us, length us, event | category | flops | bytes accessed | tf_op | source)
XLA Modules:
  0.0 86.6 jit_solution(15381334229828246698)
XLA Ops:
  0.6 0.0 copy-start
  0.6 0.0 copy-start.1
  0.7 0.0 copy-start.2
  0.7 0.0 copy-start.4
  0.7 4.4 %columns.1 = bf16[1536,128]{1,0:T(8,128)(2,1)} custom-call(f32[1,4]{1,0:T(1,128)} %weight_ref.1, bf16[1,4,128,4096]{3,2,1,0:T(8,128)(2,1)} %slab_ref.1, s32[16,128]{1,0:T(8,128)} %bitcast.14, bf16[1024,512]{1,0:T(8,128)(2,1)} %constant.8.clone.table_ref), custom_call_target="tpu_custom_call" | custom-call | tf_op jit(solution)/shard_map/columns/pallas_call | solution.py:205
  5.1 15.7 %all-to-all-start = ((bf16[768,2,128]{2,1,0:T(2,128)(2,1)}), bf16[768,2,128]{2,1,0:T(2,128)(2,1)S(1)}, u32[]{:S(2)}, u32[]{:S(2)}) async-start(bf16[768,2,128]{2,1,0:T(2,128)(2,1)} %bitcast.13), calls=%async_computation | async-start | bytes 786432 | tf_op jit(solution)/shard_map/all_to_all | solution.py:515
  20.8 0.0 copy-start.3
  20.8 18.5 %all-to-all-done = bf16[768,2,128]{2,1,0:T(2,128)(2,1)S(1)} async-done(((bf16[768,2,128]{2,1,0:T(2,128)(2,1)}), bf16[768,2,128]{2,1,0:T(2,128)(2,1)S(1)}, u32[]{:S(2)}, u32[]{:S(2)}) %all-to-all-start) | async-done | bytes 393248 | tf_op jit(solution)/shard_map/all_to_all | solution.py:515
  39.3 0.0 copy-done
  39.3 0.0 copy-done.1
  39.3 0.0 copy-done.2
  39.3 0.0 copy-done.4
  39.3 2.3 %modes.1 = (f32[32,1024]{1,0:T(8,128)S(1)}, f32[512,128]{1,0:T(8,128)S(1)}, s32[16,1024]{1,0:T(8,128)S(1)}) custom-call(s32[1]{0:T(128)} %bitcast.tile_ref, s32[4,8]{1,0:T(4,128)S(1)} %copy-done.2, f32[32]{0:T(128)S(1)} %copy-done.4, bf16[1536,128]{1,0:T(8,128)(2,1)S(1)} %bitcast.8, bf16[1024,512]{1,0:T(8,128)(2,1)S(1)} %copy-done, ...), custom_call_target="tpu_custom_call" | custom-call | tf_op jit(solution)/shard_map/modes/pallas_call | solution.py:319
  41.7 20.6 %all_to_all.27 = f32[256,2,128]{2,1,0:T(2,128)S(1)} all-to-all(f32[256,2,128]{2,1,0:T(2,128)S(1)} %bitcast.11), channel_id=1, replica_groups=mesh['plane'=8,'tile'=32] {'plane','tile'}, dimensions={0} | all-to-all | bytes 524288 | tf_op jit(solution)/shard_map/all_to_all | solution.py:517
  62.3 0.0 copy-done.3
  62.3 1.7 %adjoint.1 = (f32[10,16]{1,0:T(8,128)}, bf16[1024,128]{1,0:T(8,128)(2,1)S(1)}) custom-call(s32[4,8]{1,0:T(4,128)S(1)} %copy-done.2, f32[32]{0:T(128)S(1)} %copy-done.4, f32[512,128]{1,0:T(8,128)S(1)} %bitcast.9, f32[32,1024]{1,0:T(8,128)S(1)} %get-tuple-element.8.kappa_ref, s32[16,1024]{1,0:T(8,128)S(1)} %get-tuple-element.9.ell_ref, ...), custom_call_target="tpu_custom_call" | custom-call | tf_op jit(solution)/shard_map/adjoint/pallas_call | solution.py:439
  64.0 20.7 %all_to_all.28 = bf16[256,4,128]{2,1,0:T(4,128)(2,1)S(1)} all-to-all(bf16[256,4,128]{2,1,0:T(4,128)(2,1)S(1)} %bitcast.12), channel_id=1, replica_groups=mesh['plane'=8,'tile'=32] {'plane','tile'}, dimensions={0} | all-to-all | bytes 524288 | tf_op jit(solution)/shard_map/all_to_all | solution.py:521
  84.7 1.9 %maps.1 = f32[1,128,4096]{2,1,0:T(8,128)} custom-call(bf16[1024,128]{1,0:T(8,128)(2,1)S(1)} %bitcast.10, bf16[1024,512]{1,0:T(8,128)(2,1)S(1)} %copy-done), custom_call_target="tpu_custom_call" | custom-call | tf_op jit(solution)/shard_map/maps/pallas_call | solution.py:496
Async XLA Ops:
  0.6 38.7 %copy-start = (bf16[1024,512]{1,0:T(8,128)(2,1)S(1)}, bf16[1024,512]{1,0:T(8,128)(2,1)}, u32[]{:S(2)}) copy-start(bf16[1024,512]{1,0:T(8,128)(2,1)} %constant.8.clone.table_ref) | copy-start | bytes 3145732
  0.6 38.7 %copy-start.1 = (bf16[1024,1024]{1,0:T(8,128)(2,1)S(1)}, bf16[1024,1024]{1,0:T(8,128)(2,1)}, u32[]{:S(2)}) copy-start(bf16[1024,1024]{1,0:T(8,128)(2,1)} %constant.9.clone.order_ref) | copy-start | bytes 6291460
  0.7 38.7 %copy-start.2 = (s32[4,8]{1,0:T(4,128)S(1)}, s32[4,8]{1,0:T(4,128)}, u32[]{:S(2)}) copy-start(s32[4,8]{1,0:T(4,128)} %index_ref.3) | copy-start | bytes 388
  0.7 38.7 %copy-start.4 = (f32[32]{0:T(128)S(1)}, f32[32]{0:T(128)}, u32[]{:S(2)}) copy-start(f32[32]{0:T(128)} %values_ref.3) | copy-start | bytes 388
  5.1 34.2 %all-to-all-start = ((bf16[768,2,128]{2,1,0:T(2,128)(2,1)}), bf16[768,2,128]{2,1,0:T(2,128)(2,1)S(1)}, u32[]{:S(2)}, u32[]{:S(2)}) async-start(bf16[768,2,128]{2,1,0:T(2,128)(2,1)} %bitcast.13), calls=%async_computation | async-start | bytes 786432 | tf_op jit(solution)/shard_map/all_to_all | solution.py:515
  20.8 41.5 %copy-start.3 = (f32[10,16]{1,0:T(8,128)S(1)}, f32[10,16]{1,0:T(8,128)}, u32[]{:S(2)}) copy-start(f32[10,16]{1,0:T(8,128)} %target_ref.1) | copy-start | bytes 1924

commit v3 on v2

v3 whole, which is shorter than its diff:
```python
import functools
import math

import jax
import jax.numpy as jnp
import ml_dtypes
import numpy as np
from jax import lax
from jax.experimental import pallas as pl
from jax.experimental.pallas import tpu as pltpu
from jax.sharding import PartitionSpec as P

NPIX = 4096
KMAX = 512
BINS = 4
ELLS = 16
RADIX = 8
SPAN = NPIX // RADIX
N_PLANE = 8
N_TILE = 32
ROWS = NPIX // N_TILE
LANES = 128
CHUNK = 16
WIDTH = 2 * KMAX + ROWS
PAIRS = BINS * (BINS + 1) // 2
CHUNKS = ROWS // CHUNK

ORDER = (0, 4, 1, 7, 2, 6, 3, 5)
PLACE = {rho: place for place, rho in enumerate(ORDER)}
DUOS = ((1, 7), (2, 6), (3, 5))
HALF = math.sqrt(0.5)

PAIR_ID = {}
for _number, (_i, _j) in enumerate(zip(*np.triu_indices(BINS))):
    PAIR_ID[(int(_i), int(_j))] = PAIR_ID[(int(_j), int(_i))] = _number
FIRST_GROUP = ((0, 0), (1, 1), (2, 2), (3, 3), (0, 1), (1, 2), (2, 3), (3, 0))
SECOND_GROUP = ((0, 2), (1, 3))

F32 = jnp.float32
BF16 = jnp.bfloat16
VMEM = pl.BlockSpec(memory_space=pltpu.VMEM)
SMEM = pl.BlockSpec(memory_space=pltpu.SMEM)
LIMIT = 32 * 1024 * 1024


def wave_table():
    rows = []
    tiles = np.arange(N_TILE)
    for rho in ORDER:
        k = np.concatenate([16 * tiles + 8 * kk + rho for kk in range(2)])
        m = (k[:, None] * np.arange(SPAN)[None, :]) % NPIX
        angle = 2.0 * np.pi * m / NPIX
        rows += [np.cos(angle), -np.sin(angle)]
    return np.concatenate(rows).astype(ml_dtypes.bfloat16)


def order_matrix():
    out = np.zeros((2 * KMAX, 2 * KMAX), np.float32)
    for place, rho in enumerate(ORDER):
        for sign in range(2):
            for kk in range(2):
                for t in range(N_TILE):
                    j = 16 * t + 8 * kk + rho
                    q = KMAX + j if sign == 0 else (KMAX - j if j else 0)
                    out[q, place * LANES + sign * 64 + kk * N_TILE + t] = 1.0
    return out.astype(ml_dtypes.bfloat16)


def edge_waves():
    step = lax.broadcasted_iota(jnp.int32, (1, SPAN), 1) & 7
    diag = jnp.where(step & 1 == 1, HALF, 1.0)
    cos = jnp.where(step & 3 == 2, 0.0, jnp.where((step >= 3) & (step <= 5), -diag, diag))
    sin = jnp.where(step & 3 == 0, 0.0, jnp.where(step >= 5, -diag, diag))
    return cos.astype(F32), sin.astype(F32)


def dft4(x, sign):
    (r0, i0), (r1, i1), (r2, i2), (r3, i3) = x
    ar, ai, br, bi = r0 + r2, i0 + i2, r0 - r2, i0 - i2
    cr, ci, dr, di = r1 + r3, i1 + i3, r1 - r3, i1 - i3
    if sign < 0:
        dr, di = -dr, -di
    return [(ar + cr, ai + ci), (br - di, bi + dr), (ar - cr, ai - ci), (br + di, bi - dr)]


def dft8(x, sign):
    even = dft4(x[0::2], sign)
    odd = dft4(x[1::2], sign)
    (r1, i1), (r2, i2), (r3, i3) = odd[1:]
    if sign > 0:
        turned = [odd[0], (HALF * (r1 - i1), HALF * (r1 + i1)), (-i2, r2), (-HALF * (r3 + i3), HALF * (r3 - i3))]
    else:
        turned = [odd[0], (HALF * (r1 + i1), HALF * (i1 - r1)), (i2, -r2), (HALF * (i3 - r3), -HALF * (r3 + i3))]
    low = [(a + c, b + d) for (a, b), (c, d) in zip(even, turned)]
    high = [(a - c, b - d) for (a, b), (c, d) in zip(even, turned)]
    return low + high


def dot_nt(a, b):
    return lax.dot_general(a, b, (((1,), (1,)), ((), ())), preferred_element_type=F32)


def dot_nn(a, b):
    return lax.dot_general(a, b, (((1,), (0,)), ((), ())), preferred_element_type=F32)


def dot_tn(a, b):
    return lax.dot_general(a, b, (((0,), (0,)), ((), ())), preferred_element_type=F32)


def table_of(table_ref, *rhos):
    start = PLACE[rhos[0]] * LANES
    return table_ref[start : start + LANES * len(rhos), :]


def columns_kernel(
    weight_ref, slab_ref, table_ref, out_ref, cells_ref, held_ref, fold_ref, band_ref,
    scale_ref, sems, table_sem, scale_sem,
):
    def fetch(chunk):
        rows = pl.ds(chunk * CHUNK, CHUNK)
        return pltpu.make_async_copy(slab_ref.at[0, :, rows, :], cells_ref.at[chunk], sems.at[chunk])

    def fetch_table():
        return pltpu.make_async_copy(table_ref, held_ref, table_sem)

    for chunk in range(CHUNKS):
        fetch(chunk).start(priority=chunk % 2)
    scales = pltpu.make_async_copy(weight_ref, scale_ref, scale_sem)
    scales.start()
    fetch_table().start()
    scales.wait()
    weights = [scale_ref[0, layer] for layer in range(slab_ref.shape[1])]

    def butterfly(chunk, start):
        def segment(m):
            cols = slice(m * SPAN + start, m * SPAN + start + LANES)
            total = cells_ref[chunk, 0, :, cols].astype(F32) * weights[0]
            for layer in range(1, len(weights)):
                total = total + cells_ref[chunk, layer, :, cols].astype(F32) * weights[layer]
            return total

        def keep(index, value):
            fold_ref[index, chunk * CHUNK : (chunk + 1) * CHUNK, start : start + LANES] = value.astype(BF16)

        x0, x4 = segment(0), segment(4)
        a0, a1 = x0 + x4, x0 - x4
        x2, x6 = segment(2), segment(6)
        a2, a3 = x2 + x6, x2 - x6
        x1, x5 = segment(1), segment(5)
        b0, b1 = x1 + x5, x1 - x5
        x3, x7 = segment(3), segment(7)
        b2, b3 = x3 + x7, x3 - x7
        total, other = a0 + a2, b0 + b2
        keep(0, total + other)
        keep(1, total - other)
        minus, plus = HALF * (b1 - b3), HALF * (b1 + b3)
        keep(2, a1 + minus)
        keep(3, -a3 - plus)
        keep(4, a0 - a2)
        keep(5, b2 - b0)
        keep(6, a1 - minus)
        keep(7, a3 - plus)

    for chunk in range(CHUNKS):
        fetch(chunk).wait()
        for start in range(0, SPAN, LANES):
            butterfly(chunk, start)
    fetch_table().wait()

    def place(rho, re, im):
        for s, part in enumerate((re, im)):
            for kk in range(2):
                start = 16 * s + 8 * kk + rho
                band_ref[pl.ds(start, N_TILE, stride=32), :] = part[kk * N_TILE : (kk + 1) * N_TILE]

    for rho in (0, 4):
        got = dot_nt(table_of(held_ref, rho), fold_ref[PLACE[rho]])
        place(rho, got[:64], got[64:])
    for number, (rho, back) in enumerate(DUOS):
        pair = fold_ref[2 + 2 * number : 4 + 2 * number].reshape(2 * ROWS, SPAN)
        got = dot_nt(table_of(held_ref, rho, back), pair)
        cu, cv = got[:64, :ROWS], got[:64, ROWS:]
        su, sv = got[64:128, :ROWS], got[64:128, ROWS:]
        place(rho, cu - sv, cv + su)
        cu, cv = got[128:192, :ROWS], got[128:192, ROWS:]
        su, sv = got[192:, :ROWS], got[192:, ROWS:]
        place(back, cu + sv, su - cv)
    out_ref[...] = band_ref[...].astype(BF16)


def columns(slab, weight, table):
    hbm = pl.BlockSpec(memory_space=pltpu.HBM)
    return pl.pallas_call(
        columns_kernel,
        in_specs=[hbm] * 3,
        out_specs=VMEM,
        out_shape=jax.ShapeDtypeStruct((2 * KMAX, ROWS), BF16),
        scratch_shapes=[
            pltpu.VMEM((CHUNKS, slab.shape[1], CHUNK, NPIX), BF16),
            pltpu.VMEM(table.shape, BF16),
            pltpu.VMEM((RADIX, ROWS, SPAN), BF16),
            pltpu.VMEM((2 * KMAX, ROWS), F32),
            pltpu.SMEM(weight.shape, F32),
            pltpu.SemaphoreType.DMA((CHUNKS,)),
            pltpu.SemaphoreType.DMA,
            pltpu.SemaphoreType.DMA,
        ],
        compiler_params=pltpu.CompilerParams(vmem_limit_bytes=60 * 1024 * 1024),
        name="columns",
    )(weight, slab, table)


def kernel_value(index_ref, values_ref, b, p):
    return values_ref[index_ref[b, p]]


def rows_kernel(band_ref, table_ref, ell_ref, out_ref, fold_ref):
    cos, sin = edge_waves()
    edge_re = jnp.zeros((16, 1), F32)
    edge_im = jnp.zeros((16, 1), F32)
    for u in range(SPAN // LANES):
        cols = slice(u * LANES, (u + 1) * LANES)
        starts = [(4 * m + u) * 32 for m in range(RADIX)]
        parts = [
            tuple(band_ref[start + 16 * s : start + 16 * s + 16, :].astype(F32) for s in range(2))
            for start in starts
        ]
        folded = dft8(parts, -1)
        for rho, (re, im) in enumerate(folded):
            fold_ref[PLACE[rho], 0:16, cols] = re.astype(BF16)
            fold_ref[PLACE[rho], 16:32, cols] = im.astype(BF16)
        up, vp = folded[0]
        edge_re = edge_re + jnp.sum(up * cos[:, cols] - vp * sin[:, cols], axis=1, keepdims=True)
        edge_im = edge_im + jnp.sum(vp * cos[:, cols] + up * sin[:, cols], axis=1, keepdims=True)
    lane = lax.broadcasted_iota(jnp.int32, (16, LANES), 1)
    low = lane < 64

    def lines(ahead, back):
        (cu, cv), (du, dv) = ahead, back
        real = jnp.where(low, cu - pltpu.roll(cv, 64, 1), pltpu.roll(du, 64, 1) + dv)
        imag = jnp.where(low, cv + pltpu.roll(cu, 64, 1), pltpu.roll(dv, 64, 1) - du)
        return real, imag

    def keep(rho, real, imag):
        cols = slice(PLACE[rho] * LANES, (PLACE[rho] + 1) * LANES)
        out_ref[0:16, cols] = real.astype(BF16)
        out_ref[16:32, cols] = imag.astype(BF16)

    for rho in (0, 4):
        got = dot_nt(fold_ref[PLACE[rho]], table_of(table_ref, rho))
        both = (got[:16], got[16:])
        real, imag = lines(both, both)
        if rho == 0:
            real = jnp.where(lane == 64, edge_re, real)
            imag = jnp.where(lane == 64, edge_im, imag)
        keep(rho, real, imag)
    for rho, back in DUOS:
        four = fold_ref[PLACE[rho] : PLACE[rho] + 2].reshape(64, SPAN)
        got = dot_nt(four, table_of(table_ref, rho, back))
        for place, one in enumerate((rho, back)):
            part = got[:, place * LANES : (place + 1) * LANES]
            duo = ((part[0:16], part[16:32]), (part[32:48], part[48:64]))
            keep(one, *lines(duo[place], duo[1 - place]))
    bins = ell_ref[...].astype(F32).astype(BF16)
    out_ref[0:16, 2 * KMAX :] = bins
    out_ref[16:32, 2 * KMAX :] = bins


def rows(band, table, ell):
    return pl.pallas_call(
        rows_kernel,
        in_specs=[VMEM, VMEM, VMEM],
        out_specs=VMEM,
        out_shape=jax.ShapeDtypeStruct((32, WIDTH), BF16),
        scratch_shapes=[pltpu.VMEM((RADIX, 32, SPAN), BF16)],
        compiler_params=pltpu.CompilerParams(vmem_limit_bytes=LIMIT),
        name="rows",
    )(band, table, ell)


def modes_kernel(
    plane_ref, index_ref, values_ref, near_ref, far1_ref, far2_ref, far3_ref, order_ref,
    kappa_ref, sums_ref, ell_ref, lines_ref, terms_ref,
):
    plane = plane_ref[0]
    for number, ref in enumerate((near_ref, far1_ref, far2_ref, far3_ref)):
        for slot in range(2):
            lines_ref[plane ^ (2 * number + slot)] = ref[slot]
    bins = jnp.concatenate([lines_ref[p, 0:16, 2 * KMAX :] for p in range(N_PLANE)], axis=1)
    ell_ref[...] = dot_nn(bins, order_ref[...]).astype(jnp.int32)
    weights = [[kernel_value(index_ref, values_ref, b, p) for p in range(N_PLANE)] for b in range(BINS)]
    for tile in range(RADIX):
        cols = slice(tile * LANES, (tile + 1) * LANES)
        kappa = [None] * BINS
        for p in range(N_PLANE):
            line = lines_ref[p, :, cols].astype(F32)
            for b in range(BINS):
                term = line * weights[b][p]
                kappa[b] = term if p == 0 else kappa[b] + term
        for b in range(BINS):
            kappa_ref[32 * b : 32 * b + 32, cols] = kappa[b]
        for number, (i, j) in enumerate(FIRST_GROUP + SECOND_GROUP):
            both = kappa[i] * kappa[j]
            terms_ref[number, :, cols] = both[0:16] + both[16:32]

    lane = lax.broadcasted_iota(jnp.int32, (8, LANES), 1)
    sub = lax.broadcasted_iota(jnp.int32, (8, LANES), 0)
    spread = [jnp.zeros((8, LANES), F32), jnp.zeros((8, LANES), F32)]
    for ell in range(ELLS):
        here = ell_ref[...] == ell
        held = [jnp.zeros((8, LANES), F32), jnp.zeros((8, LANES), F32)]
        for number in range(PAIRS):
            chosen = jnp.where(here, terms_ref[number], 0.0)
            chosen = chosen[0:8] + chosen[8:16]
            total = chosen[:, 0:LANES]
            for tile in range(1, RADIX):
                total = total + chosen[:, tile * LANES : (tile + 1) * LANES]
            total = jnp.sum(total, axis=0, keepdims=True)
            group, row = divmod(number, 8)
            held[group] = jnp.where(sub == row, total, held[group])
        for group in range(2):
            total = jnp.sum(held[group], axis=1, keepdims=True)
            spread[group] = jnp.where(lane & 15 == ell, total, spread[group])
    own = (lane >> 4) == sub
    sums = [jnp.sum(jnp.where(own, part, 0.0), axis=0, keepdims=True) for part in spread]
    pattern = jnp.where(sub & 1 == 0, sums[0], sums[1])
    sums_ref[...] = jnp.broadcast_to(pattern[None], (N_TILE // 4, 8, LANES)).reshape(2 * N_TILE, LANES)


def modes(plane, index, values, near, far, order):
    return pl.pallas_call(
        modes_kernel,
        in_specs=[SMEM, SMEM, SMEM] + [VMEM] * 5,
        out_specs=[VMEM, VMEM, VMEM],
        out_shape=[
            jax.ShapeDtypeStruct((32 * BINS, 2 * KMAX), F32),
            jax.ShapeDtypeStruct((2 * N_TILE, LANES), F32),
            jax.ShapeDtypeStruct((16, 2 * KMAX), jnp.int32),
        ],
        scratch_shapes=[
            pltpu.VMEM((N_PLANE, 32, WIDTH), BF16),
            pltpu.VMEM((PAIRS, 16, 2 * KMAX), F32),
        ],
        compiler_params=pltpu.CompilerParams(vmem_limit_bytes=LIMIT),
        name="modes",
    )(plane, index, values, near, *far, order)


def adjoint_kernel(
    plane_ref, index_ref, values_ref, sums_ref, kappa_ref, ell_ref, target_ref, table_ref,
    spectra_ref, out_ref, weight_ref, line_ref, spread_ref,
):
    total = jnp.sum(sums_ref[...].reshape(N_TILE // 4, 8, LANES), axis=0)
    total = total + pltpu.roll(total, 2, 0)
    total = total + pltpu.roll(total, 4, 0)
    lane = lax.broadcasted_iota(jnp.int32, (1, LANES), 1)
    area = (2.0 * lane.astype(F32) + 1.0) * (float((KMAX // ELLS) ** 2) * (0.5 * math.pi))
    scale = float(NPIX * NPIX) * area
    for row, group in enumerate((FIRST_GROUP, SECOND_GROUP)):
        line = total[row : row + 1, :]
        for place, pair in enumerate(group):
            turned = line if place == 0 else pltpu.roll(line, LANES - 16 * place, 1)
            number = PAIR_ID[pair]
            spectra_ref[number : number + 1, :] = (turned / scale)[:, :ELLS]
    weight_ref[...] = jnp.zeros_like(weight_ref)
    weight_ref[0:10, 0:ELLS] = (spectra_ref[...] - target_ref[...]) * (
        float(KMAX) / (ELLS * NPIX)
    ) / area[:, :ELLS]

    couplings = []
    for number in range(PAIRS):
        row = weight_ref[number : number + 1, :]
        row = row + row if number in (PAIR_ID[(i, i)] for i in range(BINS)) else row
        couplings.append(jnp.broadcast_to(row, (8, LANES)))
    plane = plane_ref[0]
    weights = [kernel_value(index_ref, values_ref, b, plane) for b in range(BINS)]

    for tile in range(RADIX):
        cols = slice(tile * LANES, (tile + 1) * LANES)
        for half in range(0, 16, 8):
            where = ell_ref[half : half + 8, cols]
            mixers = [jnp.take_along_axis(table, where, axis=1) for table in couplings]
            for s in range(2):
                start = 16 * s + half
                kappa = [kappa_ref[32 * b + start : 32 * b + start + 8, cols] for b in range(BINS)]
                line = None
                for i in range(BINS):
                    grad = mixers[PAIR_ID[(i, 0)]] * kappa[0]
                    for j in range(1, BINS):
                        grad = grad + mixers[PAIR_ID[(i, j)]] * kappa[j]
                    term = grad.astype(BF16).astype(F32) * weights[i]
                    line = term if i == 0 else line + term
                line_ref[start : start + 8, cols] = line

    wide_lane = lax.broadcasted_iota(jnp.int32, (16, LANES), 1)
    low = wide_lane < 64

    def factors(rho):
        cols = slice(PLACE[rho] * LANES, (PLACE[rho] + 1) * LANES)
        g0, g1 = line_ref[0:16, cols], line_ref[16:32, cols]
        if rho == 0:
            g0 = jnp.where(wide_lane == 64, 0.0, g0)
            g1 = jnp.where(wide_lane == 64, 0.0, g1)
        t0, t1 = pltpu.roll(g0, 64, 1), pltpu.roll(g1, 64, 1)
        ahead = (jnp.where(low, g0, t1), jnp.where(low, g1, -t0))
        back = (jnp.where(low, t0, -g1), jnp.where(low, t1, g0))
        return ahead, back

    def spread(rho, re, im):
        spread_ref[2 * rho] = re
        spread_ref[2 * rho + 1] = im

    start = PLACE[0] * LANES + 64
    edge0 = line_ref[0:16, start : start + 1]
    edge1 = line_ref[16:32, start : start + 1]
    cos, sin = edge_waves()
    for rho in (0, 4):
        ahead, back = factors(rho)
        left = jnp.concatenate([ahead[0] + back[0], ahead[1] + back[1]], axis=0).astype(BF16)
        got = dot_nn(left, table_of(table_ref, rho))
        re, im = got[:16], got[16:]
        if rho == 0:
            re = re + edge0 * cos + edge1 * sin
            im = im + edge1 * cos - edge0 * sin
        spread(rho, re, im)
    for rho, back in DUOS:
        plus, minus = factors(rho)
        plus_back, minus_back = factors(back)
        left = jnp.concatenate(
            [
                jnp.concatenate(plus + minus, axis=0),
                jnp.concatenate(minus_back + plus_back, axis=0),
            ],
            axis=1,
        ).astype(BF16)
        got = dot_nn(left, table_of(table_ref, rho, back))
        spread(rho, got[0:16], got[16:32])
        spread(back, got[32:48], got[48:64])
    for u in range(SPAN // LANES):
        cols = slice(u * LANES, (u + 1) * LANES)
        parts = [(spread_ref[2 * rho, :, cols], spread_ref[2 * rho + 1, :, cols]) for rho in range(RADIX)]
        for m, both in enumerate(dft8(parts, 1)):
            for s in range(2):
                begin = (4 * m + u) * 32 + 16 * s
                out_ref[begin : begin + 16, :] = both[s].astype(BF16)


def adjoint(plane, index, values, sums, kappa, ell, target, table):
    return pl.pallas_call(
        adjoint_kernel,
        in_specs=[SMEM, SMEM, SMEM, VMEM, VMEM, VMEM, VMEM, VMEM],
        out_specs=[VMEM, VMEM],
        out_shape=[
            jax.ShapeDtypeStruct(target.shape, F32),
            jax.ShapeDtypeStruct((2 * KMAX, ROWS), BF16),
        ],
        scratch_shapes=[
            pltpu.VMEM((16, LANES), F32),
            pltpu.VMEM((32, 2 * KMAX), F32),
            pltpu.VMEM((2 * RADIX, 16, SPAN), F32),
        ],
        compiler_params=pltpu.CompilerParams(vmem_limit_bytes=LIMIT),
        name="adjoint",
    )(plane, index, values, sums, kappa, ell, target, table)


def maps_kernel(band_ref, table_ref, out_ref, wide_ref):
    wide_ref[...] = band_ref[...].astype(F32)

    def block(rho, s):
        parts = [
            wide_ref[pl.ds(16 * s + 8 * kk + rho, N_TILE, stride=32), :] for kk in range(2)
        ]
        return jnp.concatenate(parts, axis=0)

    flat = []
    for rho in (0, 4):
        left = jnp.concatenate([block(rho, 0), block(rho, 1)], axis=0).astype(BF16)
        flat.append(dot_tn(left, table_of(table_ref, rho)))
    p, q = [None], [None]
    for rho, back in DUOS:
        b0, b1, e0, e1 = block(rho, 0), block(rho, 1), block(back, 0), block(back, 1)
        left = jnp.concatenate(
            [
                jnp.concatenate([b0, b1, e0, e1], axis=0),
                jnp.concatenate([b1, -b0, -e1, e0], axis=0),
            ],
            axis=1,
        ).astype(BF16)
        got = dot_tn(left, table_of(table_ref, rho, back))
        p.append(got[:ROWS])
        q.append(got[ROWS:])
    plus, minus = flat[0] + flat[1], flat[0] - flat[1]

    def put(m, even, odd):
        out_ref[0, :, m * SPAN : (m + 1) * SPAN] = even + odd
        out_ref[0, :, (m + 4) * SPAN : (m + 5) * SPAN] = even - odd

    put(0, plus + p[2], p[1] + p[3])
    put(1, minus - q[2], HALF * (p[1] - q[1] - p[3] - q[3]))
    put(2, plus - p[2], q[3] - q[1])
    put(3, minus + q[2], HALF * (p[3] - p[1] - q[1] - q[3]))


def maps(band, table):
    return pl.pallas_call(
        maps_kernel,
        in_specs=[VMEM, VMEM],
        out_specs=VMEM,
        out_shape=jax.ShapeDtypeStruct((1, ROWS, NPIX), F32),
        scratch_shapes=[pltpu.VMEM((2 * KMAX, ROWS), F32)],
        compiler_params=pltpu.CompilerParams(vmem_limit_bytes=LIMIT),
        name="maps",
    )(band, table)


def body(slab_cells, slab_weight, kernel_table, kernel_index, ell_index, target_spectra):
    table = jnp.asarray(wave_table())
    order = jnp.asarray(order_matrix())
    exchange = functools.partial(
        lax.all_to_all, axis_name="tile", split_axis=0, concat_axis=0, tiled=True
    )

    def swap(value, bits):
        return lax.ppermute(value, "plane", [(p, p ^ bits) for p in range(N_PLANE)])

    plane = lax.axis_index("plane").astype(jnp.int32).reshape(1)
    band = exchange(columns(slab_cells, slab_weight, table))
    lines = rows(band, table, ell_index.T)
    near = jnp.stack([lines, swap(lines, 1)])
    far = [swap(near, bits) for bits in (2, 4, 6)]
    kappa, sums, ell = modes(plane, kernel_index, kernel_table, near, far, order)
    spectra, adjoint_band = adjoint(
        plane, kernel_index, kernel_table, exchange(sums), kappa, ell, target_spectra, table
    )
    return spectra, maps(exchange(adjoint_band), table)


def solution(mesh):
    return jax.shard_map(
        body,
        mesh=mesh,
        in_specs=(
            P("plane", None, "tile", None),
            P("plane", None),
            P(),
            P(),
            P("plane", "tile"),
            P(),
        ),
        out_specs=(P(), P("plane", "tile", None)),
        check_vma=False,
    )
```

time: 86.8 us -> 80.1 us (0.923)
  waiting for transfers between devices: 18.5 us -> 9.64 us
  blocking collectives: 41.3 us -> 50.1 us
  starting transfers between devices: 15.7 us -> 7.64 us
  Pallas kernels: 10.3 us -> 11.8 us
    all_to_all x1 -> x0, waiting for transfers between devices: 18.5 us -> none  [body(): band = exchange(band.reshape(-1, 2, ROWS)).reshape(-1, ROWS)]
    all_to_all x1 -> x0, starting transfers between devices: 15.7 us -> none  [body(): band = exchange(band.reshape(-1, 2, ROWS)).reshape(-1, ROWS)]
    all_to_all x1 -> x2, blocking collectives: 20.6 us -> 35.5 us  [the longest x1 21.6 us: body(): band = exchange(columns(slab_cells, slab_weight, table))]
    ppermute x0 -> x4, waiting for transfers between devices: none -> 9.64 us  [swap(): return lax.ppermute(value, 'plane', [(p, p ^ bits) for p in range(N_PLANE)])]
    ppermute x0 -> x4, starting transfers between devices: none -> 7.64 us  [swap(): return lax.ppermute(value, 'plane', [(p, p ^ bits) for p in range(N_PLANE)])]
    all_to_all x1, blocking collectives: 20.7 us -> 14.6 us  [body(): return (spectra, maps(exchange(adjoint_band), table))]
    pallas_call x3 -> x4, Pallas kernels: 8.41 us -> 9.61 us  [the longest x1 4.48 us: columns(): pl.pallas_call(columns_kernel, in_specs=[hbm] * 3, out_specs=VMEM, out_sh...]
  transfers between devices with their start and end apart: 1 -> 4, of which waited for: 1 -> 3; matrix products, arithmetic and copies ran while one was open for 0% -> 0% of each run, Pallas kernels for 0% -> 0%
where the time goes in v3:
time: 80.1 us; the launch traced here: 79.9 us
  blocking collectives  50.1 us (63%)
  Pallas kernels  11.8 us (15%)
  waiting for transfers between devices  9.64 us (12%)
  starting transfers between devices  7.64 us (10%)
    all_to_all x1, blocking collectives, body(): band = exchange(columns(slab_cells, slab_weight, table))  21.6 us
    all_to_all x1, blocking collectives, body(): return (spectra, maps(exchange(adjoint_band), table))  14.6 us
    all_to_all x1, blocking collectives, body(): exchange(sums)  13.9 us
    ppermute x4, waiting for transfers between devices, swap(): return lax.ppermute(value, 'plane', [(p, p ^ bits) for p in range(N_PLANE)])  9.64 us
    ppermute x4, starting transfers between devices, swap(): return lax.ppermute(value, 'plane', [(p, p ^ bits) for p in range(N_PLANE)])  7.64 us
    pallas_call x1, Pallas kernels, columns(): pl.pallas_call(columns_kernel, in_specs=[hbm] * 3, out_specs=VMEM, out_sh...  4.48 us
    pallas_call x1, Pallas kernels, modes(): pl.pallas_call(modes_kernel, in_specs=[SMEM, SMEM, SMEM] + [VMEM] * 5, ou...  2.76 us
    pallas_call x1, Pallas kernels, maps(): pl.pallas_call(maps_kernel, in_specs=[VMEM, VMEM], out_specs=VMEM, out_sh...  2.17 us
  transfers between devices with their start and end apart: 4, of which 3 were waited for; matrix products, arithmetic and copies ran while one was open for 0% of the time, Pallas kernels for 0%

profile of v3, /device:TPU:1, one launch (start us, length us, event | category | flops | bytes accessed | tf_op | source)
XLA Modules:
  0.0 79.9 jit_solution(10357959550956853444)
XLA Ops:
  0.6 0.0 copy-start
  0.6 0.0 copy-start.2
  0.7 4.5 %columns.1 = bf16[1024,128]{1,0:T(8,128)(2,1)} custom-call(f32[1,4]{1,0:T(1,128)} %weight_ref.1, bf16[1,4,128,4096]{3,2,1,0:T(8,128)(2,1)} %slab_ref.1, bf16[1024,512]{1,0:T(8,128)(2,1)} %constant.10.clone.table_ref), custom_call_target="tpu_custom_call" | custom-call | tf_op jit(solution)/shard_map/columns/pallas_call | solution.py:194
  5.1 0.0 copy-start.1
  5.2 0.0 copy-start.4
  5.2 0.0 copy-start.5
  5.2 21.6 %all_to_all.33 = bf16[32,32,128]{2,1,0:T(8,128)(2,1)S(1)} all-to-all(bf16[32,32,128]{2,1,0:T(8,128)(2,1)} %bitcast.17), channel_id=1, replica_groups=mesh['plane'=8,'tile'=32] {'tile'}, dimensions={0} | all-to-all | bytes 524288 | tf_op jit(solution)/shard_map/all_to_all | solution.py:529
  26.8 0.0 copy-done
  26.8 0.0 copy-done.2
  26.8 0.6 rows.1
  27.4 4.3 %collective-permute-start = (bf16[32,1152]{1,0:T(8,128)(2,1)S(1)}, bf16[32,1152]{1,0:T(8,128)(2,1)S(1)}, u32[]{:S(2)}, u32[]{:S(2)}) collective-permute-start(bf16[32,1152]{1,0:T(8,128)(2,1)S(1)} %rows.1), channel_id=1, source_target_pairs={{0,32},{32,0},{64,96},{96,64},{128,160},{160,128},{192,224},{224,1... | collective-permute-start | bytes 221192 | tf_op jit(solution)/shard_map/ppermute | solution.py:526
  31.7 3.5 %collective-permute-done = bf16[32,1152]{1,0:T(8,128)(2,1)S(1)} collective-permute-done((bf16[32,1152]{1,0:T(8,128)(2,1)S(1)}, bf16[32,1152]{1,0:T(8,128)(2,1)S(1)}, u32[]{:S(2)}, u32[]{:S(2)}) %collective-permute-start) | collective-permute-done | bytes 73760 | tf_op jit(solution)/shard_map/ppermute | solution.py:526
  35.2 2.6 %collective-permute-start.3 = (bf16[2,32,1152]{2,1,0:T(8,128)(2,1)S(1)}, bf16[2,32,1152]{2,1,0:T(8,128)(2,1)S(1)}, u32[]{:S(2)}, u32[]{:S(2)}) collective-permute-start(bf16[2,32,1152]{2,1,0:T(8,128)(2,1)S(1)} %pad_maximum_fusion.near_ref), channel_id=1, source_target_pairs={{0,192},{32,224},{64,128},{96,160},{128,64},{160,96},{192,0},{224,... | collective-permute-start | bytes 442376 | tf_op jit(solution)/shard_map/ppermute | solution.py:526
  37.8 0.5 collective-permute-start.2
  38.3 0.3 collective-permute-start.1
  38.6 5.3 %collective-permute-done.3.far3_ref = bf16[2,32,1152]{2,1,0:T(8,128)(2,1)S(1)} collective-permute-done((bf16[2,32,1152]{2,1,0:T(8,128)(2,1)S(1)}, bf16[2,32,1152]{2,1,0:T(8,128)(2,1)S(1)}, u32[]{:S(2)}, u32[]{:S(2)}) %collective-permute-start.3) | collective-permute-done | bytes 147488 | tf_op jit(solution)/shard_map/ppermute | solution.py:526
  43.8 0.0 collective-permute-done.2.far2_ref
  43.8 0.8 %collective-permute-done.1.far1_ref = bf16[2,32,1152]{2,1,0:T(8,128)(2,1)} collective-permute-done((bf16[2,32,1152]{2,1,0:T(8,128)(2,1)S(1)}, bf16[2,32,1152]{2,1,0:T(8,128)(2,1)}, u32[]{:S(2)}, u32[]{:S(2)}) %collective-permute-start.1) | collective-permute-done | bytes 147488 | tf_op jit(solution)/shard_map/ppermute | solution.py:526
  44.7 0.0 copy-done.1
  44.7 2.8 %modes.1 = (f32[128,1024]{1,0:T(8,128)S(1)}, f32[64,128]{1,0:T(8,128)S(1)}, s32[16,1024]{1,0:T(8,128)S(1)}) custom-call(s32[1]{0:T(128)} %bitcast.plane_ref, s32[4,8]{1,0:T(4,128)S(1)} %copy-done.4, f32[32]{0:T(128)S(1)} %copy-done.5, bf16[2,32,1152]{2,1,0:T(8,128)(2,1)S(1)} %pad_maximum_fusion.near_ref, ...), custom_call_target="tpu_custom_call" | custom-call | tf_op jit(solution)/shard_map/modes/pallas_call | solution.py:332
  47.4 13.9 %all_to_all.34 = f32[32,2,128]{2,1,0:T(2,128)S(1)} all-to-all(f32[32,2,128]{2,1,0:T(2,128)S(1)} %bitcast.15), channel_id=1, replica_groups=mesh['plane'=8,'tile'=32] {'tile'}, dimensions={0} | all-to-all | bytes 65536 | tf_op jit(solution)/shard_map/all_to_all | solution.py:535
  61.4 1.8 %adjoint.1 = (f32[10,16]{1,0:T(8,128)}, bf16[1024,128]{1,0:T(8,128)(2,1)S(1)}) custom-call(s32[1]{0:T(128)} %bitcast.plane_ref, s32[4,8]{1,0:T(4,128)S(1)} %copy-done.4, f32[32]{0:T(128)S(1)} %copy-done.5, f32[64,128]{1,0:T(8,128)S(1)} %bitcast.14, f32[128,1024]{1,0:T(8,128)S(1)} %get-tuple-element.8.kappa_ref, s32[16,1024]{1,0:T(8,128)S(1)} %get-tuple-element.9.ell_ref, ...), custom_call_target="tpu_custom_call" | custom-call | tf_op jit(solution)/shard_map/adjoint/pallas_call | solution.py:450
  63.2 14.6 %all_to_all.35 = bf16[32,32,128]{2,1,0:T(8,128)(2,1)S(1)} all-to-all(bf16[32,32,128]{2,1,0:T(8,128)(2,1)S(1)} %bitcast.13), channel_id=1, replica_groups=mesh['plane'=8,'tile'=32] {'tile'}, dimensions={0} | all-to-all | bytes 524288 | tf_op jit(solution)/shard_map/all_to_all | solution.py:537
  77.7 2.2 %maps.1 = f32[1,128,4096]{2,1,0:T(8,128)} custom-call(bf16[1024,128]{1,0:T(8,128)(2,1)S(1)} %bitcast.11, bf16[1024,512]{1,0:T(8,128)(2,1)S(1)} %copy-done), custom_call_target="tpu_custom_call" | custom-call | tf_op jit(solution)/shard_map/maps/pallas_call | solution.py:507
  (5 shorter events, 0.0 us)
Async XLA Ops:
  0.6 26.2 %copy-start = (bf16[1024,512]{1,0:T(8,128)(2,1)S(1)}, bf16[1024,512]{1,0:T(8,128)(2,1)}, u32[]{:S(2)}) copy-start(bf16[1024,512]{1,0:T(8,128)(2,1)} %constant.10.clone.table_ref) | copy-start | bytes 3145732
  0.6 26.2 %copy-start.2 = (s32[128,16]{0,1:T(8,128)S(1)}, s32[128,16]{0,1:T(8,128)}, u32[]{:S(2)}) copy-start(s32[128,16]{0,1:T(8,128)} %param.12) | copy-start | bytes 24580
  5.1 39.5 %copy-start.1 = (bf16[1024,1024]{1,0:T(8,128)(2,1)S(1)}, bf16[1024,1024]{1,0:T(8,128)(2,1)}, u32[]{:S(2)}) copy-start(bf16[1024,1024]{1,0:T(8,128)(2,1)} %constant.11.clone.order_ref) | copy-start | bytes 6291460
  5.2 39.5 %copy-start.4 = (s32[4,8]{1,0:T(4,128)S(1)}, s32[4,8]{1,0:T(4,128)}, u32[]{:S(2)}) copy-start(s32[4,8]{1,0:T(4,128)} %index_ref.3) | copy-start | bytes 388
  5.2 39.5 %copy-start.5 = (f32[32]{0:T(128)S(1)}, f32[32]{0:T(128)}, u32[]{:S(2)}) copy-start(f32[32]{0:T(128)} %values_ref.3) | copy-start | bytes 388
  26.8 34.6 %copy-start.3 = (f32[10,16]{1,0:T(8,128)S(1)}, f32[10,16]{1,0:T(8,128)}, u32[]{:S(2)}) copy-start(f32[10,16]{1,0:T(8,128)} %target_ref.1) | copy-start | bytes 1924
  27.4 7.8 %collective-permute-start = (bf16[32,1152]{1,0:T(8,128)(2,1)S(1)}, bf16[32,1152]{1,0:T(8,128)(2,1)S(1)}, u32[]{:S(2)}, u32[]{:S(2)}) collective-permute-start(bf16[32,1152]{1,0:T(8,128)(2,1)S(1)} %rows.1), channel_id=1, source_target_pairs={{0,32},{32,0},{64,96},{96,64},{128,160},{160,128},{192,224},{224,1... | collective-permute-start | bytes 221192 | tf_op jit(solution)/shard_map/ppermute | solution.py:526
  35.2 8.6 %collective-permute-start.3 = (bf16[2,32,1152]{2,1,0:T(8,128)(2,1)S(1)}, bf16[2,32,1152]{2,1,0:T(8,128)(2,1)S(1)}, u32[]{:S(2)}, u32[]{:S(2)}) collective-permute-start(bf16[2,32,1152]{2,1,0:T(8,128)(2,1)S(1)} %pad_maximum_fusion.near_ref), channel_id=1, source_target_pairs={{0,192},{32,224},{64,128},{96,160},{128,64},{160,96},{192,0},{224,... | collective-permute-start | bytes 442376 | tf_op jit(solution)/shard_map/ppermute | solution.py:526
  37.8 6.0 %collective-permute-start.2 = (bf16[2,32,1152]{2,1,0:T(8,128)(2,1)S(1)}, bf16[2,32,1152]{2,1,0:T(8,128)(2,1)}, u32[]{:S(2)}, u32[]{:S(2)}) collective-permute-start(bf16[2,32,1152]{2,1,0:T(8,128)(2,1)S(1)} %pad_maximum_fusion.near_ref), channel_id=1, source_target_pairs={{0,128},{32,160},{64,192},{96,224},{128,0},{160,32},{192,64},{224,... | collective-permute-start | bytes 442376 | tf_op jit(solution)/shard_map/ppermute | solution.py:526
  38.3 6.4 %collective-permute-start.1 = (bf16[2,32,1152]{2,1,0:T(8,128)(2,1)S(1)}, bf16[2,32,1152]{2,1,0:T(8,128)(2,1)}, u32[]{:S(2)}, u32[]{:S(2)}) collective-permute-start(bf16[2,32,1152]{2,1,0:T(8,128)(2,1)S(1)} %pad_maximum_fusion.near_ref), channel_id=1, source_target_pairs={{0,64},{32,96},{64,0},{96,32},{128,192},{160,224},{192,128},{224,1... | collective-permute-start | bytes 442376 | tf_op jit(solution)/shard_map/ppermute | solution.py:526

commit v4 on v3

--- a/solution.py
+++ b/solution.py
@@ -280,13 +280,12 @@
 
 
 def modes_kernel(
-    plane_ref, index_ref, values_ref, near_ref, far1_ref, far2_ref, far3_ref, order_ref,
-    kappa_ref, sums_ref, ell_ref, lines_ref, terms_ref,
+    plane_ref, index_ref, values_ref, *refs,
 ):
+    order_ref, kappa_ref, sums_ref, ell_ref, lines_ref, terms_ref = refs[N_PLANE:]
     plane = plane_ref[0]
-    for number, ref in enumerate((near_ref, far1_ref, far2_ref, far3_ref)):
-        for slot in range(2):
-            lines_ref[plane ^ (2 * number + slot)] = ref[slot]
+    for ref, bits in zip(refs, (0, 1, 2, 4, 6, 3, 5, 7)):
+        lines_ref[plane ^ bits] = ref[...]
     bins = jnp.concatenate([lines_ref[p, 0:16, 2 * KMAX :] for p in range(N_PLANE)], axis=1)
     ell_ref[...] = dot_nn(bins, order_ref[...]).astype(jnp.int32)
     weights = [[kernel_value(index_ref, values_ref, b, p) for p in range(N_PLANE)] for b in range(BINS)]
@@ -328,10 +327,10 @@
     sums_ref[...] = jnp.broadcast_to(pattern[None], (N_TILE // 4, 8, LANES)).reshape(2 * N_TILE, LANES)
 
 
-def modes(plane, index, values, near, far, order):
+def modes(plane, index, values, group, order):
     return pl.pallas_call(
         modes_kernel,
-        in_specs=[SMEM, SMEM, SMEM] + [VMEM] * 5,
+        in_specs=[SMEM, SMEM, SMEM] + [VMEM] * 9,
         out_specs=[VMEM, VMEM, VMEM],
         out_shape=[
             jax.ShapeDtypeStruct((32 * BINS, 2 * KMAX), F32),
@@ -344,7 +343,7 @@
         ],
         compiler_params=pltpu.CompilerParams(vmem_limit_bytes=LIMIT),
         name="modes",
-    )(plane, index, values, near, *far, order)
+    )(plane, index, values, *group, order)
 
 
 def adjoint_kernel(
@@ -528,9 +527,11 @@
     plane = lax.axis_index("plane").astype(jnp.int32).reshape(1)
     band = exchange(columns(slab_cells, slab_weight, table))
     lines = rows(band, table, ell_index.T)
-    near = jnp.stack([lines, swap(lines, 1)])
-    far = [swap(near, bits) for bits in (2, 4, 6)]
-    kappa, sums, ell = modes(plane, kernel_index, kernel_table, near, far, order)
+    across = swap(lines, 1)
+    group = [lines, across]
+    for part in (lines, across):
+        group += [swap(part, bits) for bits in (2, 4, 6)]
+    kappa, sums, ell = modes(plane, kernel_index, kernel_table, group, order)
     spectra, adjoint_band = adjoint(
         plane, kernel_index, kernel_table, exchange(sums), kappa, ell, target_spectra, table
     )

time: 80.1 us -> 77.8 us (0.971)
  waiting for transfers between devices: 9.64 us -> 4.32 us
  starting transfers between devices: 7.64 us -> 10.8 us
    ppermute x4 -> x7, waiting for transfers between devices: 9.64 us -> 4.32 us  [swap(): return lax.ppermute(value, 'plane', [(p, p ^ bits) for p in range(N_PLANE)])]
    ppermute x4 -> x7, starting transfers between devices: 7.64 us -> 10.8 us  [swap(): return lax.ppermute(value, 'plane', [(p, p ^ bits) for p in range(N_PLANE)])]
  transfers between devices with their start and end apart: 4 -> 7, of which waited for: 3 -> 4; matrix products, arithmetic and copies ran while one was open for 0% -> 0% of each run, Pallas kernels for 0% -> 0%
where the time goes in v4:
time: 77.8 us; the launch traced here: 77.5 us
  blocking collectives  49.8 us (64%)
  Pallas kernels  11.8 us (15%)
  starting transfers between devices  10.8 us (14%)
  waiting for transfers between devices  4.32 us (6%)
    all_to_all x1, blocking collectives, body(): band = exchange(columns(slab_cells, slab_weight, table))  21.5 us
    all_to_all x1, blocking collectives, body(): return (spectra, maps(exchange(adjoint_band), table))  14.6 us
    all_to_all x1, blocking collectives, body(): exchange(sums)  13.8 us
    ppermute x7, starting transfers between devices, swap(): return lax.ppermute(value, 'plane', [(p, p ^ bits) for p in range(N_PLANE)])  10.8 us
    pallas_call x1, Pallas kernels, columns(): pl.pallas_call(columns_kernel, in_specs=[hbm] * 3, out_specs=VMEM, out_sh...  4.55 us
    ppermute x7, waiting for transfers between devices, swap(): return lax.ppermute(value, 'plane', [(p, p ^ bits) for p in range(N_PLANE)])  4.32 us
    pallas_call x1, Pallas kernels, modes(): pl.pallas_call(modes_kernel, in_specs=[SMEM, SMEM, SMEM] + [VMEM] * 9, ou...  2.75 us
    pallas_call x1, Pallas kernels, maps(): pl.pallas_call(maps_kernel, in_specs=[VMEM, VMEM], out_specs=VMEM, out_sh...  2.17 us
  transfers between devices with their start and end apart: 7, of which 4 were waited for; matrix products, arithmetic and copies ran while one was open for 0% of the time, Pallas kernels for 0%

profile of v4, /device:TPU:1, one launch (start us, length us, event | category | flops | bytes accessed | tf_op | source)
XLA Modules:
  0.0 77.5 jit_solution(14483278787619352024)
XLA Ops:
  0.6 0.0 copy-start
  0.7 0.0 copy-start.1
  0.7 4.5 %columns.1 = bf16[1024,128]{1,0:T(8,128)(2,1)} custom-call(f32[1,4]{1,0:T(1,128)} %weight_ref.1, bf16[1,4,128,4096]{3,2,1,0:T(8,128)(2,1)} %slab_ref.1, bf16[1024,512]{1,0:T(8,128)(2,1)} %constant.10.clone.table_ref), custom_call_target="tpu_custom_call" | custom-call | tf_op jit(solution)/shard_map/columns/pallas_call | solution.py:194
  5.2 21.5 %all_to_all.33 = bf16[32,32,128]{2,1,0:T(8,128)(2,1)S(1)} all-to-all(bf16[32,32,128]{2,1,0:T(8,128)(2,1)} %bitcast.14), channel_id=1, replica_groups=mesh['plane'=8,'tile'=32] {'tile'}, dimensions={0} | all-to-all | bytes 524288 | tf_op jit(solution)/shard_map/all_to_all | solution.py:528
  26.7 0.6 rows.1.refs_0_
  27.3 4.3 %collective-permute-start = (bf16[32,1152]{1,0:T(8,128)(2,1)S(1)}, bf16[32,1152]{1,0:T(8,128)(2,1)S(1)}, u32[]{:S(2)}, u32[]{:S(2)}) collective-permute-start(bf16[32,1152]{1,0:T(8,128)(2,1)S(1)} %rows.1.refs_0_), channel_id=1, source_target_pairs={{0,32},{32,0},{64,96},{96,64},{128,160},{160,128},{192,224},{224,1... | collective-permute-start | bytes 221192 | tf_op jit(solution)/shard_map/ppermute | solution.py:525
  31.6 2.5 %collective-permute-start.3 = (bf16[32,1152]{1,0:T(8,128)(2,1)S(1)}, bf16[32,1152]{1,0:T(8,128)(2,1)S(1)}, u32[]{:S(2)}, u32[]{:S(2)}) collective-permute-start(bf16[32,1152]{1,0:T(8,128)(2,1)S(1)} %rows.1.refs_0_), channel_id=1, source_target_pairs={{0,192},{32,224},{64,128},{96,160},{128,64},{160,96},{192,0},{224,... | collective-permute-start | bytes 221192 | tf_op jit(solution)/shard_map/ppermute | solution.py:525
  34.1 0.5 collective-permute-start.2
  34.6 0.3 collective-permute-start.1
  34.8 0.3 collective-permute-done.refs_1_
  35.1 2.5 %collective-permute-start.6 = (bf16[32,1152]{1,0:T(8,128)(2,1)S(1)}, bf16[32,1152]{1,0:T(8,128)(2,1)}, u32[]{:S(2)}, u32[]{:S(2)}) collective-permute-start(bf16[32,1152]{1,0:T(8,128)(2,1)S(1)} %collective-permute-done.refs_1_), channel_id=1, source_target_pairs={{0,192},{32,224},{64,128},{96,160},{128,64},{160,96},{192,0},{224,... | collective-permute-start | bytes 221192 | tf_op jit(solution)/shard_map/ppermute | solution.py:525
  37.6 0.5 collective-permute-start.5
  38.1 0.0 collective-permute-done.3.refs_4_
  38.1 0.2 collective-permute-start.4
  38.4 0.4 collective-permute-done.2.refs_3_
  38.8 0.0 collective-permute-done.1.refs_2_
  38.8 1.5 %collective-permute-done.6.refs_7_ = bf16[32,1152]{1,0:T(8,128)(2,1)} collective-permute-done((bf16[32,1152]{1,0:T(8,128)(2,1)S(1)}, bf16[32,1152]{1,0:T(8,128)(2,1)}, u32[]{:S(2)}, u32[]{:S(2)}) %collective-permute-start.6) | collective-permute-done | bytes 73760 | tf_op jit(solution)/shard_map/ppermute | solution.py:525
  40.3 2.1 %collective-permute-done.5.refs_6_ = bf16[32,1152]{1,0:T(8,128)(2,1)} collective-permute-done((bf16[32,1152]{1,0:T(8,128)(2,1)S(1)}, bf16[32,1152]{1,0:T(8,128)(2,1)}, u32[]{:S(2)}, u32[]{:S(2)}) %collective-permute-start.5) | collective-permute-done | bytes 73760 | tf_op jit(solution)/shard_map/ppermute | solution.py:525
  42.4 0.0 collective-permute-done.4.refs_5_
  42.4 2.7 %modes.1 = (f32[128,1024]{1,0:T(8,128)S(1)}, f32[64,128]{1,0:T(8,128)S(1)}, s32[16,1024]{1,0:T(8,128)S(1)}) custom-call(s32[1]{0:T(128)} %bitcast.plane_ref, s32[4,8]{1,0:T(4,128)S(1)} %copy-done.4, f32[32]{0:T(128)S(1)} %copy-done.5, bf16[32,1152]{1,0:T(8,128)(2,1)S(1)} %rows.1.refs_0_, bf16[32,1152]{1,0:T(8,128)(2,1)S(1)} %collective-permute-done.refs_1_, ...), custom_call_target="tpu_custom_call" | custom-call | tf_op jit(solution)/shard_map/modes/pallas_call | solution.py:331
  45.2 13.8 %all_to_all.34 = f32[32,2,128]{2,1,0:T(2,128)S(1)} all-to-all(f32[32,2,128]{2,1,0:T(2,128)S(1)} %bitcast.12), channel_id=1, replica_groups=mesh['plane'=8,'tile'=32] {'tile'}, dimensions={0} | all-to-all | bytes 65536 | tf_op jit(solution)/shard_map/all_to_all | solution.py:536
  59.0 1.8 %adjoint.1 = (f32[10,16]{1,0:T(8,128)}, bf16[1024,128]{1,0:T(8,128)(2,1)S(1)}) custom-call(s32[1]{0:T(128)} %bitcast.plane_ref, s32[4,8]{1,0:T(4,128)S(1)} %copy-done.4, f32[32]{0:T(128)S(1)} %copy-done.5, f32[64,128]{1,0:T(8,128)S(1)} %bitcast.11, f32[128,1024]{1,0:T(8,128)S(1)} %get-tuple-element.8.kappa_ref, s32[16,1024]{1,0:T(8,128)S(1)} %get-tuple-element.9.ell_ref, ...), custom_call_target="tpu_custom_call" | custom-call | tf_op jit(solution)/shard_map/adjoint/pallas_call | solution.py:449
  60.8 14.6 %all_to_all.35 = bf16[32,32,128]{2,1,0:T(8,128)(2,1)S(1)} all-to-all(bf16[32,32,128]{2,1,0:T(8,128)(2,1)S(1)} %bitcast.10), channel_id=1, replica_groups=mesh['plane'=8,'tile'=32] {'tile'}, dimensions={0} | all-to-all | bytes 524288 | tf_op jit(solution)/shard_map/all_to_all | solution.py:538
  75.3 2.2 %maps.1 = f32[1,128,4096]{2,1,0:T(8,128)} custom-call(bf16[1024,128]{1,0:T(8,128)(2,1)S(1)} %bitcast.9, bf16[1024,512]{1,0:T(8,128)(2,1)S(1)} %copy-done), custom_call_target="tpu_custom_call" | custom-call | tf_op jit(solution)/shard_map/maps/pallas_call | solution.py:506
  (10 shorter events, 0.0 us)
Async XLA Ops:
  0.6 26.1 %copy-start = (bf16[1024,512]{1,0:T(8,128)(2,1)S(1)}, bf16[1024,512]{1,0:T(8,128)(2,1)}, u32[]{:S(2)}) copy-start(bf16[1024,512]{1,0:T(8,128)(2,1)} %constant.10.clone.table_ref) | copy-start | bytes 3145732
  0.6 26.1 %copy-start.2 = (s32[128,16]{0,1:T(8,128)S(1)}, s32[128,16]{0,1:T(8,128)}, u32[]{:S(2)}) copy-start(s32[128,16]{0,1:T(8,128)} %param.12) | copy-start | bytes 24580
  0.7 41.8 %copy-start.4 = (s32[4,8]{1,0:T(4,128)S(1)}, s32[4,8]{1,0:T(4,128)}, u32[]{:S(2)}) copy-start(s32[4,8]{1,0:T(4,128)} %index_ref.3) | copy-start | bytes 388
  0.7 41.8 %copy-start.5 = (f32[32]{0:T(128)S(1)}, f32[32]{0:T(128)}, u32[]{:S(2)}) copy-start(f32[32]{0:T(128)} %values_ref.3) | copy-start | bytes 388
  0.7 41.8 %copy-start.1 = (bf16[1024,1024]{1,0:T(8,128)(2,1)S(1)}, bf16[1024,1024]{1,0:T(8,128)(2,1)}, u32[]{:S(2)}) copy-start(bf16[1024,1024]{1,0:T(8,128)(2,1)} %constant.11.clone.refs_8_) | copy-start | bytes 6291460
  26.7 32.3 %copy-start.3 = (f32[10,16]{1,0:T(8,128)S(1)}, f32[10,16]{1,0:T(8,128)}, u32[]{:S(2)}) copy-start(f32[10,16]{1,0:T(8,128)} %target_ref.1) | copy-start | bytes 1924
  27.3 7.8 %collective-permute-start = (bf16[32,1152]{1,0:T(8,128)(2,1)S(1)}, bf16[32,1152]{1,0:T(8,128)(2,1)S(1)}, u32[]{:S(2)}, u32[]{:S(2)}) collective-permute-start(bf16[32,1152]{1,0:T(8,128)(2,1)S(1)} %rows.1.refs_0_), channel_id=1, source_target_pairs={{0,32},{32,0},{64,96},{96,64},{128,160},{160,128},{192,224},{224,1... | collective-permute-start | bytes 221192 | tf_op jit(solution)/shard_map/ppermute | solution.py:525
  31.6 6.5 %collective-permute-start.3 = (bf16[32,1152]{1,0:T(8,128)(2,1)S(1)}, bf16[32,1152]{1,0:T(8,128)(2,1)S(1)}, u32[]{:S(2)}, u32[]{:S(2)}) collective-permute-start(bf16[32,1152]{1,0:T(8,128)(2,1)S(1)} %rows.1.refs_0_), channel_id=1, source_target_pairs={{0,192},{32,224},{64,128},{96,160},{128,64},{160,96},{192,0},{224,... | collective-permute-start | bytes 221192 | tf_op jit(solution)/shard_map/ppermute | solution.py:525
  34.1 4.7 %collective-permute-start.2 = (bf16[32,1152]{1,0:T(8,128)(2,1)S(1)}, bf16[32,1152]{1,0:T(8,128)(2,1)S(1)}, u32[]{:S(2)}, u32[]{:S(2)}) collective-permute-start(bf16[32,1152]{1,0:T(8,128)(2,1)S(1)} %rows.1.refs_0_), channel_id=1, source_target_pairs={{0,128},{32,160},{64,192},{96,224},{128,0},{160,32},{192,64},{224,... | collective-permute-start | bytes 221192 | tf_op jit(solution)/shard_map/ppermute | solution.py:525
  34.6 4.2 %collective-permute-start.1 = (bf16[32,1152]{1,0:T(8,128)(2,1)S(1)}, bf16[32,1152]{1,0:T(8,128)(2,1)S(1)}, u32[]{:S(2)}, u32[]{:S(2)}) collective-permute-start(bf16[32,1152]{1,0:T(8,128)(2,1)S(1)} %rows.1.refs_0_), channel_id=1, source_target_pairs={{0,64},{32,96},{64,0},{96,32},{128,192},{160,224},{192,128},{224,1... | collective-permute-start | bytes 221192 | tf_op jit(solution)/shard_map/ppermute | solution.py:525
  35.1 5.2 %collective-permute-start.6 = (bf16[32,1152]{1,0:T(8,128)(2,1)S(1)}, bf16[32,1152]{1,0:T(8,128)(2,1)}, u32[]{:S(2)}, u32[]{:S(2)}) collective-permute-start(bf16[32,1152]{1,0:T(8,128)(2,1)S(1)} %collective-permute-done.refs_1_), channel_id=1, source_target_pairs={{0,192},{32,224},{64,128},{96,160},{128,64},{160,96},{192,0},{224,... | collective-permute-start | bytes 221192 | tf_op jit(solution)/shard_map/ppermute | solution.py:525
  37.6 4.8 %collective-permute-start.5 = (bf16[32,1152]{1,0:T(8,128)(2,1)S(1)}, bf16[32,1152]{1,0:T(8,128)(2,1)}, u32[]{:S(2)}, u32[]{:S(2)}) collective-permute-start(bf16[32,1152]{1,0:T(8,128)(2,1)S(1)} %collective-permute-done.refs_1_), channel_id=1, source_target_pairs={{0,128},{32,160},{64,192},{96,224},{128,0},{160,32},{192,64},{224,... | collective-permute-start | bytes 221192 | tf_op jit(solution)/shard_map/ppermute | solution.py:525
  38.1 4.3 %collective-permute-start.4 = (bf16[32,1152]{1,0:T(8,128)(2,1)S(1)}, bf16[32,1152]{1,0:T(8,128)(2,1)}, u32[]{:S(2)}, u32[]{:S(2)}) collective-permute-start(bf16[32,1152]{1,0:T(8,128)(2,1)S(1)} %collective-permute-done.refs_1_), channel_id=1, source_target_pairs={{0,64},{32,96},{64,0},{96,32},{128,192},{160,224},{192,128},{224,1... | collective-permute-start | bytes 221192 | tf_op jit(solution)/shard_map/ppermute | solution.py:525

commit v5 on v4

--- a/solution.py
+++ b/solution.py
@@ -55,14 +55,14 @@
 
 
 def order_matrix():
-    out = np.zeros((2 * KMAX, 2 * KMAX), np.float32)
+    out = np.zeros((2 * KMAX, KMAX), np.float32)
     for place, rho in enumerate(ORDER):
-        for sign in range(2):
-            for kk in range(2):
-                for t in range(N_TILE):
-                    j = 16 * t + 8 * kk + rho
-                    q = KMAX + j if sign == 0 else (KMAX - j if j else 0)
-                    out[q, place * LANES + sign * 64 + kk * N_TILE + t] = 1.0
+        for kk in range(2):
+            for t in range(N_TILE):
+                j = 16 * t + 8 * kk + rho
+                n = place * 64 + kk * N_TILE + t
+                out[KMAX + j, n] = 1.0
+                out[KMAX - j if j else 0, n] = 1.0
     return out.astype(ml_dtypes.bfloat16)
 
 
@@ -211,10 +211,6 @@
     )(weight, slab, table)
 
 
-def kernel_value(index_ref, values_ref, b, p):
-    return values_ref[index_ref[b, p]]
-
-
 def rows_kernel(band_ref, table_ref, ell_ref, out_ref, fold_ref):
     cos, sin = edge_waves()
     edge_re = jnp.zeros((16, 1), F32)
@@ -280,15 +276,34 @@
 
 
 def modes_kernel(
-    plane_ref, index_ref, values_ref, *refs,
+    index_ref, values_ref, *refs,
 ):
-    order_ref, kappa_ref, sums_ref, ell_ref, lines_ref, terms_ref = refs[N_PLANE:]
-    plane = plane_ref[0]
-    for ref, bits in zip(refs, (0, 1, 2, 4, 6, 3, 5, 7)):
+    (
+        order_ref, kappa_ref, sums_ref, ell_ref, own_ref,
+        lines_ref, terms_ref, picks_ref, entry_ref, value_ref,
+    ) = refs[N_PLANE:]
+    plane = lax.axis_index("plane")
+    entry_ref[...] = jnp.zeros_like(entry_ref)
+    entry_ref[0:BINS, 0:N_PLANE] = index_ref[...]
+    value_ref[...] = jnp.zeros_like(value_ref)
+    value_ref[:, 0 : values_ref.shape[1]] = jnp.broadcast_to(values_ref[...], (8, values_ref.shape[1]))
+    kernel = jnp.take_along_axis(value_ref[...], entry_ref[...], axis=1)
+    mine = jnp.where(lax.broadcasted_iota(jnp.int32, (8, LANES), 1) == plane, kernel, 0.0)
+    own_ref[...] = jnp.broadcast_to(jnp.sum(mine, axis=1, keepdims=True), (8, LANES))
+    for ref, bits in zip(refs, (0, 1, 2, 6, 4, 3, 7, 5)):
         lines_ref[plane ^ bits] = ref[...]
     bins = jnp.concatenate([lines_ref[p, 0:16, 2 * KMAX :] for p in range(N_PLANE)], axis=1)
-    ell_ref[...] = dot_nn(bins, order_ref[...]).astype(jnp.int32)
-    weights = [[kernel_value(index_ref, values_ref, b, p) for p in range(N_PLANE)] for b in range(BINS)]
+    minus = dot_nn(bins[:, :KMAX], order_ref[:KMAX]).astype(jnp.int32)
+    plus = dot_nn(bins[:, KMAX:], order_ref[KMAX:]).astype(jnp.int32)
+    low = lax.broadcasted_iota(jnp.int32, (16, LANES), 1) < 64
+    for pair in range(RADIX // 2):
+        cols = slice(pair * LANES, (pair + 1) * LANES)
+        ahead, back = plus[:, cols], minus[:, cols]
+        ell_ref[:, 2 * pair * LANES : (2 * pair + 1) * LANES] = jnp.where(low, ahead, pltpu.roll(back, 64, 1))
+        ell_ref[:, (2 * pair + 1) * LANES : (2 * pair + 2) * LANES] = jnp.where(low, pltpu.roll(ahead, 64, 1), back)
+    weights = [
+        [jnp.broadcast_to(kernel[b : b + 1, p : p + 1], (1, LANES)) for p in range(N_PLANE)] for b in range(BINS)
+    ]
     for tile in range(RADIX):
         cols = slice(tile * LANES, (tile + 1) * LANES)
         kappa = [None] * BINS
@@ -301,53 +316,65 @@
             kappa_ref[32 * b : 32 * b + 32, cols] = kappa[b]
         for number, (i, j) in enumerate(FIRST_GROUP + SECOND_GROUP):
             both = kappa[i] * kappa[j]
-            terms_ref[number, :, cols] = both[0:16] + both[16:32]
-
+            term = both[0:16] + both[16:32]
+            high = term.astype(BF16)
+            terms_ref[16 * number : 16 * number + 16, cols] = high
+            terms_ref[16 * (PAIRS + number) : 16 * (PAIRS + number) + 16, cols] = (
+                term - high.astype(F32)
+            ).astype(BF16)
+
+    bin_row = lax.broadcasted_iota(jnp.int32, (16, 2 * KMAX), 0)
+    for column in range(16):
+        here = ell_ref[column : column + 1, :] == bin_row
+        picks_ref[16 * column : 16 * column + 16, :] = jnp.where(here, 1.0, 0.0).astype(BF16)
+    crossed = dot_nt(terms_ref[...], picks_ref[...])
+    same = (lax.broadcasted_iota(jnp.int32, (16, 2 * LANES), 1) >> 4) == lax.broadcasted_iota(
+        jnp.int32, (16, 2 * LANES), 0
+    )
     lane = lax.broadcasted_iota(jnp.int32, (8, LANES), 1)
     sub = lax.broadcasted_iota(jnp.int32, (8, LANES), 0)
     spread = [jnp.zeros((8, LANES), F32), jnp.zeros((8, LANES), F32)]
-    for ell in range(ELLS):
-        here = ell_ref[...] == ell
-        held = [jnp.zeros((8, LANES), F32), jnp.zeros((8, LANES), F32)]
-        for number in range(PAIRS):
-            chosen = jnp.where(here, terms_ref[number], 0.0)
-            chosen = chosen[0:8] + chosen[8:16]
-            total = chosen[:, 0:LANES]
-            for tile in range(1, RADIX):
-                total = total + chosen[:, tile * LANES : (tile + 1) * LANES]
-            total = jnp.sum(total, axis=0, keepdims=True)
-            group, row = divmod(number, 8)
-            held[group] = jnp.where(sub == row, total, held[group])
-        for group in range(2):
-            total = jnp.sum(held[group], axis=1, keepdims=True)
-            spread[group] = jnp.where(lane & 15 == ell, total, spread[group])
+    for number in range(PAIRS):
+        low = 16 * (PAIRS + number)
+        part = crossed[16 * number : 16 * number + 16] + crossed[low : low + 16]
+        part = jnp.where(same, part, 0.0)
+        part = part[0:8] + part[8:16]
+        total = jnp.sum(part[:, :LANES] + part[:, LANES:], axis=0, keepdims=True)
+        for shift in (64, 32, 16):
+            total = total + pltpu.roll(total, shift, 1)
+        group, row = divmod(number, 8)
+        spread[group] = jnp.where(sub == row, total, spread[group])
     own = (lane >> 4) == sub
     sums = [jnp.sum(jnp.where(own, part, 0.0), axis=0, keepdims=True) for part in spread]
     pattern = jnp.where(sub & 1 == 0, sums[0], sums[1])
     sums_ref[...] = jnp.broadcast_to(pattern[None], (N_TILE // 4, 8, LANES)).reshape(2 * N_TILE, LANES)
 
 
-def modes(plane, index, values, group, order):
+def modes(index, values, group, order):
     return pl.pallas_call(
         modes_kernel,
-        in_specs=[SMEM, SMEM, SMEM] + [VMEM] * 9,
-        out_specs=[VMEM, VMEM, VMEM],
+        in_specs=[VMEM] * 11,
+        out_specs=[VMEM] * 4,
         out_shape=[
             jax.ShapeDtypeStruct((32 * BINS, 2 * KMAX), F32),
             jax.ShapeDtypeStruct((2 * N_TILE, LANES), F32),
             jax.ShapeDtypeStruct((16, 2 * KMAX), jnp.int32),
+            jax.ShapeDtypeStruct((8, LANES), F32),
         ],
         scratch_shapes=[
             pltpu.VMEM((N_PLANE, 32, WIDTH), BF16),
-            pltpu.VMEM((PAIRS, 16, 2 * KMAX), F32),
+            pltpu.VMEM((2 * PAIRS * 16, 2 * KMAX), BF16),
+            pltpu.VMEM((16 * ELLS, 2 * KMAX), BF16),
+            pltpu.VMEM((8, LANES), jnp.int32),
+            pltpu.VMEM((8, LANES), F32),
         ],
         compiler_params=pltpu.CompilerParams(vmem_limit_bytes=LIMIT),
         name="modes",
-    )(plane, index, values, *group, order)
+    )(index, values, *group, order)
 
 
 def adjoint_kernel(
-    plane_ref, index_ref, values_ref, sums_ref, kappa_ref, ell_ref, target_ref, table_ref,
+    own_ref, sums_ref, kappa_ref, ell_ref, target_ref, table_ref,
     spectra_ref, out_ref, weight_ref, line_ref, spread_ref,
 ):
     total = jnp.sum(sums_ref[...].reshape(N_TILE // 4, 8, LANES), axis=0)
@@ -372,8 +399,7 @@
         row = weight_ref[number : number + 1, :]
         row = row + row if number in (PAIR_ID[(i, i)] for i in range(BINS)) else row
         couplings.append(jnp.broadcast_to(row, (8, LANES)))
-    plane = plane_ref[0]
-    weights = [kernel_value(index_ref, values_ref, b, plane) for b in range(BINS)]
+    weights = [own_ref[b : b + 1, :] for b in range(BINS)]
 
     for tile in range(RADIX):
         cols = slice(tile * LANES, (tile + 1) * LANES)
@@ -445,10 +471,10 @@
                 out_ref[begin : begin + 16, :] = both[s].astype(BF16)
 
 
-def adjoint(plane, index, values, sums, kappa, ell, target, table):
+def adjoint(own, sums, kappa, ell, target, table):
     return pl.pallas_call(
         adjoint_kernel,
-        in_specs=[SMEM, SMEM, SMEM, VMEM, VMEM, VMEM, VMEM, VMEM],
+        in_specs=[VMEM] * 6,
         out_specs=[VMEM, VMEM],
         out_shape=[
             jax.ShapeDtypeStruct(target.shape, F32),
@@ -461,10 +487,10 @@
         ],
         compiler_params=pltpu.CompilerParams(vmem_limit_bytes=LIMIT),
         name="adjoint",
-    )(plane, index, values, sums, kappa, ell, target, table)
-
-
-def maps_kernel(band_ref, table_ref, out_ref, wide_ref):
+    )(own, sums, kappa, ell, target, table)
+
+
+def maps_kernel(band_ref, table_ref, out_ref, wide_ref, spread_ref, done_ref, sems):
     wide_ref[...] = band_ref[...].astype(F32)
 
     def block(rho, s):
@@ -490,25 +516,45 @@
         got = dot_tn(left, table_of(table_ref, rho, back))
         p.append(got[:ROWS])
         q.append(got[ROWS:])
-    plus, minus = flat[0] + flat[1], flat[0] - flat[1]
-
-    def put(m, even, odd):
-        out_ref[0, :, m * SPAN : (m + 1) * SPAN] = even + odd
-        out_ref[0, :, (m + 4) * SPAN : (m + 5) * SPAN] = even - odd
-
-    put(0, plus + p[2], p[1] + p[3])
-    put(1, minus - q[2], HALF * (p[1] - q[1] - p[3] - q[3]))
-    put(2, plus - p[2], q[3] - q[1])
-    put(3, minus + q[2], HALF * (p[3] - p[1] - q[1] - q[3]))
+    for index, part in enumerate(flat + p[1:] + q[1:]):
+        spread_ref[index] = part
+
+    def send(chunk):
+        rows = pl.ds(chunk * CHUNK, CHUNK)
+        return pltpu.make_async_copy(done_ref.at[rows, :], out_ref.at[0, rows, :], sems.at[chunk])
+
+    for chunk in range(CHUNKS):
+        rows = slice(chunk * CHUNK, (chunk + 1) * CHUNK)
+        for start in range(0, SPAN, LANES):
+            cols = slice(start, start + LANES)
+            a0, a4, p1, p2, p3, q1, q2, q3 = (spread_ref[index, rows, cols] for index in range(RADIX))
+
+            def put(m, even, odd):
+                done_ref[rows, m * SPAN + start : m * SPAN + start + LANES] = even + odd
+                done_ref[rows, (m + 4) * SPAN + start : (m + 4) * SPAN + start + LANES] = even - odd
+
+            plus, minus = a0 + a4, a0 - a4
+            put(0, plus + p2, p1 + p3)
+            put(1, minus - q2, HALF * (p1 - q1 - p3 - q3))
+            put(2, plus - p2, q3 - q1)
+            put(3, minus + q2, HALF * (p3 - p1 - q1 - q3))
+        send(chunk).start()
+    for chunk in range(CHUNKS):
+        send(chunk).wait()
 
 
 def maps(band, table):
     return pl.pallas_call(
         maps_kernel,
         in_specs=[VMEM, VMEM],
-        out_specs=VMEM,
+        out_specs=pl.BlockSpec(memory_space=pltpu.HBM),
         out_shape=jax.ShapeDtypeStruct((1, ROWS, NPIX), F32),
-        scratch_shapes=[pltpu.VMEM((2 * KMAX, ROWS), F32)],
+        scratch_shapes=[
+            pltpu.VMEM((2 * KMAX, ROWS), F32),
+            pltpu.VMEM((RADIX, ROWS, SPAN), F32),
+            pltpu.VMEM((ROWS, NPIX), F32),
+            pltpu.SemaphoreType.DMA((CHUNKS,)),
+        ],
         compiler_params=pltpu.CompilerParams(vmem_limit_bytes=LIMIT),
         name="maps",
     )(band, table)
@@ -524,16 +570,15 @@
     def swap(value, bits):
         return lax.ppermute(value, "plane", [(p, p ^ bits) for p in range(N_PLANE)])
 
-    plane = lax.axis_index("plane").astype(jnp.int32).reshape(1)
     band = exchange(columns(slab_cells, slab_weight, table))
     lines = rows(band, table, ell_index.T)
     across = swap(lines, 1)
     group = [lines, across]
     for part in (lines, across):
-        group += [swap(part, bits) for bits in (2, 4, 6)]
-    kappa, sums, ell = modes(plane, kernel_index, kernel_table, group, order)
+        group += [swap(part, bits) for bits in (2, 6, 4)]
+    kappa, sums, ell, own = modes(kernel_index, kernel_table.reshape(1, -1), group, order)
     spectra, adjoint_band = adjoint(
-        plane, kernel_index, kernel_table, exchange(sums), kappa, ell, target_spectra, table
+        own, exchange(sums), kappa, ell, target_spectra, table
     )
     return spectra, maps(exchange(adjoint_band), table)
 

time: 77.8 us -> 75.6 us (0.972)
  Pallas kernels: 11.8 us -> 9.83 us
  starting transfers between devices: 10.8 us -> 11.8 us
  blocking collectives: 49.8 us -> 49 us
    pallas_call x3, Pallas kernels: 6.72 us -> 4.73 us  [the longest x1 2.12 us: maps(): pl.pallas_call(maps_kernel, in_specs=[VMEM, VMEM], out_specs=pl.BlockSpec...]
    ppermute x7, starting transfers between devices: 10.8 us -> 11.8 us  [swap(): return lax.ppermute(value, 'plane', [(p, p ^ bits) for p in range(N_PLANE)])]
    all_to_all x1, blocking collectives: 13.8 us -> 13 us  [body(): exchange(sums)]
  transfers between devices with their start and end apart: 7 -> 7, of which waited for: 4 -> 2; matrix products, arithmetic and copies ran while one was open for 0% -> 0% of each run, Pallas kernels for 0% -> 0%
where the time goes in v5:
time: 75.6 us; the launch traced here: 75.4 us
  blocking collectives  49 us (65%)
  starting transfers between devices  11.8 us (16%)
  Pallas kernels  9.83 us (13%)
  waiting for transfers between devices  4.03 us (5%)
    all_to_all x1, blocking collectives, body(): band = exchange(columns(slab_cells, slab_weight, table))  21.5 us
    all_to_all x1, blocking collectives, body(): return (spectra, maps(exchange(adjoint_band), table))  14.6 us
    all_to_all x1, blocking collectives, body(): exchange(sums)  13 us
    ppermute x7, starting transfers between devices, swap(): return lax.ppermute(value, 'plane', [(p, p ^ bits) for p in range(N_PLANE)])  11.8 us
    pallas_call x1, Pallas kernels, columns(): pl.pallas_call(columns_kernel, in_specs=[hbm] * 3, out_specs=VMEM, out_sh...  4.54 us
    ppermute x7, waiting for transfers between devices, swap(): return lax.ppermute(value, 'plane', [(p, p ^ bits) for p in range(N_PLANE)])  4.03 us
    pallas_call x1, Pallas kernels, maps(): pl.pallas_call(maps_kernel, in_specs=[VMEM, VMEM], out_specs=pl.BlockSpec...  2.12 us
  transfers between devices with their start and end apart: 7, of which 2 were waited for; matrix products, arithmetic and copies ran while one was open for 0% of the time, Pallas kernels for 0%

profile of v5, /device:TPU:1, one launch (start us, length us, event | category | flops | bytes accessed | tf_op | source)
XLA Modules:
  0.0 75.4 jit_solution(9233210358702241165)
XLA Ops:
  0.6 0.0 copy-start
  0.6 0.0 copy-start.1
  0.7 4.5 %columns.1 = bf16[1024,128]{1,0:T(8,128)(2,1)} custom-call(f32[1,4]{1,0:T(1,128)} %weight_ref.1, bf16[1,4,128,4096]{3,2,1,0:T(8,128)(2,1)} %slab_ref.1, bf16[1024,512]{1,0:T(8,128)(2,1)} %constant.4.clone.table_ref), custom_call_target="tpu_custom_call" | custom-call | tf_op jit(solution)/shard_map/columns/pallas_call | solution.py:194
  5.2 21.5 %all_to_all.33 = bf16[32,32,128]{2,1,0:T(8,128)(2,1)S(1)} all-to-all(bf16[32,32,128]{2,1,0:T(8,128)(2,1)} %bitcast.15), channel_id=1, replica_groups=mesh['plane'=8,'tile'=32] {'tile'}, dimensions={0} | all-to-all | bytes 524288 | tf_op jit(solution)/shard_map/all_to_all | solution.py:573
  26.7 0.6 rows.1.refs_0_
  27.3 4.3 %collective-permute-start = (bf16[32,1152]{1,0:T(8,128)(2,1)S(1)}, bf16[32,1152]{1,0:T(8,128)(2,1)S(1)}, u32[]{:S(2)}, u32[]{:S(2)}) collective-permute-start(bf16[32,1152]{1,0:T(8,128)(2,1)S(1)} %rows.1.refs_0_), channel_id=1, source_target_pairs={{0,32},{32,0},{64,96},{96,64},{128,160},{160,128},{192,224},{224,1... | collective-permute-start | bytes 221192 | tf_op jit(solution)/shard_map/ppermute | solution.py:571
  31.6 2.7 %collective-permute-start.3 = (bf16[32,1152]{1,0:T(8,128)(2,1)S(1)}, bf16[32,1152]{1,0:T(8,128)(2,1)S(1)}, u32[]{:S(2)}, u32[]{:S(2)}) collective-permute-start(bf16[32,1152]{1,0:T(8,128)(2,1)S(1)} %rows.1.refs_0_), channel_id=1, source_target_pairs={{0,128},{32,160},{64,192},{96,224},{128,0},{160,32},{192,64},{224,... | collective-permute-start | bytes 221192 | tf_op jit(solution)/shard_map/ppermute | solution.py:571
  34.3 0.9 %collective-permute-start.2 = (bf16[32,1152]{1,0:T(8,128)(2,1)S(1)}, bf16[32,1152]{1,0:T(8,128)(2,1)S(1)}, u32[]{:S(2)}, u32[]{:S(2)}) collective-permute-start(bf16[32,1152]{1,0:T(8,128)(2,1)S(1)} %rows.1.refs_0_), channel_id=1, source_target_pairs={{0,192},{32,224},{64,128},{96,160},{128,64},{160,96},{192,0},{224,... | collective-permute-start | bytes 221192 | tf_op jit(solution)/shard_map/ppermute | solution.py:571
  35.2 0.0 collective-permute-start.1
  35.2 0.0 collective-permute-done.refs_1_
  35.2 3.0 %collective-permute-start.6 = (bf16[32,1152]{1,0:T(8,128)(2,1)S(1)}, bf16[32,1152]{1,0:T(8,128)(2,1)S(1)}, u32[]{:S(2)}, u32[]{:S(2)}) collective-permute-start(bf16[32,1152]{1,0:T(8,128)(2,1)S(1)} %collective-permute-done.refs_1_), channel_id=1, source_target_pairs={{0,128},{32,160},{64,192},{96,224},{128,0},{160,32},{192,64},{224,... | collective-permute-start | bytes 221192 | tf_op jit(solution)/shard_map/ppermute | solution.py:571
  38.2 0.9 %collective-permute-start.5 = (bf16[32,1152]{1,0:T(8,128)(2,1)S(1)}, bf16[32,1152]{1,0:T(8,128)(2,1)S(1)}, u32[]{:S(2)}, u32[]{:S(2)}) collective-permute-start(bf16[32,1152]{1,0:T(8,128)(2,1)S(1)} %collective-permute-done.refs_1_), channel_id=1, source_target_pairs={{0,192},{32,224},{64,128},{96,160},{128,64},{160,96},{192,0},{224,... | collective-permute-start | bytes 221192 | tf_op jit(solution)/shard_map/ppermute | solution.py:571
  39.1 0.0 collective-permute-done.3.refs_4_
  39.1 0.0 collective-permute-start.4
  39.1 0.0 collective-permute-done.2.refs_3_
  39.1 0.0 collective-permute-done.1.refs_2_
  39.1 1.8 %collective-permute-done.6.refs_7_ = bf16[32,1152]{1,0:T(8,128)(2,1)S(1)} collective-permute-done((bf16[32,1152]{1,0:T(8,128)(2,1)S(1)}, bf16[32,1152]{1,0:T(8,128)(2,1)S(1)}, u32[]{:S(2)}, u32[]{:S(2)}) %collective-permute-start.6) | collective-permute-done | bytes 73760 | tf_op jit(solution)/shard_map/ppermute | solution.py:571
  40.9 2.2 %collective-permute-done.5.refs_6_ = bf16[32,1152]{1,0:T(8,128)(2,1)S(1)} collective-permute-done((bf16[32,1152]{1,0:T(8,128)(2,1)S(1)}, bf16[32,1152]{1,0:T(8,128)(2,1)S(1)}, u32[]{:S(2)}, u32[]{:S(2)}) %collective-permute-start.5) | collective-permute-done | bytes 73760 | tf_op jit(solution)/shard_map/ppermute | solution.py:571
  43.1 0.0 collective-permute-done.4.refs_5_
  43.1 1.4 %modes.1 = (f32[128,1024]{1,0:T(8,128)S(1)}, f32[64,128]{1,0:T(8,128)S(1)}, s32[16,1024]{1,0:T(8,128)S(1)}, f32[8,128]{1,0:T(8,128)S(1)}) custom-call(s32[4,8]{1,0:T(4,128)S(1)} %copy-done.4, f32[1,32]{1,0:T(1,128)S(1)} %bitcast.14, bf16[32,1152]{1,0:T(8,128)(2,1)S(1)} %rows.1.refs_0_, bf16[32,1152]{1,0:T(8,128)(2,1)S(1)} %collective-permute-done.refs_1_, ...), custom_call_target="tpu_custom_call" | custom-call | tf_op jit(solution)/shard_map/modes/pallas_call | solution.py:354
  44.5 13.0 %all_to_all.34 = f32[32,2,128]{2,1,0:T(2,128)S(1)} all-to-all(f32[32,2,128]{2,1,0:T(2,128)S(1)} %bitcast.12), channel_id=1, replica_groups=mesh['plane'=8,'tile'=32] {'tile'}, dimensions={0} | all-to-all | bytes 65536 | tf_op jit(solution)/shard_map/all_to_all | solution.py:581
  57.5 1.2 %adjoint.1 = (f32[10,16]{1,0:T(8,128)}, bf16[1024,128]{1,0:T(8,128)(2,1)S(1)}) custom-call(f32[8,128]{1,0:T(8,128)S(1)} %get-tuple-element.8.own_ref, f32[64,128]{1,0:T(8,128)S(1)} %bitcast.11, f32[128,1024]{1,0:T(8,128)S(1)} %get-tuple-element.10.kappa_ref, s32[16,1024]{1,0:T(8,128)S(1)} %get-tuple-element.11.ell_ref, f32[10,16]{1,0:T(8,128)S(1)} %copy-done.3, ...), custom_call_target="tpu_custom_call" | custom-call | tf_op jit(solution)/shard_map/adjoint/pallas_call | solution.py:475
  58.7 14.6 %all_to_all.35 = bf16[32,32,128]{2,1,0:T(8,128)(2,1)S(1)} all-to-all(bf16[32,32,128]{2,1,0:T(8,128)(2,1)S(1)} %bitcast.10), channel_id=1, replica_groups=mesh['plane'=8,'tile'=32] {'tile'}, dimensions={0} | all-to-all | bytes 524288 | tf_op jit(solution)/shard_map/all_to_all | solution.py:583
  73.2 2.1 %maps.1 = f32[1,128,4096]{2,1,0:T(8,128)} custom-call(bf16[1024,128]{1,0:T(8,128)(2,1)S(1)} %bitcast.9, bf16[1024,512]{1,0:T(8,128)(2,1)S(1)} %copy-done), custom_call_target="tpu_custom_call" | custom-call | tf_op jit(solution)/shard_map/maps/pallas_call | solution.py:547
  (10 shorter events, 0.0 us)
Async XLA Ops:
  0.6 26.1 %copy-start = (bf16[1024,512]{1,0:T(8,128)(2,1)S(1)}, bf16[1024,512]{1,0:T(8,128)(2,1)}, u32[]{:S(2)}) copy-start(bf16[1024,512]{1,0:T(8,128)(2,1)} %constant.4.clone.table_ref) | copy-start | bytes 3145732
  0.6 42.5 %copy-start.1 = (bf16[1024,512]{1,0:T(8,128)(2,1)S(1)}, bf16[1024,512]{1,0:T(8,128)(2,1)}, u32[]{:S(2)}) copy-start(bf16[1024,512]{1,0:T(8,128)(2,1)} %constant.5.clone.refs_8_) | copy-start | bytes 3145732
  0.7 26.1 %copy-start.2 = (s32[128,16]{0,1:T(8,128)S(1)}, s32[128,16]{0,1:T(8,128)}, u32[]{:S(2)}) copy-start(s32[128,16]{0,1:T(8,128)} %param.12) | copy-start | bytes 24580
  0.7 42.4 %copy-start.4 = (s32[4,8]{1,0:T(4,128)S(1)}, s32[4,8]{1,0:T(4,128)}, u32[]{:S(2)}) copy-start(s32[4,8]{1,0:T(4,128)} %index_ref.1) | copy-start | bytes 388
  0.7 42.4 %copy-start.5 = (f32[32]{0:T(128)S(1)}, f32[32]{0:T(128)}, u32[]{:S(2)}) copy-start(f32[32]{0:T(128)} %param.10) | copy-start | bytes 388
  0.7 56.8 %copy-start.3 = (f32[10,16]{1,0:T(8,128)S(1)}, f32[10,16]{1,0:T(8,128)}, u32[]{:S(2)}) copy-start(f32[10,16]{1,0:T(8,128)} %target_ref.1) | copy-start | bytes 1924
  27.3 7.9 %collective-permute-start = (bf16[32,1152]{1,0:T(8,128)(2,1)S(1)}, bf16[32,1152]{1,0:T(8,128)(2,1)S(1)}, u32[]{:S(2)}, u32[]{:S(2)}) collective-permute-start(bf16[32,1152]{1,0:T(8,128)(2,1)S(1)} %rows.1.refs_0_), channel_id=1, source_target_pairs={{0,32},{32,0},{64,96},{96,64},{128,160},{160,128},{192,224},{224,1... | collective-permute-start | bytes 221192 | tf_op jit(solution)/shard_map/ppermute | solution.py:571
  31.6 7.5 %collective-permute-start.3 = (bf16[32,1152]{1,0:T(8,128)(2,1)S(1)}, bf16[32,1152]{1,0:T(8,128)(2,1)S(1)}, u32[]{:S(2)}, u32[]{:S(2)}) collective-permute-start(bf16[32,1152]{1,0:T(8,128)(2,1)S(1)} %rows.1.refs_0_), channel_id=1, source_target_pairs={{0,128},{32,160},{64,192},{96,224},{128,0},{160,32},{192,64},{224,... | collective-permute-start | bytes 221192 | tf_op jit(solution)/shard_map/ppermute | solution.py:571
  34.3 4.7 %collective-permute-start.2 = (bf16[32,1152]{1,0:T(8,128)(2,1)S(1)}, bf16[32,1152]{1,0:T(8,128)(2,1)S(1)}, u32[]{:S(2)}, u32[]{:S(2)}) collective-permute-start(bf16[32,1152]{1,0:T(8,128)(2,1)S(1)} %rows.1.refs_0_), channel_id=1, source_target_pairs={{0,192},{32,224},{64,128},{96,160},{128,64},{160,96},{192,0},{224,... | collective-permute-start | bytes 221192 | tf_op jit(solution)/shard_map/ppermute | solution.py:571
  35.2 3.9 %collective-permute-start.1 = (bf16[32,1152]{1,0:T(8,128)(2,1)S(1)}, bf16[32,1152]{1,0:T(8,128)(2,1)S(1)}, u32[]{:S(2)}, u32[]{:S(2)}) collective-permute-start(bf16[32,1152]{1,0:T(8,128)(2,1)S(1)} %rows.1.refs_0_), channel_id=1, source_target_pairs={{0,64},{32,96},{64,0},{96,32},{128,192},{160,224},{192,128},{224,1... | collective-permute-start | bytes 221192 | tf_op jit(solution)/shard_map/ppermute | solution.py:571
  35.2 5.7 %collective-permute-start.6 = (bf16[32,1152]{1,0:T(8,128)(2,1)S(1)}, bf16[32,1152]{1,0:T(8,128)(2,1)S(1)}, u32[]{:S(2)}, u32[]{:S(2)}) collective-permute-start(bf16[32,1152]{1,0:T(8,128)(2,1)S(1)} %collective-permute-done.refs_1_), channel_id=1, source_target_pairs={{0,128},{32,160},{64,192},{96,224},{128,0},{160,32},{192,64},{224,... | collective-permute-start | bytes 221192 | tf_op jit(solution)/shard_map/ppermute | solution.py:571
  38.2 4.9 %collective-permute-start.5 = (bf16[32,1152]{1,0:T(8,128)(2,1)S(1)}, bf16[32,1152]{1,0:T(8,128)(2,1)S(1)}, u32[]{:S(2)}, u32[]{:S(2)}) collective-permute-start(bf16[32,1152]{1,0:T(8,128)(2,1)S(1)} %collective-permute-done.refs_1_), channel_id=1, source_target_pairs={{0,192},{32,224},{64,128},{96,160},{128,64},{160,96},{192,0},{224,... | collective-permute-start | bytes 221192 | tf_op jit(solution)/shard_map/ppermute | solution.py:571
  39.1 4.0 %collective-permute-start.4 = (bf16[32,1152]{1,0:T(8,128)(2,1)S(1)}, bf16[32,1152]{1,0:T(8,128)(2,1)S(1)}, u32[]{:S(2)}, u32[]{:S(2)}) collective-permute-start(bf16[32,1152]{1,0:T(8,128)(2,1)S(1)} %collective-permute-done.refs_1_), channel_id=1, source_target_pairs={{0,64},{32,96},{64,0},{96,32},{128,192},{160,224},{192,128},{224,1... | collective-permute-start | bytes 221192 | tf_op jit(solution)/shard_map/ppermute | solution.py:571

commit v6 on v5

--- a/solution.py
+++ b/solution.py
@@ -24,6 +24,8 @@
 WIDTH = 2 * KMAX + ROWS
 PAIRS = BINS * (BINS + 1) // 2
 CHUNKS = ROWS // CHUNK
+STRIP = 32
+STRIPS = ROWS // STRIP
 
 ORDER = (0, 4, 1, 7, 2, 6, 3, 5)
 PLACE = {rho: place for place, rho in enumerate(ORDER)}
@@ -394,28 +396,26 @@
         float(KMAX) / (ELLS * NPIX)
     ) / area[:, :ELLS]
 
-    couplings = []
-    for number in range(PAIRS):
-        row = weight_ref[number : number + 1, :]
-        row = row + row if number in (PAIR_ID[(i, i)] for i in range(BINS)) else row
-        couplings.append(jnp.broadcast_to(row, (8, LANES)))
-    weights = [own_ref[b : b + 1, :] for b in range(BINS)]
+    tables = []
+    for j in range(BINS):
+        total = None
+        for i in range(BINS):
+            number = PAIR_ID[(i, j)]
+            row = weight_ref[number : number + 1, :]
+            term = own_ref[i : i + 1, :] * (row + row if i == j else row)
+            total = term if total is None else total + term
+        tables.append(jnp.broadcast_to(total, (8, LANES)))
 
     for tile in range(RADIX):
         cols = slice(tile * LANES, (tile + 1) * LANES)
         for half in range(0, 16, 8):
             where = ell_ref[half : half + 8, cols]
-            mixers = [jnp.take_along_axis(table, where, axis=1) for table in couplings]
+            mixers = [jnp.take_along_axis(table, where, axis=1) for table in tables]
             for s in range(2):
                 start = 16 * s + half
-                kappa = [kappa_ref[32 * b + start : 32 * b + start + 8, cols] for b in range(BINS)]
-                line = None
-                for i in range(BINS):
-                    grad = mixers[PAIR_ID[(i, 0)]] * kappa[0]
-                    for j in range(1, BINS):
-                        grad = grad + mixers[PAIR_ID[(i, j)]] * kappa[j]
-                    term = grad.astype(BF16).astype(F32) * weights[i]
-                    line = term if i == 0 else line + term
+                line = mixers[0] * kappa_ref[start : start + 8, cols]
+                for j in range(1, BINS):
+                    line = line + mixers[j] * kappa_ref[32 * j + start : 32 * j + start + 8, cols]
                 line_ref[start : start + 8, cols] = line
 
     wide_lane = lax.broadcasted_iota(jnp.int32, (16, LANES), 1)
@@ -520,11 +520,11 @@
         spread_ref[index] = part
 
     def send(chunk):
-        rows = pl.ds(chunk * CHUNK, CHUNK)
+        rows = pl.ds(chunk * STRIP, STRIP)
         return pltpu.make_async_copy(done_ref.at[rows, :], out_ref.at[0, rows, :], sems.at[chunk])
 
-    for chunk in range(CHUNKS):
-        rows = slice(chunk * CHUNK, (chunk + 1) * CHUNK)
+    for chunk in range(STRIPS):
+        rows = slice(chunk * STRIP, (chunk + 1) * STRIP)
         for start in range(0, SPAN, LANES):
             cols = slice(start, start + LANES)
             a0, a4, p1, p2, p3, q1, q2, q3 = (spread_ref[index, rows, cols] for index in range(RADIX))
@@ -539,7 +539,7 @@
             put(2, plus - p2, q3 - q1)
             put(3, minus + q2, HALF * (p3 - p1 - q1 - q3))
         send(chunk).start()
-    for chunk in range(CHUNKS):
+    for chunk in range(STRIPS):
         send(chunk).wait()
 
 
@@ -553,7 +553,7 @@
             pltpu.VMEM((2 * KMAX, ROWS), F32),
             pltpu.VMEM((RADIX, ROWS, SPAN), F32),
             pltpu.VMEM((ROWS, NPIX), F32),
-            pltpu.SemaphoreType.DMA((CHUNKS,)),
+            pltpu.SemaphoreType.DMA((STRIPS,)),
         ],
         compiler_params=pltpu.CompilerParams(vmem_limit_bytes=LIMIT),
         name="maps",

time: 75.6 us -> 75.4 us (level)
  no operation moved by 1% of the time
where the time goes in v6:
time: 75.4 us; the launch traced here: 75.2 us
  blocking collectives  49 us (65%)
  starting transfers between devices  11.8 us (16%)
  Pallas kernels  9.64 us (13%)
  waiting for transfers between devices  4.03 us (5%)
    all_to_all x1, blocking collectives, body(): band = exchange(columns(slab_cells, slab_weight, table))  21.5 us
    all_to_all x1, blocking collectives, body(): return (spectra, maps(exchange(adjoint_band), table))  14.6 us
    all_to_all x1, blocking collectives, body(): exchange(sums)  13 us
    ppermute x7, starting transfers between devices, swap(): return lax.ppermute(value, 'plane', [(p, p ^ bits) for p in range(N_PLANE)])  11.8 us
    pallas_call x1, Pallas kernels, columns(): pl.pallas_call(columns_kernel, in_specs=[hbm] * 3, out_specs=VMEM, out_sh...  4.54 us
    ppermute x7, waiting for transfers between devices, swap(): return lax.ppermute(value, 'plane', [(p, p ^ bits) for p in range(N_PLANE)])  4.03 us
    pallas_call x1, Pallas kernels, maps(): pl.pallas_call(maps_kernel, in_specs=[VMEM, VMEM], out_specs=pl.BlockSpec...  2.1 us
  transfers between devices with their start and end apart: 7, of which 2 were waited for; matrix products, arithmetic and copies ran while one was open for 0% of the time, Pallas kernels for 0%

profile of v6, /device:TPU:1, one launch (start us, length us, event | category | flops | bytes accessed | tf_op | source)
XLA Modules:
  0.0 75.2 jit_solution(14796686014678146744)
XLA Ops:
  0.6 0.0 copy-start
  0.6 0.0 copy-start.1
  0.7 4.5 %columns.1 = bf16[1024,128]{1,0:T(8,128)(2,1)} custom-call(f32[1,4]{1,0:T(1,128)} %weight_ref.1, bf16[1,4,128,4096]{3,2,1,0:T(8,128)(2,1)} %slab_ref.1, bf16[1024,512]{1,0:T(8,128)(2,1)} %constant.4.clone.table_ref), custom_call_target="tpu_custom_call" | custom-call | tf_op jit(solution)/shard_map/columns/pallas_call | solution.py:196
  5.2 21.5 %all_to_all.33 = bf16[32,32,128]{2,1,0:T(8,128)(2,1)S(1)} all-to-all(bf16[32,32,128]{2,1,0:T(8,128)(2,1)} %bitcast.15), channel_id=1, replica_groups=mesh['plane'=8,'tile'=32] {'tile'}, dimensions={0} | all-to-all | bytes 524288 | tf_op jit(solution)/shard_map/all_to_all | solution.py:573
  26.7 0.6 rows.1.refs_0_
  27.3 4.3 %collective-permute-start = (bf16[32,1152]{1,0:T(8,128)(2,1)S(1)}, bf16[32,1152]{1,0:T(8,128)(2,1)S(1)}, u32[]{:S(2)}, u32[]{:S(2)}) collective-permute-start(bf16[32,1152]{1,0:T(8,128)(2,1)S(1)} %rows.1.refs_0_), channel_id=1, source_target_pairs={{0,32},{32,0},{64,96},{96,64},{128,160},{160,128},{192,224},{224,1... | collective-permute-start | bytes 221192 | tf_op jit(solution)/shard_map/ppermute | solution.py:571
  31.6 2.7 %collective-permute-start.3 = (bf16[32,1152]{1,0:T(8,128)(2,1)S(1)}, bf16[32,1152]{1,0:T(8,128)(2,1)S(1)}, u32[]{:S(2)}, u32[]{:S(2)}) collective-permute-start(bf16[32,1152]{1,0:T(8,128)(2,1)S(1)} %rows.1.refs_0_), channel_id=1, source_target_pairs={{0,128},{32,160},{64,192},{96,224},{128,0},{160,32},{192,64},{224,... | collective-permute-start | bytes 221192 | tf_op jit(solution)/shard_map/ppermute | solution.py:571
  34.3 0.9 %collective-permute-start.2 = (bf16[32,1152]{1,0:T(8,128)(2,1)S(1)}, bf16[32,1152]{1,0:T(8,128)(2,1)S(1)}, u32[]{:S(2)}, u32[]{:S(2)}) collective-permute-start(bf16[32,1152]{1,0:T(8,128)(2,1)S(1)} %rows.1.refs_0_), channel_id=1, source_target_pairs={{0,192},{32,224},{64,128},{96,160},{128,64},{160,96},{192,0},{224,... | collective-permute-start | bytes 221192 | tf_op jit(solution)/shard_map/ppermute | solution.py:571
  35.2 0.0 collective-permute-start.1
  35.2 0.0 collective-permute-done.refs_1_
  35.2 3.0 %collective-permute-start.6 = (bf16[32,1152]{1,0:T(8,128)(2,1)S(1)}, bf16[32,1152]{1,0:T(8,128)(2,1)S(1)}, u32[]{:S(2)}, u32[]{:S(2)}) collective-permute-start(bf16[32,1152]{1,0:T(8,128)(2,1)S(1)} %collective-permute-done.refs_1_), channel_id=1, source_target_pairs={{0,128},{32,160},{64,192},{96,224},{128,0},{160,32},{192,64},{224,... | collective-permute-start | bytes 221192 | tf_op jit(solution)/shard_map/ppermute | solution.py:571
  38.2 0.9 %collective-permute-start.5 = (bf16[32,1152]{1,0:T(8,128)(2,1)S(1)}, bf16[32,1152]{1,0:T(8,128)(2,1)S(1)}, u32[]{:S(2)}, u32[]{:S(2)}) collective-permute-start(bf16[32,1152]{1,0:T(8,128)(2,1)S(1)} %collective-permute-done.refs_1_), channel_id=1, source_target_pairs={{0,192},{32,224},{64,128},{96,160},{128,64},{160,96},{192,0},{224,... | collective-permute-start | bytes 221192 | tf_op jit(solution)/shard_map/ppermute | solution.py:571
  39.1 0.0 collective-permute-done.3.refs_4_
  39.1 0.0 collective-permute-start.4
  39.1 0.0 collective-permute-done.2.refs_3_
  39.1 0.0 collective-permute-done.1.refs_2_
  39.1 1.8 %collective-permute-done.6.refs_7_ = bf16[32,1152]{1,0:T(8,128)(2,1)S(1)} collective-permute-done((bf16[32,1152]{1,0:T(8,128)(2,1)S(1)}, bf16[32,1152]{1,0:T(8,128)(2,1)S(1)}, u32[]{:S(2)}, u32[]{:S(2)}) %collective-permute-start.6) | collective-permute-done | bytes 73760 | tf_op jit(solution)/shard_map/ppermute | solution.py:571
  40.9 2.2 %collective-permute-done.5.refs_6_ = bf16[32,1152]{1,0:T(8,128)(2,1)S(1)} collective-permute-done((bf16[32,1152]{1,0:T(8,128)(2,1)S(1)}, bf16[32,1152]{1,0:T(8,128)(2,1)S(1)}, u32[]{:S(2)}, u32[]{:S(2)}) %collective-permute-start.5) | collective-permute-done | bytes 73760 | tf_op jit(solution)/shard_map/ppermute | solution.py:571
  43.1 0.0 collective-permute-done.4.refs_5_
  43.1 1.4 %modes.1 = (f32[128,1024]{1,0:T(8,128)S(1)}, f32[64,128]{1,0:T(8,128)S(1)}, s32[16,1024]{1,0:T(8,128)S(1)}, f32[8,128]{1,0:T(8,128)S(1)}) custom-call(s32[4,8]{1,0:T(4,128)S(1)} %copy-done.4, f32[1,32]{1,0:T(1,128)S(1)} %bitcast.14, bf16[32,1152]{1,0:T(8,128)(2,1)S(1)} %rows.1.refs_0_, bf16[32,1152]{1,0:T(8,128)(2,1)S(1)} %collective-permute-done.refs_1_, ...), custom_call_target="tpu_custom_call" | custom-call | tf_op jit(solution)/shard_map/modes/pallas_call | solution.py:356
  44.5 13.0 %all_to_all.34 = f32[32,2,128]{2,1,0:T(2,128)S(1)} all-to-all(f32[32,2,128]{2,1,0:T(2,128)S(1)} %bitcast.12), channel_id=1, replica_groups=mesh['plane'=8,'tile'=32] {'tile'}, dimensions={0} | all-to-all | bytes 65536 | tf_op jit(solution)/shard_map/all_to_all | solution.py:581
  57.5 1.1 %adjoint.1 = (f32[10,16]{1,0:T(8,128)}, bf16[1024,128]{1,0:T(8,128)(2,1)S(1)}) custom-call(f32[8,128]{1,0:T(8,128)S(1)} %get-tuple-element.8.own_ref, f32[64,128]{1,0:T(8,128)S(1)} %bitcast.11, f32[128,1024]{1,0:T(8,128)S(1)} %get-tuple-element.10.kappa_ref, s32[16,1024]{1,0:T(8,128)S(1)} %get-tuple-element.11.ell_ref, f32[10,16]{1,0:T(8,128)S(1)} %copy-done.3, ...), custom_call_target="tpu_custom_call" | custom-call | tf_op jit(solution)/shard_map/adjoint/pallas_call | solution.py:475
  58.5 14.6 %all_to_all.35 = bf16[32,32,128]{2,1,0:T(8,128)(2,1)S(1)} all-to-all(bf16[32,32,128]{2,1,0:T(8,128)(2,1)S(1)} %bitcast.10), channel_id=1, replica_groups=mesh['plane'=8,'tile'=32] {'tile'}, dimensions={0} | all-to-all | bytes 524288 | tf_op jit(solution)/shard_map/all_to_all | solution.py:583
  73.1 2.1 %maps.1 = f32[1,128,4096]{2,1,0:T(8,128)} custom-call(bf16[1024,128]{1,0:T(8,128)(2,1)S(1)} %bitcast.9, bf16[1024,512]{1,0:T(8,128)(2,1)S(1)} %copy-done), custom_call_target="tpu_custom_call" | custom-call | tf_op jit(solution)/shard_map/maps/pallas_call | solution.py:547
  (10 shorter events, 0.0 us)
Async XLA Ops:
  0.6 26.1 %copy-start = (bf16[1024,512]{1,0:T(8,128)(2,1)S(1)}, bf16[1024,512]{1,0:T(8,128)(2,1)}, u32[]{:S(2)}) copy-start(bf16[1024,512]{1,0:T(8,128)(2,1)} %constant.4.clone.table_ref) | copy-start | bytes 3145732
  0.6 42.5 %copy-start.1 = (bf16[1024,512]{1,0:T(8,128)(2,1)S(1)}, bf16[1024,512]{1,0:T(8,128)(2,1)}, u32[]{:S(2)}) copy-start(bf16[1024,512]{1,0:T(8,128)(2,1)} %constant.5.clone.refs_8_) | copy-start | bytes 3145732
  0.7 26.1 %copy-start.2 = (s32[128,16]{0,1:T(8,128)S(1)}, s32[128,16]{0,1:T(8,128)}, u32[]{:S(2)}) copy-start(s32[128,16]{0,1:T(8,128)} %param.12) | copy-start | bytes 24580
  0.7 42.4 %copy-start.4 = (s32[4,8]{1,0:T(4,128)S(1)}, s32[4,8]{1,0:T(4,128)}, u32[]{:S(2)}) copy-start(s32[4,8]{1,0:T(4,128)} %index_ref.1) | copy-start | bytes 388
  0.7 42.4 %copy-start.5 = (f32[32]{0:T(128)S(1)}, f32[32]{0:T(128)}, u32[]{:S(2)}) copy-start(f32[32]{0:T(128)} %param.10) | copy-start | bytes 388
  0.7 56.8 %copy-start.3 = (f32[10,16]{1,0:T(8,128)S(1)}, f32[10,16]{1,0:T(8,128)}, u32[]{:S(2)}) copy-start(f32[10,16]{1,0:T(8,128)} %target_ref.1) | copy-start | bytes 1924
  27.3 7.9 %collective-permute-start = (bf16[32,1152]{1,0:T(8,128)(2,1)S(1)}, bf16[32,1152]{1,0:T(8,128)(2,1)S(1)}, u32[]{:S(2)}, u32[]{:S(2)}) collective-permute-start(bf16[32,1152]{1,0:T(8,128)(2,1)S(1)} %rows.1.refs_0_), channel_id=1, source_target_pairs={{0,32},{32,0},{64,96},{96,64},{128,160},{160,128},{192,224},{224,1... | collective-permute-start | bytes 221192 | tf_op jit(solution)/shard_map/ppermute | solution.py:571
  31.6 7.5 %collective-permute-start.3 = (bf16[32,1152]{1,0:T(8,128)(2,1)S(1)}, bf16[32,1152]{1,0:T(8,128)(2,1)S(1)}, u32[]{:S(2)}, u32[]{:S(2)}) collective-permute-start(bf16[32,1152]{1,0:T(8,128)(2,1)S(1)} %rows.1.refs_0_), channel_id=1, source_target_pairs={{0,128},{32,160},{64,192},{96,224},{128,0},{160,32},{192,64},{224,... | collective-permute-start | bytes 221192 | tf_op jit(solution)/shard_map/ppermute | solution.py:571
  34.3 4.7 %collective-permute-start.2 = (bf16[32,1152]{1,0:T(8,128)(2,1)S(1)}, bf16[32,1152]{1,0:T(8,128)(2,1)S(1)}, u32[]{:S(2)}, u32[]{:S(2)}) collective-permute-start(bf16[32,1152]{1,0:T(8,128)(2,1)S(1)} %rows.1.refs_0_), channel_id=1, source_target_pairs={{0,192},{32,224},{64,128},{96,160},{128,64},{160,96},{192,0},{224,... | collective-permute-start | bytes 221192 | tf_op jit(solution)/shard_map/ppermute | solution.py:571
  35.2 3.9 %collective-permute-start.1 = (bf16[32,1152]{1,0:T(8,128)(2,1)S(1)}, bf16[32,1152]{1,0:T(8,128)(2,1)S(1)}, u32[]{:S(2)}, u32[]{:S(2)}) collective-permute-start(bf16[32,1152]{1,0:T(8,128)(2,1)S(1)} %rows.1.refs_0_), channel_id=1, source_target_pairs={{0,64},{32,96},{64,0},{96,32},{128,192},{160,224},{192,128},{224,1... | collective-permute-start | bytes 221192 | tf_op jit(solution)/shard_map/ppermute | solution.py:571
  35.2 5.7 %collective-permute-start.6 = (bf16[32,1152]{1,0:T(8,128)(2,1)S(1)}, bf16[32,1152]{1,0:T(8,128)(2,1)S(1)}, u32[]{:S(2)}, u32[]{:S(2)}) collective-permute-start(bf16[32,1152]{1,0:T(8,128)(2,1)S(1)} %collective-permute-done.refs_1_), channel_id=1, source_target_pairs={{0,128},{32,160},{64,192},{96,224},{128,0},{160,32},{192,64},{224,... | collective-permute-start | bytes 221192 | tf_op jit(solution)/shard_map/ppermute | solution.py:571
  38.2 4.9 %collective-permute-start.5 = (bf16[32,1152]{1,0:T(8,128)(2,1)S(1)}, bf16[32,1152]{1,0:T(8,128)(2,1)S(1)}, u32[]{:S(2)}, u32[]{:S(2)}) collective-permute-start(bf16[32,1152]{1,0:T(8,128)(2,1)S(1)} %collective-permute-done.refs_1_), channel_id=1, source_target_pairs={{0,192},{32,224},{64,128},{96,160},{128,64},{160,96},{192,0},{224,... | collective-permute-start | bytes 221192 | tf_op jit(solution)/shard_map/ppermute | solution.py:571
  39.1 4.0 %collective-permute-start.4 = (bf16[32,1152]{1,0:T(8,128)(2,1)S(1)}, bf16[32,1152]{1,0:T(8,128)(2,1)S(1)}, u32[]{:S(2)}, u32[]{:S(2)}) collective-permute-start(bf16[32,1152]{1,0:T(8,128)(2,1)S(1)} %collective-permute-done.refs_1_), channel_id=1, source_target_pairs={{0,64},{32,96},{64,0},{96,32},{128,192},{160,224},{192,128},{224,1... | collective-permute-start | bytes 221192 | tf_op jit(solution)/shard_map/ppermute | solution.py:571

commit v7 on v6

--- a/solution.py
+++ b/solution.py
@@ -126,8 +126,8 @@
     def fetch_table():
         return pltpu.make_async_copy(table_ref, held_ref, table_sem)
 
-    for chunk in range(CHUNKS):
-        fetch(chunk).start(priority=chunk % 2)
+    for chunk in range(8):
+        fetch(chunk).start()
     scales = pltpu.make_async_copy(weight_ref, scale_ref, scale_sem)
     scales.start()
     fetch_table().start()
@@ -166,6 +166,8 @@
 
     for chunk in range(CHUNKS):
         fetch(chunk).wait()
+        if chunk + 8 < CHUNKS:
+            fetch(chunk + 8).start()
         for start in range(0, SPAN, LANES):
             butterfly(chunk, start)
     fetch_table().wait()
@@ -208,7 +210,7 @@
             pltpu.SemaphoreType.DMA,
             pltpu.SemaphoreType.DMA,
         ],
-        compiler_params=pltpu.CompilerParams(vmem_limit_bytes=60 * 1024 * 1024),
+        compiler_params=pltpu.CompilerParams(vmem_limit_bytes=53 * 1024 * 1024),
         name="columns",
     )(weight, slab, table)
 

time: 75.4 us -> 74.8 us (level)
  Pallas kernels: 9.64 us -> 8.47 us
  local copies, waits for them, and re-layouts: 0.03 us -> 0.82 us
    pallas_call x1, Pallas kernels: 4.54 us -> 3.31 us  [columns(): pl.pallas_call(columns_kernel, in_specs=[hbm] * 3, out_specs=VMEM, out_sh...]
    unnamed x12 -> x14, local copies, waits for them, and re-layouts: 0.03 us -> 0.82 us
where the time goes in v7:
time: 74.8 us; the launch traced here: 74.6 us
  blocking collectives  48.8 us (65%)
  starting transfers between devices  11.8 us (16%)
  Pallas kernels  8.47 us (11%)
  waiting for transfers between devices  4.02 us (5%)
  local copies, waits for them, and re-layouts  0.82 us (1%)
    all_to_all x1, blocking collectives, body(): band = exchange(columns(slab_cells, slab_weight, table))  21.3 us
    all_to_all x1, blocking collectives, body(): return (spectra, maps(exchange(adjoint_band), table))  14.6 us
    all_to_all x1, blocking collectives, body(): exchange(sums)  13 us
    ppermute x7, starting transfers between devices, swap(): return lax.ppermute(value, 'plane', [(p, p ^ bits) for p in range(N_PLANE)])  11.8 us
    ppermute x7, waiting for transfers between devices, swap(): return lax.ppermute(value, 'plane', [(p, p ^ bits) for p in range(N_PLANE)])  4.02 us
    pallas_call x1, Pallas kernels, columns(): pl.pallas_call(columns_kernel, in_specs=[hbm] * 3, out_specs=VMEM, out_sh...  3.31 us
    pallas_call x1, Pallas kernels, maps(): pl.pallas_call(maps_kernel, in_specs=[VMEM, VMEM], out_specs=pl.BlockSpec...  2.13 us
  transfers between devices with their start and end apart: 7, of which 2 were waited for; matrix products, arithmetic and copies ran while one was open for 0% of the time, Pallas kernels for 0%

profile of v7, /device:TPU:1, one launch (start us, length us, event | category | flops | bytes accessed | tf_op | source)
XLA Modules:
  0.0 74.6 jit_solution(9356861396335983846)
XLA Ops:
  0.6 0.0 copy-start
  0.6 0.0 copy-start.1
  0.7 0.8 %copy-done.5 = f32[1,4]{1,0:T(1,128)S(1)} copy-done((f32[1,4]{1,0:T(1,128)S(1)}, f32[1,4]{1,0:T(1,128)}, u32[]{:S(2)}) %copy-start.5) | copy-done | bytes 40
  1.5 3.3 %columns.1 = bf16[1024,128]{1,0:T(8,128)(2,1)S(1)} custom-call(f32[1,4]{1,0:T(1,128)S(1)} %copy-done.5, bf16[1,4,128,4096]{3,2,1,0:T(8,128)(2,1)} %slab_ref.1, bf16[1024,512]{1,0:T(8,128)(2,1)} %constant.4.clone.table_ref), custom_call_target="tpu_custom_call" | custom-call | tf_op jit(solution)/shard_map/columns/pallas_call | solution.py:198
  4.8 21.3 %all_to_all.33 = bf16[32,32,128]{2,1,0:T(8,128)(2,1)S(1)} all-to-all(bf16[32,32,128]{2,1,0:T(8,128)(2,1)S(1)} %bitcast.8), channel_id=1, replica_groups=mesh['plane'=8,'tile'=32] {'tile'}, dimensions={0} | all-to-all | bytes 524288 | tf_op jit(solution)/shard_map/all_to_all | solution.py:575
  26.1 0.6 rows.1.refs_0_
  26.6 4.3 %collective-permute-start = (bf16[32,1152]{1,0:T(8,128)(2,1)S(1)}, bf16[32,1152]{1,0:T(8,128)(2,1)S(1)}, u32[]{:S(2)}, u32[]{:S(2)}) collective-permute-start(bf16[32,1152]{1,0:T(8,128)(2,1)S(1)} %rows.1.refs_0_), channel_id=1, source_target_pairs={{0,32},{32,0},{64,96},{96,64},{128,160},{160,128},{192,224},{224,1... | collective-permute-start | bytes 221192 | tf_op jit(solution)/shard_map/ppermute | solution.py:573
  31.0 2.7 %collective-permute-start.3 = (bf16[32,1152]{1,0:T(8,128)(2,1)S(1)}, bf16[32,1152]{1,0:T(8,128)(2,1)S(1)}, u32[]{:S(2)}, u32[]{:S(2)}) collective-permute-start(bf16[32,1152]{1,0:T(8,128)(2,1)S(1)} %rows.1.refs_0_), channel_id=1, source_target_pairs={{0,128},{32,160},{64,192},{96,224},{128,0},{160,32},{192,64},{224,... | collective-permute-start | bytes 221192 | tf_op jit(solution)/shard_map/ppermute | solution.py:573
  33.7 0.9 %collective-permute-start.2 = (bf16[32,1152]{1,0:T(8,128)(2,1)S(1)}, bf16[32,1152]{1,0:T(8,128)(2,1)S(1)}, u32[]{:S(2)}, u32[]{:S(2)}) collective-permute-start(bf16[32,1152]{1,0:T(8,128)(2,1)S(1)} %rows.1.refs_0_), channel_id=1, source_target_pairs={{0,192},{32,224},{64,128},{96,160},{128,64},{160,96},{192,0},{224,... | collective-permute-start | bytes 221192 | tf_op jit(solution)/shard_map/ppermute | solution.py:573
  34.6 0.0 collective-permute-start.1
  34.6 0.0 collective-permute-done.refs_1_
  34.6 3.0 %collective-permute-start.6 = (bf16[32,1152]{1,0:T(8,128)(2,1)S(1)}, bf16[32,1152]{1,0:T(8,128)(2,1)S(1)}, u32[]{:S(2)}, u32[]{:S(2)}) collective-permute-start(bf16[32,1152]{1,0:T(8,128)(2,1)S(1)} %collective-permute-done.refs_1_), channel_id=1, source_target_pairs={{0,128},{32,160},{64,192},{96,224},{128,0},{160,32},{192,64},{224,... | collective-permute-start | bytes 221192 | tf_op jit(solution)/shard_map/ppermute | solution.py:573
  37.6 0.9 %collective-permute-start.5 = (bf16[32,1152]{1,0:T(8,128)(2,1)S(1)}, bf16[32,1152]{1,0:T(8,128)(2,1)S(1)}, u32[]{:S(2)}, u32[]{:S(2)}) collective-permute-start(bf16[32,1152]{1,0:T(8,128)(2,1)S(1)} %collective-permute-done.refs_1_), channel_id=1, source_target_pairs={{0,192},{32,224},{64,128},{96,160},{128,64},{160,96},{192,0},{224,... | collective-permute-start | bytes 221192 | tf_op jit(solution)/shard_map/ppermute | solution.py:573
  38.4 0.0 collective-permute-done.3.refs_4_
  38.4 0.0 collective-permute-start.4
  38.4 0.0 collective-permute-done.2.refs_3_
  38.4 0.0 collective-permute-done.1.refs_2_
  38.4 1.8 %collective-permute-done.6.refs_7_ = bf16[32,1152]{1,0:T(8,128)(2,1)S(1)} collective-permute-done((bf16[32,1152]{1,0:T(8,128)(2,1)S(1)}, bf16[32,1152]{1,0:T(8,128)(2,1)S(1)}, u32[]{:S(2)}, u32[]{:S(2)}) %collective-permute-start.6) | collective-permute-done | bytes 73760 | tf_op jit(solution)/shard_map/ppermute | solution.py:573
  40.2 2.2 %collective-permute-done.5.refs_6_ = bf16[32,1152]{1,0:T(8,128)(2,1)S(1)} collective-permute-done((bf16[32,1152]{1,0:T(8,128)(2,1)S(1)}, bf16[32,1152]{1,0:T(8,128)(2,1)S(1)}, u32[]{:S(2)}, u32[]{:S(2)}) %collective-permute-start.5) | collective-permute-done | bytes 73760 | tf_op jit(solution)/shard_map/ppermute | solution.py:573
  42.5 1.4 %modes.1 = (f32[128,1024]{1,0:T(8,128)S(1)}, f32[64,128]{1,0:T(8,128)S(1)}, s32[16,1024]{1,0:T(8,128)S(1)}, f32[8,128]{1,0:T(8,128)S(1)}) custom-call(s32[4,8]{1,0:T(4,128)S(1)} %copy-done.4, f32[1,32]{1,0:T(1,128)S(1)} %bitcast.15, bf16[32,1152]{1,0:T(8,128)(2,1)S(1)} %rows.1.refs_0_, bf16[32,1152]{1,0:T(8,128)(2,1)S(1)} %collective-permute-done.refs_1_, ...), custom_call_target="tpu_custom_call" | custom-call | tf_op jit(solution)/shard_map/modes/pallas_call | solution.py:358
  43.9 13.0 %all_to_all.34 = f32[32,2,128]{2,1,0:T(2,128)S(1)} all-to-all(f32[32,2,128]{2,1,0:T(2,128)S(1)} %bitcast.13), channel_id=1, replica_groups=mesh['plane'=8,'tile'=32] {'tile'}, dimensions={0} | all-to-all | bytes 65536 | tf_op jit(solution)/shard_map/all_to_all | solution.py:583
  56.8 1.1 %adjoint.1 = (f32[10,16]{1,0:T(8,128)}, bf16[1024,128]{1,0:T(8,128)(2,1)S(1)}) custom-call(f32[8,128]{1,0:T(8,128)S(1)} %get-tuple-element.8.own_ref, f32[64,128]{1,0:T(8,128)S(1)} %bitcast.12, f32[128,1024]{1,0:T(8,128)S(1)} %get-tuple-element.10.kappa_ref, s32[16,1024]{1,0:T(8,128)S(1)} %get-tuple-element.11.ell_ref, f32[10,16]{1,0:T(8,128)S(1)} %copy-done.3, ...), custom_call_target="tpu_custom_call" | custom-call | tf_op jit(solution)/shard_map/adjoint/pallas_call | solution.py:477
  57.9 14.6 %all_to_all.35 = bf16[32,32,128]{2,1,0:T(8,128)(2,1)S(1)} all-to-all(bf16[32,32,128]{2,1,0:T(8,128)(2,1)S(1)} %bitcast.11), channel_id=1, replica_groups=mesh['plane'=8,'tile'=32] {'tile'}, dimensions={0} | all-to-all | bytes 524288 | tf_op jit(solution)/shard_map/all_to_all | solution.py:585
  72.4 2.1 %maps.1 = f32[1,128,4096]{2,1,0:T(8,128)} custom-call(bf16[1024,128]{1,0:T(8,128)(2,1)S(1)} %bitcast.10, bf16[1024,512]{1,0:T(8,128)(2,1)S(1)} %copy-done), custom_call_target="tpu_custom_call" | custom-call | tf_op jit(solution)/shard_map/maps/pallas_call | solution.py:549
  (12 shorter events, 0.0 us)
Async XLA Ops:
  0.6 25.4 %copy-start = (bf16[1024,512]{1,0:T(8,128)(2,1)S(1)}, bf16[1024,512]{1,0:T(8,128)(2,1)}, u32[]{:S(2)}) copy-start(bf16[1024,512]{1,0:T(8,128)(2,1)} %constant.4.clone.table_ref) | copy-start | bytes 3145732
  0.6 41.8 %copy-start.1 = (bf16[1024,512]{1,0:T(8,128)(2,1)S(1)}, bf16[1024,512]{1,0:T(8,128)(2,1)}, u32[]{:S(2)}) copy-start(bf16[1024,512]{1,0:T(8,128)(2,1)} %constant.5.clone.refs_8_) | copy-start | bytes 3145732
  0.7 25.4 %copy-start.2 = (s32[128,16]{0,1:T(8,128)S(1)}, s32[128,16]{0,1:T(8,128)}, u32[]{:S(2)}) copy-start(s32[128,16]{0,1:T(8,128)} %param.12) | copy-start | bytes 24580
  0.7 41.8 %copy-start.4 = (s32[4,8]{1,0:T(4,128)S(1)}, s32[4,8]{1,0:T(4,128)}, u32[]{:S(2)}) copy-start(s32[4,8]{1,0:T(4,128)} %index_ref.1) | copy-start | bytes 388
  0.7 0.8 %copy-start.5 = (f32[1,4]{1,0:T(1,128)S(1)}, f32[1,4]{1,0:T(1,128)}, u32[]{:S(2)}) copy-start(f32[1,4]{1,0:T(1,128)} %weight_ref.1) | copy-start | bytes 52
  1.5 41.0 %copy-start.6 = (f32[32]{0:T(128)S(1)}, f32[32]{0:T(128)}, u32[]{:S(2)}) copy-start(f32[32]{0:T(128)} %param.10) | copy-start | bytes 388
  1.5 55.3 %copy-start.3 = (f32[10,16]{1,0:T(8,128)S(1)}, f32[10,16]{1,0:T(8,128)}, u32[]{:S(2)}) copy-start(f32[10,16]{1,0:T(8,128)} %target_ref.1) | copy-start | bytes 1924
  26.6 7.9 %collective-permute-start = (bf16[32,1152]{1,0:T(8,128)(2,1)S(1)}, bf16[32,1152]{1,0:T(8,128)(2,1)S(1)}, u32[]{:S(2)}, u32[]{:S(2)}) collective-permute-start(bf16[32,1152]{1,0:T(8,128)(2,1)S(1)} %rows.1.refs_0_), channel_id=1, source_target_pairs={{0,32},{32,0},{64,96},{96,64},{128,160},{160,128},{192,224},{224,1... | collective-permute-start | bytes 221192 | tf_op jit(solution)/shard_map/ppermute | solution.py:573
  31.0 7.5 %collective-permute-start.3 = (bf16[32,1152]{1,0:T(8,128)(2,1)S(1)}, bf16[32,1152]{1,0:T(8,128)(2,1)S(1)}, u32[]{:S(2)}, u32[]{:S(2)}) collective-permute-start(bf16[32,1152]{1,0:T(8,128)(2,1)S(1)} %rows.1.refs_0_), channel_id=1, source_target_pairs={{0,128},{32,160},{64,192},{96,224},{128,0},{160,32},{192,64},{224,... | collective-permute-start | bytes 221192 | tf_op jit(solution)/shard_map/ppermute | solution.py:573
  33.7 4.7 %collective-permute-start.2 = (bf16[32,1152]{1,0:T(8,128)(2,1)S(1)}, bf16[32,1152]{1,0:T(8,128)(2,1)S(1)}, u32[]{:S(2)}, u32[]{:S(2)}) collective-permute-start(bf16[32,1152]{1,0:T(8,128)(2,1)S(1)} %rows.1.refs_0_), channel_id=1, source_target_pairs={{0,192},{32,224},{64,128},{96,160},{128,64},{160,96},{192,0},{224,... | collective-permute-start | bytes 221192 | tf_op jit(solution)/shard_map/ppermute | solution.py:573
  34.6 3.9 %collective-permute-start.1 = (bf16[32,1152]{1,0:T(8,128)(2,1)S(1)}, bf16[32,1152]{1,0:T(8,128)(2,1)S(1)}, u32[]{:S(2)}, u32[]{:S(2)}) collective-permute-start(bf16[32,1152]{1,0:T(8,128)(2,1)S(1)} %rows.1.refs_0_), channel_id=1, source_target_pairs={{0,64},{32,96},{64,0},{96,32},{128,192},{160,224},{192,128},{224,1... | collective-permute-start | bytes 221192 | tf_op jit(solution)/shard_map/ppermute | solution.py:573
  34.6 5.7 %collective-permute-start.6 = (bf16[32,1152]{1,0:T(8,128)(2,1)S(1)}, bf16[32,1152]{1,0:T(8,128)(2,1)S(1)}, u32[]{:S(2)}, u32[]{:S(2)}) collective-permute-start(bf16[32,1152]{1,0:T(8,128)(2,1)S(1)} %collective-permute-done.refs_1_), channel_id=1, source_target_pairs={{0,128},{32,160},{64,192},{96,224},{128,0},{160,32},{192,64},{224,... | collective-permute-start | bytes 221192 | tf_op jit(solution)/shard_map/ppermute | solution.py:573
  37.6 4.9 %collective-permute-start.5 = (bf16[32,1152]{1,0:T(8,128)(2,1)S(1)}, bf16[32,1152]{1,0:T(8,128)(2,1)S(1)}, u32[]{:S(2)}, u32[]{:S(2)}) collective-permute-start(bf16[32,1152]{1,0:T(8,128)(2,1)S(1)} %collective-permute-done.refs_1_), channel_id=1, source_target_pairs={{0,192},{32,224},{64,128},{96,160},{128,64},{160,96},{192,0},{224,... | collective-permute-start | bytes 221192 | tf_op jit(solution)/shard_map/ppermute | solution.py:573
  38.4 4.0 %collective-permute-start.4 = (bf16[32,1152]{1,0:T(8,128)(2,1)S(1)}, bf16[32,1152]{1,0:T(8,128)(2,1)S(1)}, u32[]{:S(2)}, u32[]{:S(2)}) collective-permute-start(bf16[32,1152]{1,0:T(8,128)(2,1)S(1)} %collective-permute-done.refs_1_), channel_id=1, source_target_pairs={{0,64},{32,96},{64,0},{96,32},{128,192},{160,224},{192,128},{224,1... | collective-permute-start | bytes 221192 | tf_op jit(solution)/shard_map/ppermute | solution.py:573
